TPU v7x, 256 devices: a whole 4x4x8 slice. The times are simulated.
256 devices in a mesh: dom: 64 (over y, z, core), feat: 4 (over x).
Axes of the slice: x: 4, y: 4, z: 8, core: 2. Of those that a mesh axis runs over, the one named last changes fastest.
Arguments:
- features: bfloat16 [131072, 256], P('dom', 'feat'), may hold values from -6 to 6
- w_self: bfloat16 [256, 256], P('feat'), may hold values from -0.375 to 0.375
- w_neigh: bfloat16 [256, 256], P('feat'), may hold values from -0.75 to 0.75
- bias: float32 [256], P('feat'), may hold values from -3 to 3
- grad_out: bfloat16 [131072, 256], P('dom', 'feat'), may hold values from -6 to 6
- degree: int32 [131072], P('dom'), may hold values from 1 to 18188, as said below
- tiles: bfloat16 [8192, 128, 128], P('dom'), may hold values from 0 to 1, as said below
- tile_src: int32 [8192], P('dom'), may hold values from 0 to 15
- tile_dst: int32 [8192], P('dom'), may hold values from 0 to 15
- tile_count: int32 [64], P('dom'), may hold values from 32 to 128, as said below
- halo_adj: bfloat16 [131072, 1536], P('dom'), may hold values from 0 to 1, as said below
- send_rows: int32 [64, 64, 24], P('dom'), may hold values from 0 to 2047
- send_count: int32 [64, 64], P('dom'), may hold values from 0 to 24, as said below
- hub_adj: bfloat16 [131072, 256], P('dom'), may hold values from 0 to 1, as said below
- hub_local: int32 [256], P('dom'), may hold values from 0 to 2047
Outputs:
- output: bfloat16 [131072, 256], P('dom', 'feat')
- grad_features: bfloat16 [131072, 256], P('dom', 'feat')
- grad_self: float32 [256, 256], P('feat')
- grad_neigh: float32 [256, 256], P('feat')
- grad_bias: float32 [256], P('feat')
Inputs may be any that keep to these rules, and one draw needn't show every extreme that they name: `tiles`: entries are 0 or 1. `halo_adj`: entries are 0 or 1. `hub_adj`: entries are 0 or 1. `tile_count`: some partition uses all 128 slots of its list. `send_count`: A partition sends nothing to itself; every partition fills all 24 slots to some other partition. Each node's degree exceeds its number of edges in tiles, halo_adj and hub_adj by 1 to 11, except one node, whose degree is the maximum.
All inputs are finite; a program needn't handle non-finite values.
Results may differ from a plain program's by a relative error of at most 0.015.
Values may be sent and summed in bfloat16 or wider, within the bound.
No kernel may reach another device: no remote copies, remote signals or barrier semaphores. Data moves between devices by JAX's collectives and lax.ppermute only.
A program may use at most 64 MiB of HBM per device.

v0:
```python
import jax
import jax.numpy as jnp
from jax import lax
from jax.sharding import PartitionSpec as P


def silu_slope(value):
    sigma = jax.nn.sigmoid(value)
    return sigma * (1.0 + value * (1.0 - sigma))


def contract_rows(left, right):
    return lax.dot_general(
        left, right, (((0,), (0,)), ((), ())), preferred_element_type=jnp.float32
    )


def contract_cols(left, right):
    return lax.dot_general(
        left, right, (((1,), (1,)), ((), ())), preferred_element_type=jnp.float32
    )


def on_device(
    features,
    w_self,
    w_neigh,
    bias,
    grad_out,
    degree,
    tiles,
    tile_src,
    tile_dst,
    tile_count,
    halo_adj,
    send_rows,
    send_count,
    hub_adj,
    hub_local,
):
    rows_dev, fin_dev = features.shape
    block_rows = tiles.shape[1]
    block_count = rows_dev // block_rows
    domains = lax.axis_size("dom")
    slot_count = send_rows.shape[2]
    live_slot = jnp.arange(slot_count, dtype=jnp.int32)[None, :] < send_count[0][:, None]
    outgoing = features[send_rows[0]] * live_slot[:, :, None].astype(jnp.bfloat16)
    own_hubs = features[hub_local]
    arrived = lax.all_to_all(outgoing, "dom", split_axis=0, concat_axis=0, tiled=True)
    hub_rows = lax.all_gather(own_hubs, "dom", axis=0, tiled=True)
    live_tile = (jnp.arange(tiles.shape[0], dtype=jnp.int32) < tile_count[0]).astype(jnp.float32)
    block_ids = jnp.arange(block_count, dtype=jnp.int32)[None, :]
    source_pick = (tile_src[:, None] == block_ids).astype(jnp.float32) * live_tile[:, None]
    target_pick = (tile_dst[:, None] == block_ids).astype(jnp.float32) * live_tile[:, None]
    picked = features.reshape(block_count, block_rows, fin_dev)[tile_src]
    products = jnp.einsum("tij,tjf->tif", tiles, picked, preferred_element_type=jnp.float32)
    local_sum = jnp.einsum(
        "tb,tif->bif", target_pick, products, precision=lax.Precision.HIGHEST
    ).reshape(rows_dev, fin_dev)
    halo_sum = jnp.dot(halo_adj, arrived.reshape(-1, fin_dev), preferred_element_type=jnp.float32)
    hub_sum = jnp.dot(hub_adj, hub_rows, preferred_element_type=jnp.float32)
    degrees = degree.astype(jnp.float32)[:, None]
    mean = ((local_sum + halo_sum + hub_sum) / degrees).astype(jnp.bfloat16)
    partial_terms = jnp.dot(features, w_self, preferred_element_type=jnp.float32) + jnp.dot(
        mean, w_neigh, preferred_element_type=jnp.float32
    )
    pre = (
        lax.psum_scatter(
            partial_terms.astype(jnp.bfloat16), "feat", scatter_dimension=1, tiled=True
        ).astype(jnp.float32)
        + bias[None, :]
    )
    output = jax.nn.silu(pre).astype(jnp.bfloat16)
    grad_pre = (grad_out.astype(jnp.float32) * silu_slope(pre)).astype(jnp.bfloat16)
    grad_full = lax.all_gather(grad_pre, "feat", axis=1, tiled=True)
    grad_self, grad_neigh, grad_bias = lax.psum(
        (
            contract_rows(features, grad_full),
            contract_rows(mean, grad_full),
            jnp.sum(grad_pre, axis=0, dtype=jnp.float32),
        ),
        "dom",
    )
    grad_input = contract_cols(grad_full, w_self)
    grad_mean = (contract_cols(grad_full, w_neigh) / degrees).astype(jnp.bfloat16)
    picked_back = grad_mean.reshape(block_count, block_rows, fin_dev)[tile_dst]
    back_products = jnp.einsum(
        "tji,tjf->tif", tiles, picked_back, preferred_element_type=jnp.float32
    )
    local_back = jnp.einsum(
        "tb,tif->bif", source_pick, back_products, precision=lax.Precision.HIGHEST
    ).reshape(rows_dev, fin_dev)
    halo_back = contract_rows(halo_adj, grad_mean).reshape(domains, slot_count, fin_dev)
    hub_back = contract_rows(hub_adj, grad_mean)
    returned = lax.all_to_all(
        halo_back.astype(jnp.bfloat16), "dom", split_axis=0, concat_axis=0, tiled=True
    ).astype(halo_back.dtype)
    hub_grads = lax.psum_scatter(hub_back, "dom", scatter_dimension=0, tiled=True)
    returned = returned * live_slot[:, :, None].astype(jnp.float32)
    total = grad_input + local_back
    total = total.at[send_rows[0].reshape(-1)].add(returned.reshape(-1, fin_dev))
    total = total.at[hub_local].add(hub_grads)
    return (output, total.astype(jnp.bfloat16), grad_self, grad_neigh, grad_bias)


def solution(mesh):
    in_specs = (
        P("dom", "feat"),
        P("feat", None),
        P("feat", None),
        P("feat"),
        P("dom", "feat"),
        P("dom"),
        P("dom", None, None),
        P("dom"),
        P("dom"),
        P("dom"),
        P("dom", None),
        P("dom", None, None),
        P("dom", None),
        P("dom", None),
        P("dom"),
    )
    out_specs = (P("dom", "feat"), P("dom", "feat"), P("feat", None), P("feat", None), P("feat"))
    return jax.shard_map(
        on_device, mesh=mesh, in_specs=in_specs, out_specs=out_specs, check_vma=False
    )
```

profile of v0, /device:TPU:1, one launch (start us, length us, event | category | flops | bytes accessed | tf_op | source)
XLA Modules:
  0.0 485.0 jit_solution(6499253757087366442)
XLA Ops:
  7.2 1.3 copy.49
  9.5 1.3 fusion.11
  10.8 3.2 gather_fusion.1
  14.3 0.9 reshape.212
  15.2 13.2 %all-to-all-start = ((bf16[64,2,768]{2,1,0:T(2,128)(2,1)}), bf16[64,2,768]{2,1,0:T(2,128)(2,1)S(1)}, u32[]{:S(2)}, u32[]{:S(2)}) async-start(bf16[64,2,768]{2,1,0:T(2,128)(2,1)} %reshape.212), calls=%async_computation | async-start | bytes 393216 | tf_op jit(solution)/shard_map/all_to_all | solution.py:49
  29.2 1.8 fusion.26
  31.0 2.2 gather_fusion
  33.2 7.8 %convolution_bitcast_fusion.3 = f32[128,128,64]{1,2,0:T(8,128)} fusion(bf16[128,128,64]{1,2,0:T(8,128)(2,1)} %gather_fusion, bf16[128,128,128]{2,1,0:T(8,128)(2,1)} %param.21), kind=kOutput, calls=%fused_computation.24 | convolution fusion | flops 268435456 | bytes 10485760 | tf_op jit(solution)/shard_map/tij,tjf->tif/dot_general | solution.py:56
  41.6 44.7 %all-gather.1 = bf16[64,4,64]{2,1,0:T(4,128)(2,1)S(1)} all-gather(bf16[1,4,64]{2,1,0:T(4,128)(2,1)S(1)} %bitcast.95), channel_id=2, replica_groups=mesh['dom'=64,'feat'=4] {'dom'}, dimensions={0}, use_global_device_ids=true | all-gather | bytes 33280 | tf_op jit(solution)/shard_map/all_gather | solution.py:50
  86.3 6.8 %fusion.2 = f32[16,128,64]{1,0,2:T(8,128)S(1)} fusion(f32[128,128,64]{1,2,0:T(8,128)} %convolution_bitcast_fusion.3, f32[128]{0:T(128)S(1)} %compare_convert_fusion, s32[128]{0:T(128)S(1)} %copy-done.16), kind=kOutput, calls=%fused_computation.8 | convolution fusion | flops 201330688 | bytes 4719616 | tf_op jit(solution)/shard_map/tb,tif->bif/dot_general | solution.py:57
  93.4 5.0 %fusion.7 = f32[2048,64]{0,1:T(8,128)S(1)} fusion(bf16[1536,64]{1,0:T(8,128)(2,1)S(1)} %bitcast.93, bf16[2048,1536]{1,0:T(8,128)(2,1)} %param.25, f32[8,8,16,128]{3,2,1,0:T(8,128)S(1)} %bitcast.90), kind=kOutput, calls=%fused_computation.18 | convolution fusion | flops 402784256 | bytes 7536640 | tf_op jit(solution)/shard_map/dot_general | solution.py:60
  99.6 1.5 fusion.4
  101.1 22.8 %reduce-scatter.3.cloned.1.call-done = bf16[2048,64]{0,1:T(8,128)(2,1)} async-done(((bf16[2048,256]{0,1:T(8,128)(2,1)}), bf16[2048,64]{0,1:T(8,128)(2,1)}) %reduce-scatter.3.cloned.1.call-update) | async-done | bytes 262160 | tf_op jit(solution)/shard_map/reduce_scatter | solution.py:68
  123.9 2.2 convert_reduce_fusion
  127.7 126.7 %psum.23 = f32[64]{0:T(128)} all-reduce(f32[64]{0:T(128)S(1)} %get-tuple-element.28), channel_id=1, replica_groups=mesh['dom'=64,'feat'=4] {'dom'}, use_global_device_ids=true, to_apply=%region_7.8 | all-reduce | flops 64 | bytes 512 | tf_op jit(solution)/shard_map/psum | solution.py:76
  254.3 1.5 fusion.9
  255.9 0.9 convolution_bitcast_fusion.5
  256.9 4.7 fusion.10
  261.5 0.9 gather_fusion.3
  262.5 3.4 convolution_bitcast_fusion.2
  266.0 4.4 fusion
  270.3 1.1 copy.54
  271.5 0.9 reshape.214
  272.4 8.6 %all-to-all-start.1 = ((bf16[64,2,768]{2,1,0:T(2,128)(2,1)}), bf16[64,2,768]{2,1,0:T(2,128)(2,1)}, u32[]{:S(2)}, u32[]{:S(2)}) async-start(bf16[64,2,768]{2,1,0:T(2,128)(2,1)} %reshape.214), calls=%async_computation.2 | async-start | bytes 393216 | tf_op jit(solution)/shard_map/all_to_all | solution.py:95
  281.1 1.1 fusion.27
  282.1 1.1 convolution_bitcast_fusion.4
  283.2 1.1 convolution_add_fusion.1
  284.7 178.9 %all-reduce.4.cloned.1.call-done = (f32[256,64]{0,1:T(8,128)}, f32[64,256]{1,0:T(8,128)}, f32[64,256]{1,0:T(8,128)}) async-done(((f32[256,64]{0,1:T(8,128)}, f32[64,256]{1,0:T(8,128)}, f32[64,256]{1,0:T(8,128)}), (f32[256,64]{0,1:T(8,128)}, f32[64,256]{1,0:T(8,128)}, f32[64,256]{1,0:T(8,128)})) %all-reduce.4.cloned.1.call-update) | async-done | bytes 196624
  464.5 1.2 reshape.215
  466.0 9.1 %scatter_fusion = f32[2048,64]{1,0:T(8,128)S(1)} fusion(f32[2048,64]{1,0:T(8,128)S(1)} %copy.55, s32[1536]{0:T(1024)S(1)} %fusion.17, f32[1536,64]{1,0:T(8,128)S(1)} %bitcast.88), kind=kCustom, calls=%fused_computation.4 | custom fusion | flops 98304 | bytes 1185792 | tf_op jit(solution)/shard_map/scatter-add | solution.py:101
  475.2 1.0 scatter_fusion.1
  476.3 0.9 copy.57
  (80 shorter events, 7.2 us)
Async XLA Ops:
  7.2 91.2 %copy-start = (bf16[2048,256]{1,0:T(8,128)(2,1)S(1)}, bf16[2048,256]{1,0:T(8,128)(2,1)}, u32[]{:S(2)}) copy-start(bf16[2048,256]{1,0:T(8,128)(2,1)} %param.28) | copy-start | bytes 3145732
  7.2 21.2 %copy-start.3 = (bf16[2048,64]{0,1:T(8,128)(2,1)S(1)}, bf16[2048,64]{0,1:T(8,128)(2,1)}, u32[]{:S(2)}) copy-start(bf16[2048,64]{0,1:T(8,128)(2,1)} %param.15) | copy-start | bytes 786436
  7.2 21.9 %copy-start.17 = (s32[128]{0:T(128)S(1)}, s32[128]{0:T(128)}, u32[]{:S(2)}) copy-start(s32[128]{0:T(128)} %param.22) | copy-start | bytes 1540
  7.2 22.0 %copy-start.19 = (s32[4]{0:T(128)S(1)}, s32[4]{0:T(128)}, u32[]{:S(2)}) copy-start(s32[4]{0:T(128)} %param.29) | copy-start | bytes 52
  7.2 22.0 %copy-start.8 = (bf16[64,256]{1,0:T(8,128)(2,1)S(1)}, bf16[64,256]{1,0:T(8,128)(2,1)}, u32[]{:S(2)}) copy-start(bf16[64,256]{1,0:T(8,128)(2,1)} %param.16) | copy-start | bytes 98308
  15.2 77.9 %all-to-all-start = ((bf16[64,2,768]{2,1,0:T(2,128)(2,1)}), bf16[64,2,768]{2,1,0:T(2,128)(2,1)S(1)}, u32[]{:S(2)}, u32[]{:S(2)}) async-start(bf16[64,2,768]{2,1,0:T(2,128)(2,1)} %reshape.212), calls=%async_computation | async-start | bytes 393216 | tf_op jit(solution)/shard_map/all_to_all | solution.py:49
  28.4 95.6 %reduce-scatter.3.cloned.1.call-start = ((), (), s32[]{:S(2)}) async-start(), calls=%async_computation.3 | async-start | bytes 1310720 | tf_op jit(solution)/shard_map/reduce_scatter | solution.py:68
  33.2 8.4 %copy-start.14 = (s32[2048]{0:T(1024)S(1)}, s32[2048]{0:T(1024)}, u32[]{:S(2)}) copy-start(s32[2048]{0:T(1024)} %param.20) | copy-start | bytes 24580
  33.2 53.1 %copy-start.16 = (s32[128]{0:T(128)S(1)}, s32[128]{0:T(128)}, u32[]{:S(2)}) copy-start(s32[128]{0:T(128)} %param.23) | copy-start | bytes 1540
  93.4 6.2 %copy-start.2 = (f32[2048,256]{0,1:T(8,128)S(1)}, f32[2048,256]{0,1:T(8,128)}, u32[]{:S(2)}) copy-start(f32[2048,256]{0,1:T(8,128)} %fusion.26) | copy-start | bytes 6291460
  93.4 6.2 %copy-start.13 = (bf16[64,256]{1,0:T(8,128)(2,1)S(1)}, bf16[64,256]{1,0:T(8,128)(2,1)}, u32[]{:S(2)}) copy-start(bf16[64,256]{1,0:T(8,128)(2,1)} %param.17) | copy-start | bytes 98308
  98.4 25.6 %copy-start.7 = (bf16[2048,64]{0,1:T(8,128)(2,1)S(1)}, bf16[2048,64]{0,1:T(8,128)(2,1)}, u32[]{:S(2)}) copy-start(bf16[2048,64]{0,1:T(8,128)(2,1)} %param.19) | copy-start | bytes 786436
  98.4 25.6 %copy-start.15 = (f32[64]{0:T(128)S(1)}, f32[64]{0:T(128)}, u32[]{:S(2)}) copy-start(f32[64]{0:T(128)} %param.18) | copy-start | bytes 772
  98.4 27.8 %copy-start.12 = (s32[1,64,24]{1,2,0:T(8,128)S(1)}, s32[1,64,24]{1,2,0:T(8,128)}, u32[]{:S(2)}) copy-start(s32[1,64,24]{1,2,0:T(8,128)} %param.26) | copy-start | bytes 18436
  98.4 28.0 %copy-start.20 = (u32[256]{0:T(256)S(1)}, u32[256]{0:T(256)}, u32[]{:S(2)}) copy-start(u32[256]{0:T(256)} %constant.25) | copy-start | bytes 3076
  98.9 0.7 copy-start.5
  101.1 153.2 %all-gather.4.cloned.1.call-start = ((), (), s32[]{:S(2)}) async-start(), calls=%async_computation.4 | async-start | bytes 1310720 | tf_op jit(solution)/shard_map/all_gather | solution.py:75
  262.5 3.4 copy-start.18
  265.9 15.1 %copy-start.1 = (bf16[2048,256]{0,1:T(8,128)(2,1)S(1)}, bf16[2048,256]{0,1:T(8,128)(2,1)}, u32[]{:S(2)}) copy-start(bf16[2048,256]{0,1:T(8,128)(2,1)} %all-gather.4.cloned.1.call-done) | copy-start | bytes 3145732
  265.9 15.1 %copy-start.6 = (bf16[2048,64]{0,1:T(8,128)(2,1)S(1)}, bf16[2048,64]{0,1:T(8,128)(2,1)}, u32[]{:S(2)}) copy-start(bf16[2048,64]{0,1:T(8,128)(2,1)} %copy-done.5) | copy-start | bytes 786436
  265.9 16.2 %copy-start.4 = (bf16[2048,64]{0,1:T(8,128)(2,1)S(1)}, bf16[2048,64]{0,1:T(8,128)(2,1)}, u32[]{:S(2)}) copy-start(bf16[2048,64]{0,1:T(8,128)(2,1)} %param.15) | copy-start | bytes 786436
  272.4 192.1 %all-to-all-start.1 = ((bf16[64,2,768]{2,1,0:T(2,128)(2,1)}), bf16[64,2,768]{2,1,0:T(2,128)(2,1)}, u32[]{:S(2)}, u32[]{:S(2)}) async-start(bf16[64,2,768]{2,1,0:T(2,128)(2,1)} %reshape.214), calls=%async_computation.2 | async-start | bytes 393216 | tf_op jit(solution)/shard_map/all_to_all | solution.py:95
  281.0 182.6 %all-reduce.4.cloned.1.call-start = ((), (), s32[]{:S(2)}) async-start(), calls=%async_computation.5 | async-start | bytes 393216
  282.1 183.6 %copy-start.9 = (f32[64,24]{1,0:T(8,128)S(1)}, f32[64,24]{1,0:T(8,128)}, u32[]{:S(2)}) copy-start(f32[64,24]{1,0:T(8,128)} %get-tuple-element.31) | copy-start | bytes 18436
  466.0 11.2 %copy-start.11 = (f32[64,256]{1,0:T(8,128)S(1)}, f32[64,256]{1,0:T(8,128)}, u32[]{:S(2)}) copy-start(f32[64,256]{1,0:T(8,128)} %get-tuple-element.35) | copy-start | bytes 196612
  466.0 11.8 %copy-start.10 = (f32[64,256]{1,0:T(8,128)S(1)}, f32[64,256]{1,0:T(8,128)}, u32[]{:S(2)}) copy-start(f32[64,256]{1,0:T(8,128)} %get-tuple-element.36) | copy-start | bytes 196612
Sparse Core Ops, SparseCore 0:
  101.2 22.6 reduce-scatter.2
  126.5 26.7 all-gather.3
  286.6 176.8 all-reduce.3
where the time goes:
time: 486 us; the launch traced here: 485 us
  waiting for transfers between devices  202 us (42%)
  blocking collectives  171 us (35%)
  matrix products  41.4 us (9%)
  starting transfers between devices  21.9 us (5%)
  local copies, waits for them, and re-layouts  18 us (4%)
  between operations  15.6 us (3%)
  other arithmetic  15.1 us (3%)
    unnamed x4, waiting for transfers between devices  179 us
    psum x1, blocking collectives, on_device(): lax.psum((contract_rows(features, grad_full), contract_rows(mean, grad_fu...  127 us
    all_gather x1, blocking collectives, on_device(): hub_rows = lax.all_gather(own_hubs, 'dom', axis=0, tiled=True)  44.7 us
    reduce_scatter x1, waiting for transfers between devices, on_device(): lax.psum_scatter(partial_terms.astype(jnp.bfloat16), 'feat', scatter_dime...  22.8 us
    all_to_all x1, starting transfers between devices, on_device(): lax.all_to_all(outgoing, 'dom', split_axis=0, concat_axis=0, tiled=True)  13.2 us
  transfers between devices with their start and end apart: 5, of which 2 were waited for; matrix products, arithmetic and copies ran while one was open for 5% of the time, Pallas kernels for 0%

commit v1 on v0

v1 whole, which is shorter than its diff:
```python
import functools

import jax
import jax.numpy as jnp
from jax import lax
from jax.experimental import pallas as pl
from jax.experimental.pallas import tpu as pltpu
from jax.sharding import PartitionSpec as P

BF = jnp.bfloat16
F32 = jnp.float32
I32 = jnp.int32

PEERS = 64
FEATS = 4
SLOT = 24
HUBS = 4
ROWS = 16
WIDE = 24
LANES = 128
FIN = 64
FOUT = 256
NODES = 2048
BLOCK = 128
TILES = 128
HALO = PEERS * SLOT
HUB_ALL = PEERS * HUBS
WPACK = 144

VMEM_LIMIT = 48 * 1024 * 1024


def matmul(left, right):
    return lax.dot_general(
        left, right, (((1,), (0,)), ((), ())), preferred_element_type=F32
    )


def matmul_nt(left, right):
    return lax.dot_general(
        left, right, (((1,), (1,)), ((), ())), preferred_element_type=F32
    )


def params(semantics=None):
    return pltpu.CompilerParams(
        dimension_semantics=semantics, vmem_limit_bytes=VMEM_LIMIT
    )


def cost(flops, moved):
    return pl.CostEstimate(flops=flops, bytes_accessed=moved, transcendentals=0)


def iota(shape, axis):
    return lax.broadcasted_iota(I32, shape, axis)


def pick_hubs():
    hub = iota((HUB_ALL, PEERS * 8), 0)
    place = iota((HUB_ALL, PEERS * 8), 1)
    same = (hub // HUBS == place // 8) & (hub % HUBS == place % 8)
    return same.astype(F32).astype(BF)


def gather_kernel(hub_ref, send_ref, count_ref, feat_ref, wire_ref, index_ref):
    slot = iota((SLOT, PEERS), 0)
    sent = jnp.where(slot < count_ref[...], send_ref[...], -1)
    place = iota((8, PEERS), 0)
    hubs = jnp.full((8, PEERS), -1, I32)
    for h in range(HUBS):
        hubs = jnp.where(place == h, hub_ref[h], hubs)
    rows = jnp.concatenate([sent, hubs], axis=0)
    high = lax.shift_right_arithmetic(rows, 6)
    low = rows - high * 64
    split = jnp.concatenate([high, low], axis=0).astype(F32).astype(BF)
    count = PEERS * ROWS
    spread = (iota((PEERS, count), 0) == iota((PEERS, count), 1) // ROWS)
    wide = matmul(split, spread.astype(F32).astype(BF))
    wide = wide[:32] * 64.0 + wide[32:]
    mine = iota((ROWS, count), 0) == iota((ROWS, count), 1) % ROWS
    left = jnp.sum(jnp.where(mine, wide[:ROWS], 0.0), axis=0, keepdims=True)
    right = jnp.sum(jnp.where(mine, wide[ROWS:], 0.0), axis=0, keepdims=True)
    both = jnp.concatenate([left, right], axis=1)
    index_ref[...] = jnp.broadcast_to(both, (8, 2 * count))
    target = both.astype(I32)
    step = 256
    total = jnp.zeros((FIN, 2 * count), F32)
    node = iota((step, 2 * count), 0)
    for k in range(NODES // step):
        hot = (node == target - k * step).astype(F32).astype(BF)
        total += matmul(feat_ref[:, k * step:(k + 1) * step], hot)
    stacked = jnp.concatenate([total[:, :count], total[:, count:]], axis=0)
    wire_ref[...] = stacked.T.astype(BF)


def gather_rows(hub_local, send, count, feat):
    slots = PEERS * ROWS
    full = lambda *_: (0, 0)
    return pl.pallas_call(
        gather_kernel,
        grid_spec=pltpu.PrefetchScalarGridSpec(
            num_scalar_prefetch=1,
            grid=(1,),
            in_specs=[
                pl.BlockSpec((SLOT, PEERS), full),
                pl.BlockSpec((1, PEERS), full),
                pl.BlockSpec((FIN, NODES), full),
            ],
            out_specs=[
                pl.BlockSpec((slots, LANES), full),
                pl.BlockSpec((8, 2 * slots), full),
            ],
        ),
        out_shape=[
            jax.ShapeDtypeStruct((slots, LANES), BF),
            jax.ShapeDtypeStruct((8, 2 * slots), F32),
        ],
        compiler_params=params(),
        cost_estimate=cost(2 * 2 * slots * NODES * 256, 1000000),
        name="gather_rows",
    )(hub_local, send, count, feat)


def local_kernel(src_ref, dst_ref, count_ref, tiles_ref, feat_ref, sum_ref, adj_ref):
    step = pl.program_id(0)
    group = tiles_ref.shape[0]

    @pl.when(step == 0)
    def clear():
        adj_ref[...] = jnp.zeros_like(adj_ref)

    for j in range(group):
        t = step * group + j

        @pl.when(t < count_ref[0])
        def add():
            rows = pl.ds(pl.multiple_of(dst_ref[t] * BLOCK, BLOCK), BLOCK)
            cols = pl.ds(pl.multiple_of(src_ref[t] * BLOCK, BLOCK), BLOCK)
            adj_ref[rows, cols] += tiles_ref[j]

    @pl.when(step == pl.num_programs(0) - 1)
    def finish():
        width = 256
        for k in range(NODES // width):
            part = adj_ref[k * width:(k + 1) * width, :]
            sum_ref[:, k * width:(k + 1) * width] = matmul_nt(feat_ref[...], part)


def local_sum(src, dst, count, tiles, feat):
    group = 16
    return pl.pallas_call(
        local_kernel,
        grid_spec=pltpu.PrefetchScalarGridSpec(
            num_scalar_prefetch=3,
            grid=(TILES // group,),
            in_specs=[
                pl.BlockSpec((group, BLOCK, BLOCK), lambda i, *_: (i, 0, 0)),
                pl.BlockSpec((FIN, NODES), lambda i, *_: (0, 0)),
            ],
            out_specs=[
                pl.BlockSpec((FIN, NODES), lambda i, *_: (0, 0)),
                pl.BlockSpec((NODES, NODES), lambda i, *_: (0, 0)),
            ],
        ),
        out_shape=[
            jax.ShapeDtypeStruct((FIN, NODES), F32),
            jax.ShapeDtypeStruct((NODES, NODES), BF),
        ],
        compiler_params=params(("arbitrary",)),
        cost_estimate=cost(2 * NODES * NODES * 256, 13000000),
        name="local_sum",
    )(src, dst, count, tiles, feat)


def mean_kernel(wire_ref, halo_ref, hub_ref, local_ref, degree_ref, mean_ref, rows_ref, hubs_ref):
    @pl.when(pl.program_id(0) == 0)
    def unpack():
        wire = wire_ref[...].astype(F32).reshape(PEERS, ROWS, LANES)
        left = wire[:, :, :FIN]
        right = wire[:, :, FIN:]
        rows = jnp.concatenate([left, right[:, :8]], axis=1)
        rows_ref[...] = rows.reshape(HALO, FIN).astype(BF)
        owned = right[:, 8:].reshape(PEERS * 8, FIN).astype(BF)
        hubs_ref[...] = matmul(pick_hubs(), owned).astype(BF)

    total = matmul(halo_ref[...], rows_ref[...]) + matmul(hub_ref[...], hubs_ref[...])
    total = total.T + local_ref[...]
    mean_ref[...] = (total / degree_ref[...].astype(F32)).astype(BF)


def mean_rows(wire, halo_adj, hub_adj, local, degree):
    chunk = 512
    return pl.pallas_call(
        mean_kernel,
        grid=(NODES // chunk,),
        in_specs=[
            pl.BlockSpec((PEERS * ROWS, LANES), lambda i: (0, 0)),
            pl.BlockSpec((chunk, HALO), lambda i: (i, 0)),
            pl.BlockSpec((chunk, HUB_ALL), lambda i: (i, 0)),
            pl.BlockSpec((FIN, chunk), lambda i: (0, i)),
            pl.BlockSpec((1, chunk), lambda i: (0, i)),
        ],
        out_specs=pl.BlockSpec((FIN, chunk), lambda i: (0, i)),
        out_shape=jax.ShapeDtypeStruct((FIN, NODES), BF),
        scratch_shapes=[
            pltpu.VMEM((HALO, FIN), BF),
            pltpu.VMEM((HUB_ALL, FIN), BF),
        ],
        compiler_params=params(("arbitrary",)),
        cost_estimate=cost(2 * NODES * (HALO + HUB_ALL) * 256, 8000000),
        name="mean_rows",
    )(wire, halo_adj, hub_adj, local, degree)


def dense_kernel(
    mine_ref, feat_ref, gout_ref, mean0_ref, mean1_ref, mean2_ref, mean3_ref,
    pack_ref, degree_ref, halo_ref, hub_ref,
    out_ref, gmean_ref, ginput_ref, wire_ref,
    weight_ref, bias_ref, back_ref, pre_ref, halo_acc, hub_acc, grad_acc,
):
    step = pl.program_id(0)
    mine = mine_ref[0]
    own = pl.multiple_of(mine * FIN, FIN)
    means = (mean0_ref, mean1_ref, mean2_ref, mean3_ref)

    @pl.when(step == 0)
    def prepare():
        eye = iota((FIN, FIN), 0) == iota((FIN, FIN), 1)
        for g in range(FEATS):
            both = pack_ref[g, :2 * FIN, :].astype(F32)
            weight_ref[g] = both.T.astype(BF)
            parts = pack_ref[g, 2 * FIN:2 * FIN + 16, :].astype(F32)
            row = parts[0:1, :FIN] + parts[1:2, :FIN] + parts[2:3, :FIN]
            column = jnp.sum(jnp.where(eye, row, 0.0), axis=1, keepdims=True)
            bias_ref[g * FIN:(g + 1) * FIN, :] = jnp.broadcast_to(column, (FIN, LANES))
        back_ref[...] = pack_ref[mine, :2 * FIN, :]
        halo_acc[...] = jnp.zeros_like(halo_acc)
        hub_acc[...] = jnp.zeros_like(hub_acc)
        grad_acc[...] = jnp.zeros_like(grad_acc)

    chunk = feat_ref.shape[1]
    pre = jnp.tile(bias_ref[...], (1, chunk // LANES))
    for k in range(FEATS):
        g = lax.rem(mine - k + FEATS, FEATS)
        rows = pl.ds(pl.multiple_of(g * FIN, FIN), FIN)
        both = jnp.concatenate([feat_ref[rows, :], means[k][...]], axis=0)
        pre = pre + matmul(weight_ref[g], both).astype(BF).astype(F32)
    sigma = 1.0 / (1.0 + jnp.exp(-pre))
    pre_ref[...] = pre * sigma
    out_ref[...] = pre_ref[pl.ds(own, FIN), :].astype(BF)
    slope = sigma * (1.0 + pre * (1.0 - sigma))
    gpre = (gout_ref[...].astype(F32) * slope).astype(BF)
    back = matmul(back_ref[...], gpre)
    ginput_ref[...] = back[:FIN]
    gmean = (back[FIN:] / degree_ref[...].astype(F32)).astype(BF)
    gmean_ref[...] = gmean
    left = jnp.concatenate(
        [feat_ref[pl.ds(own, FIN), :], mean0_ref[...], jnp.ones((16, chunk), BF)], axis=0
    )
    grad_acc[...] += matmul_nt(left, gpre)
    halo_acc[...] += matmul(gmean, halo_ref[...])
    hub_acc[...] += matmul(gmean, hub_ref[...])

    @pl.when(step == pl.num_programs(0) - 1)
    def ship():
        rows = halo_acc[...].T.reshape(PEERS, SLOT, FIN)
        hubs = matmul(hub_acc[...].astype(BF), pick_hubs()).T.reshape(PEERS, 8, FIN)
        bias = grad_acc[2 * FIN:2 * FIN + 1, :]
        row = bias[:, :FIN]
        for g in range(1, FEATS):
            row = jnp.where(mine == g, bias[:, g * FIN:(g + 1) * FIN], row)
        high = row.astype(BF).astype(F32)
        place = iota((8, FIN), 0)
        extra = jnp.where(place == 4, high, jnp.where(place == 5, row - high, 0.0))
        hubs = hubs + extra[None]
        right = jnp.concatenate([rows[:, 16:], hubs], axis=1)
        main = jnp.concatenate([rows[:, :16], right], axis=2)
        grads = grad_acc[:2 * FIN, :].reshape(16, 8, FOUT)
        grads = jnp.stack([grads[:, :, :LANES], grads[:, :, LANES:]], axis=1)
        grads = grads.reshape(32, 8, LANES)
        high = grads.astype(BF).astype(F32)
        low = grads - high
        swap = lambda x: jnp.concatenate([x[:, 4:], x[:, :4]], axis=1)
        first = iota((32, 8, LANES), 1) < 4
        even = jnp.where(first, high, swap(low))
        odd = jnp.where(first, swap(high), low)
        pieces = jnp.stack([even, odd], axis=1).reshape(PEERS, 8, LANES)
        wire = jnp.concatenate([main, pieces], axis=1)
        wire_ref[...] = wire.reshape(PEERS * WIDE, LANES).astype(BF)


def dense(mine, feat, gout, means, pack, degree, halo_adj, hub_adj):
    chunk = 256
    full = lambda i, *_: (0, 0)
    column = lambda i, *_: (0, i)
    return pl.pallas_call(
        dense_kernel,
        grid_spec=pltpu.PrefetchScalarGridSpec(
            num_scalar_prefetch=1,
            grid=(NODES // chunk,),
            in_specs=[
                pl.BlockSpec((FEATS * FIN, chunk), column),
                pl.BlockSpec((FOUT, chunk), column),
            ]
            + [pl.BlockSpec((FIN, chunk), column)] * FEATS
            + [
                pl.BlockSpec((FEATS, WPACK, FOUT), lambda i, *_: (0, 0, 0)),
                pl.BlockSpec((1, chunk), column),
                pl.BlockSpec((chunk, HALO), lambda i, *_: (i, 0)),
                pl.BlockSpec((chunk, HUB_ALL), lambda i, *_: (i, 0)),
            ],
            out_specs=[
                pl.BlockSpec((FIN, chunk), column),
                pl.BlockSpec((FIN, chunk), column),
                pl.BlockSpec((FIN, chunk), column),
                pl.BlockSpec((PEERS * WIDE, LANES), full),
            ],
            scratch_shapes=[
                pltpu.VMEM((FEATS, FOUT, 2 * FIN), BF),
                pltpu.VMEM((FOUT, LANES), F32),
                pltpu.VMEM((2 * FIN, FOUT), BF),
                pltpu.VMEM((FOUT, chunk), F32),
                pltpu.VMEM((FIN, HALO), F32),
                pltpu.VMEM((FIN, HUB_ALL), F32),
                pltpu.VMEM((2 * FIN + 16, FOUT), F32),
            ],
        ),
        out_shape=[
            jax.ShapeDtypeStruct((FIN, NODES), BF),
            jax.ShapeDtypeStruct((FIN, NODES), BF),
            jax.ShapeDtypeStruct((FIN, NODES), F32),
            jax.ShapeDtypeStruct((PEERS * WIDE, LANES), BF),
        ],
        compiler_params=params(("arbitrary",)),
        cost_estimate=cost(2 * NODES * 2048 * 256, 12000000),
        name="dense",
    )(mine, feat, gout, *means, pack, degree, halo_adj, hub_adj)


def back_kernel(ginput_ref, gmean_ref, adj_ref, total_ref):
    total_ref[...] = ginput_ref[...] + matmul(gmean_ref[...], adj_ref[...])


def local_back(ginput, gmean, adj):
    chunk = 512
    return pl.pallas_call(
        back_kernel,
        grid=(NODES // chunk,),
        in_specs=[
            pl.BlockSpec((FIN, chunk), lambda i: (0, i)),
            pl.BlockSpec((FIN, NODES), lambda i: (0, 0)),
            pl.BlockSpec((NODES, chunk), lambda i: (0, i)),
        ],
        out_specs=pl.BlockSpec((FIN, chunk), lambda i: (0, i)),
        out_shape=jax.ShapeDtypeStruct((FIN, NODES), F32),
        compiler_params=params(("arbitrary",)),
        cost_estimate=cost(2 * NODES * NODES * 256, 10000000),
        name="local_back",
    )(ginput, gmean, adj)


def reduce_kernel(wire_ref, sums_ref, bias_ref):
    wire = wire_ref[...].astype(F32).reshape(PEERS, WIDE, LANES)
    pieces = jnp.sum(wire[:, 16:], axis=0)
    half = pieces[:4] + pieces[4:]
    both = jnp.concatenate([half, half], axis=0)
    sums_ref[...] = jnp.broadcast_to(both[None], (PEERS // 2, 8, LANES)).reshape(
        PEERS * 4, LANES
    )
    tail = jnp.sum(wire[:, 8:16], axis=0)
    bias_ref[...] = tail[4:5, FIN:] + tail[5:6, FIN:]


def reduce_grads(wire):
    return pl.pallas_call(
        reduce_kernel,
        out_shape=[
            jax.ShapeDtypeStruct((PEERS * 4, LANES), F32),
            jax.ShapeDtypeStruct((1, FIN), F32),
        ],
        compiler_params=params(),
        cost_estimate=cost(1000000, 1000000),
        name="reduce_grads",
    )(wire)


def scatter_kernel(wire_ref, index_ref, total_ref, out_ref, back_ref):
    count = PEERS * ROWS

    @pl.when(pl.program_id(0) == 0)
    def unpack():
        wire = wire_ref[...].astype(F32).reshape(PEERS, WIDE, LANES)
        both = wire[:, :16].reshape(count, LANES).T
        back_ref[...] = jnp.concatenate([both[:FIN], both[FIN:]], axis=1).astype(BF)

    step = out_ref.shape[1]
    target = index_ref[0:1, :].astype(I32) - pl.program_id(0) * step
    hot = (iota((step, 2 * count), 0) == target).astype(F32).astype(BF)
    out_ref[...] = (total_ref[...] + matmul_nt(back_ref[...], hot)).astype(BF)


def scatter_rows(wire, index, total):
    chunk = 256
    count = PEERS * ROWS
    return pl.pallas_call(
        scatter_kernel,
        grid=(NODES // chunk,),
        in_specs=[
            pl.BlockSpec((PEERS * WIDE, LANES), lambda i: (0, 0)),
            pl.BlockSpec((8, 2 * count), lambda i: (0, 0)),
            pl.BlockSpec((FIN, chunk), lambda i: (0, i)),
        ],
        out_specs=pl.BlockSpec((FIN, chunk), lambda i: (0, i)),
        out_shape=jax.ShapeDtypeStruct((FIN, NODES), BF),
        scratch_shapes=[pltpu.VMEM((FIN, 2 * count), BF)],
        compiler_params=params(("arbitrary",)),
        cost_estimate=cost(2 * 2 * count * NODES * 256, 2000000),
        name="scatter_rows",
    )(wire, index, total)


def three_parts(value):
    high = lax.reduce_precision(value, 8, 7)
    middle = lax.reduce_precision(value - high, 8, 7)
    low = value - high - middle
    return jnp.stack([high, middle, low]).astype(BF)


def on_device(
    features,
    w_self,
    w_neigh,
    bias,
    grad_out,
    degree,
    tiles,
    tile_src,
    tile_dst,
    tile_count,
    halo_adj,
    send_rows,
    send_count,
    hub_adj,
    hub_local,
):
    feat = features.T
    gout = grad_out.T
    mine = lax.axis_index("feat").astype(I32).reshape(1)
    degree = degree.reshape(1, NODES)
    biases = jnp.pad(three_parts(bias), ((0, WPACK - 2 * FIN - 3), (0, FOUT - FIN)))
    pack = jnp.concatenate([w_self, w_neigh, biases], axis=0)
    feat_all = lax.all_gather(feat, "feat", axis=0, tiled=True)
    gout_all = lax.all_gather(gout, "feat", axis=0, tiled=True)
    pack_all = lax.all_gather(pack, "feat", axis=0, tiled=True)
    pack_all = pack_all.reshape(FEATS, WPACK, FOUT)
    send = jnp.transpose(send_rows[0])
    wire, index = gather_rows(hub_local, send, send_count, feat)
    arrived = lax.all_to_all(wire, "dom", split_axis=0, concat_axis=0, tiled=True)
    local, adj = local_sum(tile_src, tile_dst, tile_count, tiles, feat)
    mean = mean_rows(arrived, halo_adj, hub_adj, local, degree)
    means = [mean] + [
        lax.ppermute(mean, "feat", [(j, (j + k) % FEATS) for j in range(FEATS)])
        for k in range(1, FEATS)
    ]
    out, gmean, ginput, wire = dense(
        mine, feat_all, gout_all, means, pack_all, degree, halo_adj, hub_adj
    )
    returned = lax.all_to_all(wire, "dom", split_axis=0, concat_axis=0, tiled=True)
    total = local_back(ginput, gmean, adj)
    sums, grad_bias = reduce_grads(returned)
    shared = lax.all_to_all(sums, "dom", split_axis=0, concat_axis=0, tiled=True)
    grad_features = scatter_rows(returned, index, total)
    grads = shared.reshape(16, 2, 8, LANES).transpose(0, 2, 1, 3).reshape(2 * FIN, FOUT)
    return (
        out.T,
        grad_features.T,
        grads[:FIN],
        grads[FIN:],
        grad_bias.reshape(FIN),
    )


def solution(mesh):
    in_specs = (
        P("dom", "feat"),
        P("feat", None),
        P("feat", None),
        P("feat"),
        P("dom", "feat"),
        P("dom"),
        P("dom", None, None),
        P("dom"),
        P("dom"),
        P("dom"),
        P("dom", None),
        P("dom", None, None),
        P("dom", None),
        P("dom", None),
        P("dom"),
    )
    out_specs = (P("dom", "feat"), P("dom", "feat"), P("feat", None), P("feat", None), P("feat"))
    return jax.shard_map(
        on_device, mesh=mesh, in_specs=in_specs, out_specs=out_specs, check_vma=False
    )
```

time: 486 us -> 140 us (0.29)
  waiting for transfers between devices: 202 us -> 1.84 us
  blocking collectives: 171 us -> 52.4 us
  matrix products: 41.4 us -> 0 us
  Pallas kernels: 0 us -> 39 us
  other arithmetic: 15.1 us -> 0.03 us
  local copies, waits for them, and re-layouts: 18 us -> 8.27 us
    unnamed x4 -> x2, waiting for transfers between devices: 179 us -> 1.38 us
    psum x1 -> x0, blocking collectives: 127 us -> none  [on_device(): lax.psum((contract_rows(features, grad_full), contract_rows(mean, grad_fu...]
    dot_general x14 -> x0, matrix products: 41.4 us -> none  [the longest x1 7.78 us: on_device(): jnp.einsum('tij,tjf->tif', tiles, picked, preferred_element_type=jnp.floa...]
    pallas_call x0 -> x7, Pallas kernels: none -> 39 us  [the longest x1 10.5 us: dense(): pl.pallas_call(dense_kernel, grid_spec=pltpu.PrefetchScalarGridSpec(num_s...]
    all_to_all x0 -> x1, blocking collectives: none -> 26.2 us  [on_device(): lax.all_to_all(wire, 'dom', split_axis=0, concat_axis=0, tiled=True)]
    reduce_scatter x1 -> x0, waiting for transfers between devices: 22.8 us -> none  [on_device(): lax.psum_scatter(partial_terms.astype(jnp.bfloat16), 'feat', scatter_dime...]
    all_gather x1, blocking collectives: 44.7 us -> 26.2 us  [on_device(): pack_all = lax.all_gather(pack, 'feat', axis=0, tiled=True)]
    scatter-add x2 -> x0, other arithmetic: 10.2 us -> none  [the longest x1 9.15 us: on_device(): total.at[send_rows[0].reshape(-1)].add(returned.reshape(-1, fin_dev))]
  transfers between devices with their start and end apart: 5 -> 7, of which waited for: 2 -> 1; matrix products, arithmetic and copies ran while one was open for 5% -> 0% of each run, Pallas kernels for 0% -> 20%
where the time goes in v1:
time: 140 us
  blocking collectives  52.4 us (37%)
  Pallas kernels  39 us (28%)
  starting transfers between devices  23.1 us (16%)
  between operations  14.9 us (11%)
  local copies, waits for them, and re-layouts  8.27 us (6%)
  waiting for transfers between devices  1.84 us (1%)
    all_gather x1, blocking collectives, on_device(): pack_all = lax.all_gather(pack, 'feat', axis=0, tiled=True)  26.2 us
    all_to_all x1, blocking collectives, on_device(): lax.all_to_all(wire, 'dom', split_axis=0, concat_axis=0, tiled=True)  26.2 us
    all_to_all x1, starting transfers between devices, on_device(): lax.all_to_all(wire, 'dom', split_axis=0, concat_axis=0, tiled=True)  13.2 us
    pallas_call x1, Pallas kernels, dense(): pl.pallas_call(dense_kernel, grid_spec=pltpu.PrefetchScalarGridSpec(num_s...  10.5 us
    pallas_call x1, Pallas kernels, local_sum(): pl.pallas_call(local_kernel, grid_spec=pltpu.PrefetchScalarGridSpec(num_s...  9.45 us
    unnamed x30, local copies, waits for them, and re-layouts  7.62 us
    all_to_all x1, starting transfers between devices, on_device(): lax.all_to_all(sums, 'dom', split_axis=0, concat_axis=0, tiled=True)  6.2 us
    pallas_call x1, Pallas kernels, mean_rows(): pl.pallas_call(mean_kernel, grid=(NODES // chunk,), in_specs=[pl.BlockSpe...  5.42 us
  transfers between devices with their start and end apart: 7, of which 1 were waited for; matrix products, arithmetic and copies ran while one was open for 0% of the time, Pallas kernels for 20%

profile of v1, /device:TPU:1, one launch (start us, length us, event | category | flops | bytes accessed | tf_op | source)
XLA Modules:
  0.0 139.6 jit_solution(11827070048518698665)
XLA Ops:
  7.2 0.0 all-gather.3.cloned.1.call-start
  7.2 0.7 all-gather.3.cloned.1.call-update
  7.9 0.0 all-gather.5.cloned.1.call-start
  8.0 0.7 all-gather.5.cloned.1.call-update
  8.7 0.9 copy-done.3
  9.6 0.7 copy-done.7
  10.3 0.7 copy-done.8
  11.0 0.7 copy-done.9
  11.7 3.0 %gather_rows.1 = (bf16[1024,128]{1,0:T(8,128)(2,1)}, f32[8,2048]{1,0:T(8,128)S(1)}) custom-call(s32[4]{0:T(128)S(1)} %copy-done.8, s32[24,64]{1,0:T(8,128)S(1)} %bitcast.39, s32[1,64]{1,0:T(1,128)S(1)} %copy-done.9, bf16[64,2048]{1,0:T(8,128)(2,1)S(1)} %bitcast.35), custom_call_target="tpu_custom_call" | custom-call | flops 2147483648 | bytes 1000000 | tf_op jit(solution)/shard_map/gather_rows/pallas_call | solution.py:100
  14.7 13.2 %all-to-all-start = ((bf16[64,16,128]{2,1,0:T(8,128)(2,1)}), bf16[64,16,128]{2,1,0:T(8,128)(2,1)S(1)}, u32[]{:S(2)}, u32[]{:S(2)}) async-start(bf16[64,16,128]{2,1,0:T(8,128)(2,1)} %bitcast.5), calls=%async_computation | async-start | bytes 524288 | tf_op jit(solution)/shard_map/all_to_all | solution.py:459
  28.5 0.0 copy-start.6
  28.5 2.2 %copy-done.6 = bf16[128,128,128]{2,1,0:T(8,128)(2,1)S(1)} copy-done((bf16[128,128,128]{2,1,0:T(8,128)(2,1)S(1)}, bf16[128,128,128]{2,1,0:T(8,128)(2,1)}, u32[]{:S(2)}) %copy-start.6) | copy-done | bytes 4194328
  30.7 9.4 %local_sum.1 = (f32[64,2048]{1,0:T(8,128)S(1)}, bf16[2048,2048]{1,0:T(8,128)(2,1)}) custom-call(s32[128]{0:T(128)S(1)} %copy-done.10, s32[128]{0:T(128)S(1)} %copy-done.11, s32[1]{0:T(128)S(6)} %copy.20.count_ref, bf16[128,128,128]{2,1,0:T(8,128)(2,1)S(1)} %copy-done.6, bf16[64,2048]{1,0:T(8,128)(2,1)S(1)} %bitcast.36), custom_call_target="tpu_custom_call" | custom-call | flops 2147483648 | bytes 13000000 | tf_op jit(solution)/shard_map/local_sum/pallas_call | solution.py:152
  40.2 5.4 %mean_rows.1.mean0_ref = bf16[64,2048]{1,0:T(8,128)(2,1)S(1)} custom-call(bf16[1024,128]{1,0:T(8,128)(2,1)S(1)} %bitcast.32, bf16[2048,1536]{1,0:T(8,128)(2,1)} %halo_ref.3, bf16[2048,256]{1,0:T(8,128)(2,1)S(1)} %copy-done, f32[64,2048]{1,0:T(8,128)S(1)} %get-tuple-element.16.local_ref, s32[1,2048]{1,0:T(1,128)S(1)} %bitcast.37), custom_call_target="tpu_custom_call" | custom-call | flops 1879048192 | bytes 8000000 | tf_op jit(solution)/shard_map/mean_rows/pallas_call | solution.py:194
  45.6 2.6 %collective-permute-start.2 = (bf16[64,2048]{1,0:T(8,128)(2,1)S(1)}, bf16[64,2048]{1,0:T(8,128)(2,1)S(1)}, u32[]{:S(2)}, u32[]{:S(2)}) collective-permute-start(bf16[64,2048]{1,0:T(8,128)(2,1)S(1)} %mean_rows.1.mean0_ref), channel_id=1, source_target_pairs={{0,3},{1,0},{2,1},{3,2},{4,7},{5,4},{6,5},{7,6},{8,11},{9,8},{10,9... | collective-permute-start | bytes 786440 | tf_op jit(solution)/shard_map/ppermute | solution.py:463
  48.2 0.5 collective-permute-start.1
  48.7 0.6 collective-permute-start
  49.4 26.2 %all_gather.11 = bf16[576,256]{1,0:T(8,128)(2,1)S(1)} all-gather(bf16[144,256]{1,0:T(8,128)(2,1)S(1)} %pad_maximum_fusion), channel_id=1, replica_groups=mesh['dom'=64,'feat'=4] {'feat'}, dimensions={0}, use_global_device_ids=true | all-gather | bytes 368640 | tf_op jit(solution)/shard_map/all_gather | solution.py:455
  75.6 0.0 collective-permute-done.1.mean2_ref
  75.6 0.0 collective-permute-done.mean1_ref
  75.6 0.0 all-gather.3.cloned.1.call-done.feat_ref
  75.7 0.0 all-gather.5.cloned.1.call-done.gout_ref
  75.7 1.2 copy-done.1
  76.9 1.2 copy-done.2
  78.1 10.5 %dense.1 = (bf16[64,2048]{1,0:T(8,128)(2,1)}, bf16[64,2048]{1,0:T(8,128)(2,1)S(1)}, f32[64,2048]{1,0:T(8,128)S(1)}, bf16[1536,128]{1,0:T(8,128)(2,1)S(1)}) custom-call(s32[1]{0:T(128)} %bitcast.mine_ref, bf16[256,2048]{1,0:T(8,128)(2,1)S(1)} %copy-done.1, bf16[256,2048]{1,0:T(8,128)(2,1)S(1)} %copy-done.2, bf16[64,2048]{1,0:T(8,128)(2,1)S(1)} %mean_rows.1.mean0_ref, ...), custom_call_target="tpu_custom_call" | custom-call | flops 2147483648 | bytes 12000000 | tf_op jit(solution)/shard_map/dense/pallas_call | solution.py:297
  88.7 26.2 %all_to_all.31 = bf16[64,24,128]{2,1,0:T(8,128)(2,1)S(1)} all-to-all(bf16[64,24,128]{2,1,0:T(8,128)(2,1)S(1)} %bitcast.33), channel_id=1, replica_groups=mesh['dom'=64,'feat'=4] {'dom'}, dimensions={0} | all-to-all | bytes 786432 | tf_op jit(solution)/shard_map/all_to_all | solution.py:469
  114.8 0.7 reduce_grads.1
  115.6 6.2 %all-to-all-start.2 = ((f32[64,4,128]{2,1,0:T(4,128)}), f32[64,4,128]{2,1,0:T(4,128)S(1)}, u32[]{:S(2)}, u32[]{:S(2)}) async-start(f32[64,4,128]{2,1,0:T(4,128)} %bitcast.16), calls=%async_computation.2 | async-start | bytes 262144 | tf_op jit(solution)/shard_map/all_to_all | solution.py:472
  121.8 5.0 %local_back.1.total_ref = f32[64,2048]{1,0:T(8,128)S(1)} custom-call(f32[64,2048]{1,0:T(8,128)S(1)} %get-tuple-element.20.ginput_ref, bf16[64,2048]{1,0:T(8,128)(2,1)S(1)} %get-tuple-element.21.gmean_ref, bf16[2048,2048]{1,0:T(8,128)(2,1)} %get-tuple-element.22.adj_ref), custom_call_target="tpu_custom_call" | custom-call | flops 2147483648 | bytes 10000000 | tf_op jit(solution)/shard_map/local_back/pallas_call | solution.py:347
  126.8 4.9 %scatter_rows.1 = bf16[64,2048]{1,0:T(8,128)(2,1)} custom-call(bf16[1536,128]{1,0:T(8,128)(2,1)S(1)} %bitcast.30, f32[8,2048]{1,0:T(8,128)S(1)} %get-tuple-element.19.index_ref, f32[64,2048]{1,0:T(8,128)S(1)} %local_back.1.total_ref), custom_call_target="tpu_custom_call" | custom-call | flops 2147483648 | bytes 2000000 | tf_op jit(solution)/shard_map/scatter_rows/pallas_call | solution.py:406
  131.7 0.4 all-to-all-done.2
  132.1 0.7 slice_bitcast_fusion
  (27 shorter events, 0.1 us)
Async XLA Ops:
  7.2 21.3 %copy-start.4 = (bf16[2048,64]{0,1:T(8,128)(2,1)S(1)}, bf16[2048,64]{0,1:T(8,128)(2,1)}, u32[]{:S(2)}) copy-start(bf16[2048,64]{0,1:T(8,128)(2,1)} %param.15) | copy-start | bytes 786436
  7.2 21.3 %copy-start.11 = (s32[128]{0:T(128)S(1)}, s32[128]{0:T(128)}, u32[]{:S(2)}) copy-start(s32[128]{0:T(128)} %dst_ref.1) | copy-start | bytes 1540
  7.2 21.3 %copy-start.10 = (s32[128]{0:T(128)S(1)}, s32[128]{0:T(128)}, u32[]{:S(2)}) copy-start(s32[128]{0:T(128)} %src_ref.1) | copy-start | bytes 1540
  7.2 68.5 %all-gather.3.cloned.1.call-start = ((), (), s32[]{:S(2)}) async-start(), calls=%async_computation.3 | async-start | bytes 1310720 | tf_op jit(solution)/shard_map/all_gather | solution.py:453
  7.9 67.7 %all-gather.5.cloned.1.call-start = ((), (), s32[]{:S(2)}) async-start(), calls=%async_computation.4 | async-start | bytes 1310720 | tf_op jit(solution)/shard_map/all_gather | solution.py:454
  8.7 1.0 copy-start.3
  9.6 0.7 copy-start.7
  10.3 0.7 copy-start.8
  11.0 0.7 copy-start.9
  11.7 28.5 %copy-start.14 = (f32[64]{0:T(128)S(1)}, f32[64]{0:T(128)}, u32[]{:S(2)}) copy-start(f32[64]{0:T(128)} %param.18) | copy-start | bytes 772
  11.7 28.5 %copy-start = (bf16[2048,256]{1,0:T(8,128)(2,1)S(1)}, bf16[2048,256]{1,0:T(8,128)(2,1)}, u32[]{:S(2)}) copy-start(bf16[2048,256]{1,0:T(8,128)(2,1)} %hub_ref.5) | copy-start | bytes 3145732
  11.7 28.5 %copy-start.5 = (s32[2048]{0:T(1024)S(1)}, s32[2048]{0:T(1024)}, u32[]{:S(2)}) copy-start(s32[2048]{0:T(1024)} %param.20) | copy-start | bytes 24580
  14.7 25.5 %all-to-all-start = ((bf16[64,16,128]{2,1,0:T(8,128)(2,1)}), bf16[64,16,128]{2,1,0:T(8,128)(2,1)S(1)}, u32[]{:S(2)}, u32[]{:S(2)}) async-start(bf16[64,16,128]{2,1,0:T(8,128)(2,1)} %bitcast.5), calls=%async_computation | async-start | bytes 524288 | tf_op jit(solution)/shard_map/all_to_all | solution.py:459
  28.5 2.2 %copy-start.6 = (bf16[128,128,128]{2,1,0:T(8,128)(2,1)S(1)}, bf16[128,128,128]{2,1,0:T(8,128)(2,1)}, u32[]{:S(2)}) copy-start(bf16[128,128,128]{2,1,0:T(8,128)(2,1)} %tiles_ref.1) | copy-start | bytes 12582916
  30.7 18.6 %copy-start.12 = (bf16[64,256]{1,0:T(8,128)(2,1)S(1)}, bf16[64,256]{1,0:T(8,128)(2,1)}, u32[]{:S(2)}) copy-start(bf16[64,256]{1,0:T(8,128)(2,1)} %param.17) | copy-start | bytes 98308
  30.7 18.6 %copy-start.13 = (bf16[64,256]{1,0:T(8,128)(2,1)S(1)}, bf16[64,256]{1,0:T(8,128)(2,1)}, u32[]{:S(2)}) copy-start(bf16[64,256]{1,0:T(8,128)(2,1)} %param.16) | copy-start | bytes 98308
  45.6 30.0 %collective-permute-start.2 = (bf16[64,2048]{1,0:T(8,128)(2,1)S(1)}, bf16[64,2048]{1,0:T(8,128)(2,1)S(1)}, u32[]{:S(2)}, u32[]{:S(2)}) collective-permute-start(bf16[64,2048]{1,0:T(8,128)(2,1)S(1)} %mean_rows.1.mean0_ref), channel_id=1, source_target_pairs={{0,3},{1,0},{2,1},{3,2},{4,7},{5,4},{6,5},{7,6},{8,11},{9,8},{10,9... | collective-permute-start | bytes 786440 | tf_op jit(solution)/shard_map/ppermute | solution.py:463
  48.2 27.4 %collective-permute-start.1 = (bf16[64,2048]{1,0:T(8,128)(2,1)S(1)}, bf16[64,2048]{1,0:T(8,128)(2,1)S(1)}, u32[]{:S(2)}, u32[]{:S(2)}) collective-permute-start(bf16[64,2048]{1,0:T(8,128)(2,1)S(1)} %mean_rows.1.mean0_ref), channel_id=1, source_target_pairs={{0,2},{1,3},{2,0},{3,1},{4,6},{5,7},{6,4},{7,5},{8,10},{9,11},{10,... | collective-permute-start | bytes 786440 | tf_op jit(solution)/shard_map/ppermute | solution.py:463
  48.7 26.9 %collective-permute-start = (bf16[64,2048]{1,0:T(8,128)(2,1)S(1)}, bf16[64,2048]{1,0:T(8,128)(2,1)S(1)}, u32[]{:S(2)}, u32[]{:S(2)}) collective-permute-start(bf16[64,2048]{1,0:T(8,128)(2,1)S(1)} %mean_rows.1.mean0_ref), channel_id=1, source_target_pairs={{0,1},{1,2},{2,3},{3,0},{4,5},{5,6},{6,7},{7,4},{8,9},{9,10},{10,1... | collective-permute-start | bytes 786440 | tf_op jit(solution)/shard_map/ppermute | solution.py:463
  75.7 1.2 copy-start.1
  76.9 1.2 copy-start.2
  115.6 16.5 %all-to-all-start.2 = ((f32[64,4,128]{2,1,0:T(4,128)}), f32[64,4,128]{2,1,0:T(4,128)S(1)}, u32[]{:S(2)}, u32[]{:S(2)}) async-start(f32[64,4,128]{2,1,0:T(4,128)} %bitcast.16), calls=%async_computation.2 | async-start | bytes 262144 | tf_op jit(solution)/shard_map/all_to_all | solution.py:472
Sparse Core Ops, SparseCore 0:
  9.8 29.3 all-gather.2
  41.1 32.8 all-gather.4

commit v2 on v0

v2 whole, which is shorter than its diff:
```python
import jax
import jax.numpy as jnp
from jax import lax
from jax.experimental import pallas as pl
from jax.experimental.pallas import tpu as pltpu
from jax.sharding import PartitionSpec as P

BF = jnp.bfloat16
F32 = jnp.float32
I32 = jnp.int32

PEERS = 64
FEATS = 4
SLOT = 24
HUBS = 4
ROWS = 16
WIDE = 24
LANES = 128
FIN = 64
FOUT = 256
NODES = 2048
BLOCK = 128
TILES = 128
HALO = PEERS * SLOT
HUB_ALL = PEERS * HUBS
BUNDLE = 160
PACK = 2 * FIN
HALF = NODES // 2
SLOTS = PEERS * ROWS
CHUNK = 256

def matmul(left, right):
    return lax.dot_general(
        left, right, (((1,), (0,)), ((), ())), preferred_element_type=F32
    )


def matmul_nt(left, right):
    return lax.dot_general(
        left, right, (((1,), (1,)), ((), ())), preferred_element_type=F32
    )


def params(mebibytes=24):
    return pltpu.CompilerParams(vmem_limit_bytes=mebibytes * 1024 * 1024)


def cost(flops, moved):
    return pl.CostEstimate(flops=flops, bytes_accessed=moved, transcendentals=0)


def in_vmem(count):
    return [pl.BlockSpec(memory_space=pltpu.VMEM)] * count


def in_hbm(count):
    return [pl.BlockSpec(memory_space=pltpu.HBM)] * count


def keep_hbm(*values):
    return [pltpu.with_memory_space_constraint(value, pltpu.HBM) for value in values]


def iota(shape, axis):
    return lax.broadcasted_iota(I32, shape, axis)


def pick_hubs():
    hub = iota((HUB_ALL, PEERS * 8), 0)
    place = iota((HUB_ALL, PEERS * 8), 1)
    same = (hub // HUBS == place // 8) & (hub % HUBS == place % 8)
    return same.astype(F32).astype(BF)


def start_all(pairs, sems):
    copies = [
        pltpu.make_async_copy(src, dst, sems.at[i]) for i, (src, dst) in enumerate(pairs)
    ]
    for copy in copies:
        copy.start()
    return copies


def slot_targets(hub_ref, send_ref, count_ref):
    slot = iota((SLOT, PEERS), 0)
    sent = jnp.where(slot < count_ref[...], send_ref[...], -1)
    place = iota((8, PEERS), 0)
    hubs = jnp.full((8, PEERS), -1, I32)
    for h in range(HUBS):
        hubs = jnp.where(place == h, hub_ref[h], hubs)
    rows = jnp.concatenate([sent, hubs], axis=0)
    high = lax.shift_right_arithmetic(rows, 6)
    low = rows - high * 64
    split = jnp.concatenate([high, low], axis=0).astype(F32).astype(BF)
    spread = (iota((PEERS, SLOTS), 0) == iota((PEERS, SLOTS), 1) // ROWS)
    wide = matmul(split, spread.astype(F32).astype(BF))
    wide = wide[:32] * 64.0 + wide[32:]
    mine = iota((ROWS, SLOTS), 0) == iota((ROWS, SLOTS), 1) % ROWS
    left = jnp.sum(jnp.where(mine, wide[:ROWS], 0.0), axis=0, keepdims=True)
    right = jnp.sum(jnp.where(mine, wide[ROWS:], 0.0), axis=0, keepdims=True)
    return jnp.concatenate([left, right], axis=1)


def front_kernel(
    hub_hbm, send_hbm, count_hbm, feat_hbm, gout_hbm, self_hbm, neigh_hbm, bias_hbm, degree_hbm,
    wire_ref, index_ref, bundle_hbm,
    hub_ref, send_ref, count_ref, self_ref, neigh_ref, bias_ref, degree_ref, bundle_ref, sems,
    out_sem,
):
    pairs = [
        (hub_hbm, hub_ref),
        (send_hbm, send_ref),
        (count_hbm, count_ref),
        (feat_hbm, bundle_ref.at[pl.ds(0, FIN)]),
        (self_hbm, self_ref),
        (neigh_hbm, neigh_ref),
        (bias_hbm, bias_ref),
        (degree_hbm, degree_ref),
        (gout_hbm, bundle_ref.at[pl.ds(FIN, FIN)]),
    ]
    copies = start_all(pairs, sems)
    for copy in copies[:3]:
        copy.wait()
    both = slot_targets(hub_ref, send_ref, count_ref)
    index_ref[:8] = jnp.broadcast_to(both, (8, 2 * SLOTS))
    for copy in copies[4:8]:
        copy.wait()
    index_ref[8:] = jnp.broadcast_to(degree_ref[...].astype(F32), (8, NODES))
    for i in range(4):
        rows = slice(16 * i, 16 * i + 16)
        bundle_ref[PACK:PACK + 16, FOUT * i:FOUT * (i + 1)] = self_ref[rows]
        bundle_ref[PACK:PACK + 16, FOUT * (i + 4):FOUT * (i + 5)] = neigh_ref[rows]
    bias = bias_ref[...]
    high = bias.astype(BF).astype(F32)
    middle = (bias - high).astype(BF).astype(F32)
    low = bias - high - middle
    place = iota((16, FIN), 0)
    parts = jnp.where(
        place == 0, high, jnp.where(place == 1, middle, jnp.where(place == 2, low, 0.0))
    )
    parts = jnp.concatenate([parts, jnp.zeros((16, LANES - FIN), F32)], axis=1).astype(BF)
    bundle_ref[PACK + 16:] = jnp.zeros((16, NODES), BF)
    bundle_ref[PACK + 16:, :LANES] = parts
    copies[3].wait()
    copies[8].wait()
    (outgoing,) = start_all([(bundle_ref, bundle_hbm)], out_sem)
    target = both.astype(I32)
    step = 256
    total = jnp.zeros((FIN, 2 * SLOTS), F32)
    node = iota((step, 2 * SLOTS), 0)
    for k in range(NODES // step):
        hot = (node == target - k * step).astype(F32).astype(BF)
        total += matmul(bundle_ref[:FIN, k * step:(k + 1) * step], hot)
    stacked = jnp.concatenate([total[:, :SLOTS], total[:, SLOTS:]], axis=0)
    wire_ref[...] = stacked.T.astype(BF)
    outgoing.wait()


def front(*operands):
    return pl.pallas_call(
        front_kernel,
        in_specs=in_hbm(9),
        out_specs=in_vmem(2) + in_hbm(1),
        out_shape=[
            jax.ShapeDtypeStruct((SLOTS, LANES), BF),
            pltpu.VMEM((16, NODES), F32),
            pltpu.HBM((BUNDLE, NODES), BF),
        ],
        scratch_shapes=[
            pltpu.SMEM((HUBS,), I32),
            pltpu.VMEM((SLOT, PEERS), I32),
            pltpu.VMEM((1, PEERS), I32),
            pltpu.VMEM((FIN, FOUT), BF),
            pltpu.VMEM((FIN, FOUT), BF),
            pltpu.VMEM((1, FIN), F32),
            pltpu.VMEM((1, NODES), I32),
            pltpu.VMEM((BUNDLE, NODES), BF),
            pltpu.SemaphoreType.DMA((9,)),
            pltpu.SemaphoreType.DMA((1,)),
        ],
        compiler_params=params(),
        cost_estimate=cost(2 * 2 * SLOTS * NODES * 256, 1000000),
        name="front",
    )(*keep_hbm(*operands))


def local_kernel(
    count_ref, src_hbm, dst_hbm, tiles_hbm, bundle_hbm, sum_ref, adj_hbm,
    src_ref, dst_ref, feat_ref, tiles_ref, adj_ref, sems, tile_sems, out_sems,
):
    small = start_all(
        [(src_hbm, src_ref), (dst_hbm, dst_ref), (bundle_hbm.at[pl.ds(0, FIN)], feat_ref)], sems
    )
    groups = tile_sems.shape[0]
    group = TILES // groups
    here = [pl.ds(g * group, group) for g in range(groups)]
    incoming = start_all([(tiles_hbm.at[g], tiles_ref.at[g]) for g in here], tile_sems)
    adj_ref[...] = jnp.zeros_like(adj_ref)
    for copy in small:
        copy.wait()
    for g in range(groups):
        incoming[g].wait()
        for j in range(group):
            t = g * group + j

            @pl.when(t < count_ref[0])
            def add():
                rows = pl.ds(pl.multiple_of(dst_ref[t] * BLOCK, BLOCK), BLOCK)
                cols = pl.ds(pl.multiple_of(src_ref[t] * BLOCK, BLOCK), BLOCK)
                adj_ref[rows, cols] += tiles_ref[t]

    width = 256
    here = [pl.ds(k * width, width) for k in range(NODES // width)]
    outgoing = start_all([(adj_ref.at[k], adj_hbm.at[k]) for k in here], out_sems)
    for k in range(NODES // width):
        part = adj_ref[k * width:(k + 1) * width, :]
        sum_ref[:, k * width:(k + 1) * width] = matmul_nt(feat_ref[...], part)
    for copy in outgoing:
        copy.wait()


def local_sum(src, dst, count, tiles, packed):
    return pl.pallas_call(
        local_kernel,
        in_specs=[pl.BlockSpec(memory_space=pltpu.SMEM)] + in_hbm(4),
        out_specs=in_vmem(1) + in_hbm(1),
        out_shape=[
            pltpu.VMEM((FIN, NODES), F32),
            pltpu.HBM((NODES, NODES), BF),
        ],
        scratch_shapes=[
            pltpu.SMEM((TILES,), I32),
            pltpu.SMEM((TILES,), I32),
            pltpu.VMEM((FIN, NODES), BF),
            pltpu.VMEM((TILES, BLOCK, BLOCK), BF),
            pltpu.VMEM((NODES, NODES), BF),
            pltpu.SemaphoreType.DMA((3,)),
            pltpu.SemaphoreType.DMA((8,)),
            pltpu.SemaphoreType.DMA((8,)),
        ],
        compiler_params=params(),
        cost_estimate=cost(2 * NODES * NODES * 256, 13000000),
        name="local_sum",
    )(count, *keep_hbm(src, dst, tiles, packed))


def adjacency_copies(part, pieces, halo_hbm, hub_hbm, halo_ref, hub_ref, sems):
    piece = HALF // pieces
    pairs = []
    for i in range(pieces):
        there = pl.ds(part * HALF + i * piece, piece)
        pairs.append((halo_hbm.at[there], halo_ref.at[pl.ds(i * piece, piece)]))
    pairs.append((hub_hbm.at[pl.ds(part * HALF, HALF)], hub_ref))
    return start_all(pairs, sems)


def mean_half(part, rows, hubs, halo_ref, hub_ref, local_ref, index_ref, mean_ref, ready):
    chunk = 512
    for i in range(HALF // chunk):
        ready(i)
        here = slice(i * chunk, (i + 1) * chunk)
        whole = slice(part * HALF + i * chunk, part * HALF + (i + 1) * chunk)
        total = matmul(halo_ref[here], rows) + matmul(hub_ref[here], hubs)
        total = total.T + local_ref[:, whole]
        mean_ref[:, here] = (total / index_ref[8:9, whole]).astype(BF)


def first_mean_kernel(
    wire_ref, local_ref, index_ref, halo_hbm, hub_hbm,
    mean_ref, rows_ref, hubs_ref, later_halo, later_hub,
    halo_ref, hub_ref, sems, later_sems,
):
    copies = adjacency_copies(0, 2, halo_hbm, hub_hbm, halo_ref, hub_ref, sems)
    later = []
    wire = wire_ref[...].astype(F32).reshape(PEERS, ROWS, LANES)
    left = wire[:, :, :FIN]
    right = wire[:, :, FIN:]
    rows = jnp.concatenate([left, right[:, :8]], axis=1)
    rows_ref[...] = rows.reshape(HALO, FIN).astype(BF)
    owned = right[:, 8:].reshape(PEERS * 8, FIN).astype(BF)
    hubs_ref[...] = matmul(pick_hubs(), owned).astype(BF)
    copies[-1].wait()

    def ready(i):
        copies[i].wait()
        if i:
            later.extend(
                adjacency_copies(1, 2, halo_hbm, hub_hbm, later_halo, later_hub, later_sems)
            )

    mean_half(
        0, rows_ref[...], hubs_ref[...], halo_ref, hub_ref, local_ref, index_ref, mean_ref, ready
    )
    for copy in later:
        copy.wait()


def later_mean_kernel(rows_ref, hubs_ref, halo_ref, hub_ref, local_ref, index_ref, mean_ref):
    mean_half(
        1, rows_ref[...], hubs_ref[...], halo_ref, hub_ref, local_ref, index_ref, mean_ref,
        lambda i: None,
    )


def first_mean(wire, halo_adj, hub_adj, local, index):
    shapes = [(FIN, HALF), (HALO, FIN), (HUB_ALL, FIN), (HALF, HALO), (HALF, HUB_ALL)]
    return pl.pallas_call(
        first_mean_kernel,
        in_specs=in_vmem(3) + in_hbm(2),
        out_specs=in_vmem(len(shapes)),
        out_shape=[pltpu.VMEM(shape, BF) for shape in shapes],
        scratch_shapes=[
            pltpu.VMEM((HALF, HALO), BF),
            pltpu.VMEM((HALF, HUB_ALL), BF),
            pltpu.SemaphoreType.DMA((3,)),
            pltpu.SemaphoreType.DMA((3,)),
        ],
        compiler_params=params(),
        cost_estimate=cost(HALF * (HALO + HUB_ALL) * 512, 1000000),
        name="mean_rows",
    )(wire, local, index, *keep_hbm(halo_adj, hub_adj))


def later_mean(known, local, index):
    return pl.pallas_call(
        later_mean_kernel,
        in_specs=in_vmem(6),
        out_specs=in_vmem(1)[0],
        out_shape=pltpu.VMEM((FIN, HALF), BF),
        compiler_params=params(),
        cost_estimate=cost(HALF * (HALO + HUB_ALL) * 512, 1000000),
        name="mean_rows",
    )(*known, local, index)


def prepare_weights(mine, packs, weight_ref, bias_ref, back_ref):
    eye = iota((FIN, FIN), 0) == iota((FIN, FIN), 1)
    for k in range(FEATS):
        pieces = [
            packs[k, :16, FOUT * i:FOUT * (i + 1)].astype(F32) for i in range(8)
        ]
        turned = jnp.concatenate(pieces, axis=0).T.astype(BF)
        for b in range(FEATS):
            place = lax.rem(b - mine + FEATS, FEATS)
            rows = pl.ds(pl.multiple_of(place * FIN, FIN), FIN)
            weight_ref[k, rows, :] = turned[b * FIN:(b + 1) * FIN]
        parts = packs[k, 16:, :LANES].astype(F32)
        row = parts[0:1, :FIN] + parts[1:2, :FIN] + parts[2:3, :FIN]
        column = jnp.sum(jnp.where(eye, row, 0.0), axis=1, keepdims=True)
        bias_ref[k * FIN:(k + 1) * FIN, :] = jnp.broadcast_to(column, (FIN, LANES))
    back_ref[...] = weight_ref[0].astype(F32).T.astype(BF)


def ship_gradients(mine, halo_acc, hub_acc, grad_acc, wire_ref):
    rows = halo_acc[...].T.reshape(PEERS, SLOT, FIN)
    hubs = matmul(hub_acc[...].astype(BF), pick_hubs()).T.reshape(PEERS, 8, FIN)
    row = grad_acc[2 * FIN:2 * FIN + 1, :FIN]
    high = row.astype(BF).astype(F32)
    place = iota((8, FIN), 0)
    extra = jnp.where(place == 4, high, jnp.where(place == 5, row - high, 0.0))
    hubs = hubs + extra[None]
    right = jnp.concatenate([rows[:, 16:], hubs], axis=1)
    main = jnp.concatenate([rows[:, :16], right], axis=2)
    grads = pltpu.roll(grad_acc[:2 * FIN, :], mine * FIN, 1).reshape(16, 8, FOUT)
    grads = jnp.stack([grads[:, :, :LANES], grads[:, :, LANES:]], axis=1)
    grads = grads.reshape(32, 8, LANES)
    high = grads.astype(BF).astype(F32)
    low = grads - high
    swap = lambda x: jnp.concatenate([x[:, 4:], x[:, :4]], axis=1)
    first = iota((32, 8, LANES), 1) < 4
    even = jnp.where(first, high, swap(low))
    odd = jnp.where(first, swap(high), low)
    pieces = jnp.stack([even, odd], axis=1).reshape(PEERS, 8, LANES)
    wire = jnp.concatenate([main, pieces], axis=1)
    wire_ref[...] = wire.reshape(PEERS * WIDE, LANES).astype(BF)


def value_copies(part, bundles, value_ref, sems):
    own = pl.ds(part * HALF, HALF)
    return start_all(
        [(bundles[k].at[pl.ds(0, PACK), own], value_ref.at[k]) for k in range(FEATS)], sems
    )


def mean_copies(means, mean_ref, sems):
    return start_all([(means[k], mean_ref.at[k]) for k in range(FEATS - 1)], sems)


def dense_half(
    part, own_mean, mean_ref, value_ref, weight_ref, bias_ref, back_ref, index_ref, copies,
    halo_ref, hub_ref, out_ref, gmean_ref, ginput_ref, gpre_ref,
):
    chunk = CHUNK
    for i in range(HALF // chunk):
        here = slice(i * chunk, (i + 1) * chunk)
        whole = slice(part * HALF + i * chunk, part * HALF + (i + 1) * chunk)
        pre = jnp.tile(bias_ref[...], (1, chunk // LANES))
        for k in range(FEATS):
            mean = mean_ref[k - 1, :, here] if k else own_mean[:, here]
            both = jnp.concatenate([value_ref[k, :FIN, here], mean], axis=0)
            pre = pre + matmul(weight_ref[k], both).astype(BF).astype(F32)
        sigma = 1.0 / (1.0 + jnp.exp(-pre))
        out_ref[:, here] = (pre[:FIN] * sigma[:FIN]).astype(BF)
        slope = sigma * (1.0 + pre * (1.0 - sigma))
        gout = jnp.concatenate([value_ref[k, FIN:, here] for k in range(FEATS)], axis=0)
        gpre = (gout.astype(F32) * slope).astype(BF)
        gpre_ref[:, here] = gpre
        back = matmul(back_ref[...], gpre)
        ginput_ref[:, here] = back[:FIN]
        gmean_ref[:, here] = (back[FIN:] / index_ref[8:9, whole]).astype(BF)
    left = jnp.concatenate([value_ref[0, :FIN], own_mean[...], jnp.ones((16, HALF), BF)], axis=0)
    grads = matmul_nt(left, gpre_ref[...])
    for copy in copies:
        copy.wait()
    halos = matmul(gmean_ref[...], halo_ref[...])
    hubs = matmul(gmean_ref[...], hub_ref[...])
    return halos, hubs, grads


def first_dense_kernel(mine_ref, own_mean, index_ref, *refs):
    bundles, means, halo_hbm, hub_hbm = refs[:4], refs[4:7], refs[7], refs[8]
    out_ref, gmean_ref, ginput_ref, halo_acc, hub_acc, grad_acc = refs[9:15]
    weight_ref, bias_ref, back_ref, later_ref = refs[15:19]
    gpre_ref, halo_ref, hub_ref, pack_ref, value_ref, mean_ref = refs[19:25]
    pack_sems, value_sems, mean_sems, sems, later_sems = refs[25:]
    packs = start_all(
        [(bundles[k].at[pl.ds(PACK, 32)], pack_ref.at[k]) for k in range(FEATS)], pack_sems
    )
    ready = value_copies(0, bundles, value_ref, value_sems)
    ready = ready + mean_copies(means, mean_ref, mean_sems)
    copies = adjacency_copies(0, 4, halo_hbm, hub_hbm, halo_ref, hub_ref, sems)
    later = value_copies(1, bundles, later_ref, later_sems)
    for copy in packs:
        copy.wait()
    prepare_weights(mine_ref[0], pack_ref, weight_ref, bias_ref, back_ref)
    for copy in ready:
        copy.wait()
    halo_acc[...], hub_acc[...], grad_acc[...] = dense_half(
        0, own_mean, mean_ref, value_ref, weight_ref, bias_ref, back_ref, index_ref, copies,
        halo_ref, hub_ref, out_ref, gmean_ref, ginput_ref, gpre_ref,
    )
    for copy in later:
        copy.wait()


def later_dense_kernel(mine_ref, own_mean, index_ref, *refs):
    held_halo, held_hub, held_grad, weight_ref, bias_ref, back_ref, value_ref = refs[:7]
    means, halo_hbm, hub_hbm = refs[7:10], refs[10], refs[11]
    out_ref, gmean_ref, ginput_ref, wire_ref = refs[12:16]
    gpre_ref, halo_ref, hub_ref, halo_acc, hub_acc, grad_acc, mean_ref = refs[16:23]
    mean_sems, sems = refs[23:]
    ready = mean_copies(means, mean_ref, mean_sems)
    copies = adjacency_copies(1, 4, halo_hbm, hub_hbm, halo_ref, hub_ref, sems)
    for copy in ready:
        copy.wait()
    halos, hubs, grads = dense_half(
        1, own_mean, mean_ref, value_ref, weight_ref, bias_ref, back_ref, index_ref, copies,
        halo_ref, hub_ref, out_ref, gmean_ref, ginput_ref, gpre_ref,
    )
    halo_acc[...] = held_halo[...] + halos
    hub_acc[...] = held_hub[...] + hubs
    grad_acc[...] = held_grad[...] + grads
    ship_gradients(mine_ref[0], halo_acc, hub_acc, grad_acc, wire_ref)


ACCUMULATORS = [(FIN, HALO), (FIN, HUB_ALL), (PACK + 16, FOUT)]


def dense(part, mine, bundles, means, index, halo_adj, hub_adj, held):
    out_shape = [
        jax.ShapeDtypeStruct((FIN, HALF), BF),
        jax.ShapeDtypeStruct((FIN, HALF), BF),
        jax.ShapeDtypeStruct((FIN, HALF), F32),
    ]
    scratch = [
        pltpu.VMEM((FOUT, HALF), BF),
        pltpu.VMEM((HALF, HALO), BF),
        pltpu.VMEM((HALF, HUB_ALL), BF),
    ]
    remote = pltpu.VMEM((FEATS - 1, FIN, HALF), BF)
    value = pltpu.VMEM((FEATS, PACK, HALF), BF)
    if part == 0:
        out_shape += [pltpu.VMEM(shape, F32) for shape in ACCUMULATORS]
        out_shape += [
            pltpu.VMEM((FEATS, FOUT, PACK), BF),
            pltpu.VMEM((FOUT, LANES), F32),
            pltpu.VMEM((PACK, FOUT), BF),
            value,
        ]
        scratch += [pltpu.VMEM((FEATS, 32, NODES), BF), value, remote]
        counts = [4, 4, 3, 5, 4]
        far = keep_hbm(*bundles, *means[1:], halo_adj, hub_adj)
    else:
        out_shape += [jax.ShapeDtypeStruct((PEERS * WIDE, LANES), BF)]
        scratch += [pltpu.VMEM(shape, F32) for shape in ACCUMULATORS] + [remote]
        counts = [3, 5]
        far = keep_hbm(*means[1:], halo_adj, hub_adj)
    scratch += [pltpu.SemaphoreType.DMA((count,)) for count in counts]
    return pl.pallas_call(
        later_dense_kernel if part else first_dense_kernel,
        in_specs=[pl.BlockSpec(memory_space=pltpu.SMEM)]
        + in_vmem(2 + len(held))
        + in_hbm(len(far)),
        out_specs=in_vmem(len(out_shape)),
        out_shape=out_shape,
        scratch_shapes=scratch,
        compiler_params=params(),
        cost_estimate=cost(NODES * 2048 * 256, 6000000),
        name="dense",
    )(mine, means[0], index, *held, *far)


def back_kernel(
    ginput0, ginput1, gmean0, gmean1, out0, out1, adj_hbm, total_ref, out_ref, adj_ref, sems
):
    chunk = 512
    here = [pl.ds(i * chunk, chunk) for i in range(NODES // chunk)]
    blocks = start_all([(adj_hbm.at[:, i], adj_ref.at[:, i]) for i in here], sems)
    out_ref[:, :HALF] = out0[...]
    out_ref[:, HALF:] = out1[...]
    for i in range(NODES // chunk):
        blocks[i].wait()
        here = slice(i * chunk, (i + 1) * chunk)
        total = matmul(gmean0[...], adj_ref[:HALF, here])
        total = total + matmul(gmean1[...], adj_ref[HALF:, here])
        half = ginput0 if i * chunk < HALF else ginput1
        start = i * chunk % HALF
        total_ref[:, here] = total + half[:, start:start + chunk]


def local_back(ginputs, gmeans, outs, adj):
    return pl.pallas_call(
        back_kernel,
        in_specs=in_vmem(6) + in_hbm(1),
        out_specs=in_vmem(2),
        out_shape=[
            pltpu.VMEM((FIN, NODES), F32),
            jax.ShapeDtypeStruct((FIN, NODES), BF),
        ],
        scratch_shapes=[
            pltpu.VMEM((NODES, NODES), BF),
            pltpu.SemaphoreType.DMA((4,)),
        ],
        compiler_params=params(),
        cost_estimate=cost(2 * NODES * NODES * 256, 10000000),
        name="local_back",
    )(*ginputs, *gmeans, *outs, *keep_hbm(adj))


def reduce_kernel(wire_ref, sums_ref, bias_ref):
    wire = wire_ref[...].astype(F32).reshape(PEERS, WIDE, LANES)
    pieces = jnp.sum(wire[:, 16:], axis=0)
    half = pieces[:4] + pieces[4:]
    both = jnp.concatenate([half, half], axis=0)
    sums_ref[...] = jnp.broadcast_to(both[None], (PEERS // 2, 8, LANES)).reshape(
        PEERS * 4, LANES
    )
    tail = jnp.sum(wire[:, 8:16], axis=0)
    bias_ref[...] = tail[4:5, FIN:] + tail[5:6, FIN:]


def reduce_grads(wire):
    return pl.pallas_call(
        reduce_kernel,
        out_shape=[
            jax.ShapeDtypeStruct((PEERS * 4, LANES), F32),
            jax.ShapeDtypeStruct((1, FIN), F32),
        ],
        compiler_params=params(),
        in_specs=in_vmem(1),
        out_specs=in_vmem(2),
        cost_estimate=cost(1000000, 1000000),
        name="reduce_grads",
    )(wire)


def scatter_kernel(wire_ref, index_ref, total_ref, out_ref):
    wire = wire_ref[...].astype(F32).reshape(PEERS, WIDE, LANES)
    both = wire[:, :16].reshape(SLOTS, LANES).T
    back = jnp.concatenate([both[:FIN], both[FIN:]], axis=1).astype(BF)
    chunk = 256
    target = index_ref[0:1, :].astype(I32)
    node = iota((chunk, 2 * SLOTS), 0)
    for k in range(NODES // chunk):
        here = slice(k * chunk, (k + 1) * chunk)
        hot = (node == target - k * chunk).astype(F32).astype(BF)
        out_ref[:, here] = (total_ref[:, here] + matmul_nt(back, hot)).astype(BF)


def scatter_rows(wire, index, total):
    return pl.pallas_call(
        scatter_kernel,
        in_specs=in_vmem(3),
        out_specs=in_vmem(1)[0],
        out_shape=jax.ShapeDtypeStruct((FIN, NODES), BF),
        compiler_params=params(),
        cost_estimate=cost(2 * 2 * SLOTS * NODES * 256, 2000000),
        name="scatter_rows",
    )(wire, index, total)


def from_feat(value):
    shifted = [
        lax.ppermute(value, "feat", [(j, (j - k) % FEATS) for j in range(FEATS)])
        for k in range(1, FEATS)
    ]
    return [value] + shifted


def on_device(
    features,
    w_self,
    w_neigh,
    bias,
    grad_out,
    degree,
    tiles,
    tile_src,
    tile_dst,
    tile_count,
    halo_adj,
    send_rows,
    send_count,
    hub_adj,
    hub_local,
):
    feat = features.T
    gout = grad_out.T
    mine = lax.axis_index("feat").astype(I32).reshape(1)
    degree = degree.reshape(1, NODES)
    send = jnp.transpose(send_rows[0])
    wire, index, packed = front(
        hub_local, send, send_count, feat, gout, w_self, w_neigh, bias.reshape(1, FIN), degree
    )
    bundles = from_feat(packed)
    arrived = lax.all_to_all(wire, "dom", split_axis=0, concat_axis=0, tiled=True)
    local, adj = local_sum(tile_src, tile_dst, tile_count, tiles, packed)
    mean, *known = first_mean(arrived, halo_adj, hub_adj, local, index)
    mean, bundles = lax.optimization_barrier((mean, bundles))
    first = from_feat(mean)
    mean = later_mean(known, local, index)
    second = from_feat(mean)
    out0, gmean0, ginput0, *held = dense(0, mine, bundles, first, index, halo_adj, hub_adj, [])
    out1, gmean1, ginput1, wire = dense(1, mine, bundles, second, index, halo_adj, hub_adj, held)
    returned = lax.all_to_all(wire, "dom", split_axis=0, concat_axis=0, tiled=True)
    total, out = local_back([ginput0, ginput1], [gmean0, gmean1], [out0, out1], adj)
    returned, total = lax.optimization_barrier((returned, total))
    sums, grad_bias = reduce_grads(returned)
    shared = lax.all_to_all(sums, "dom", split_axis=0, concat_axis=0, tiled=True)
    grad_features = scatter_rows(returned, index, total)
    grads = shared.reshape(16, 2, 8, LANES).transpose(0, 2, 1, 3).reshape(PACK, FOUT)
    return (
        out.T,
        grad_features.T,
        grads[:FIN],
        grads[FIN:],
        grad_bias.reshape(FIN),
    )


def solution(mesh):
    in_specs = (
        P("dom", "feat"),
        P("feat", None),
        P("feat", None),
        P("feat"),
        P("dom", "feat"),
        P("dom"),
        P("dom", None, None),
        P("dom"),
        P("dom"),
        P("dom"),
        P("dom", None),
        P("dom", None, None),
        P("dom", None),
        P("dom", None),
        P("dom"),
    )
    out_specs = (P("dom", "feat"), P("dom", "feat"), P("feat", None), P("feat", None), P("feat"))
    return jax.shard_map(
        on_device, mesh=mesh, in_specs=in_specs, out_specs=out_specs, check_vma=False
    )
```

time: 486 us -> 107 us (0.22)
  waiting for transfers between devices: 202 us -> 24 us
  blocking collectives: 171 us -> 0 us
  matrix products: 41.4 us -> 0 us
  Pallas kernels: 0 us -> 36.8 us
  starting transfers between devices: 21.9 us -> 42.2 us
  local copies, waits for them, and re-layouts: 18 us -> 2.03 us
  other arithmetic: 15.1 us -> 0 us
  between operations: 15.6 us -> 1.49 us
    unnamed x4 -> x0, waiting for transfers between devices: 179 us -> none
    psum x1 -> x0, blocking collectives: 127 us -> none  [on_device(): lax.psum((contract_rows(features, grad_full), contract_rows(mean, grad_fu...]
    all_gather x1 -> x0, blocking collectives: 44.7 us -> none  [on_device(): hub_rows = lax.all_gather(own_hubs, 'dom', axis=0, tiled=True)]
    dot_general x14 -> x0, matrix products: 41.4 us -> none  [the longest x1 7.78 us: on_device(): jnp.einsum('tij,tjf->tif', tiles, picked, preferred_element_type=jnp.floa...]
    pallas_call x0 -> x9, Pallas kernels: none -> 36.8 us  [the longest x2 11.2 us: dense(): pl.pallas_call(later_dense_kernel if part else first_dense_kernel, in_spe...]
    reduce_scatter x1 -> x0, waiting for transfers between devices: 22.8 us -> none  [on_device(): lax.psum_scatter(partial_terms.astype(jnp.bfloat16), 'feat', scatter_dime...]
    all_to_all x2 -> x3, waiting for transfers between devices: 0.01 us -> 21.5 us  [the longest x2 14.5 us: on_device(): lax.all_to_all(wire, 'dom', split_axis=0, concat_axis=0, tiled=True)]
    ppermute x0 -> x9, starting transfers between devices: none -> 11 us  [from_feat(): lax.ppermute(value, 'feat', [(j, (j - k) % FEATS) for j in range(FEATS)])]
  transfers between devices with their start and end apart: 5 -> 12, of which waited for: 2 -> 5; matrix products, arithmetic and copies ran while one was open for 5% -> 0% of each run, Pallas kernels for 0% -> 25%
where the time goes in v2:
time: 107 us
  starting transfers between devices  42.2 us (39%)
  Pallas kernels  36.8 us (34%)
  waiting for transfers between devices  24 us (22%)
  local copies, waits for them, and re-layouts  2.03 us (2%)
  between operations  1.49 us (1%)
    all_to_all x2, starting transfers between devices, on_device(): lax.all_to_all(wire, 'dom', split_axis=0, concat_axis=0, tiled=True)  25 us
    all_to_all x2, waiting for transfers between devices, on_device(): lax.all_to_all(wire, 'dom', split_axis=0, concat_axis=0, tiled=True)  14.5 us
    pallas_call x2, Pallas kernels, dense(): pl.pallas_call(later_dense_kernel if part else first_dense_kernel, in_spe...  11.2 us
    ppermute x9, starting transfers between devices, from_feat(): lax.ppermute(value, 'feat', [(j, (j - k) % FEATS) for j in range(FEATS)])  11 us
    pallas_call x1, Pallas kernels, local_sum(): pl.pallas_call(local_kernel, in_specs=[pl.BlockSpec(memory_space=pltpu.SM...  7.19 us
    all_to_all x1, waiting for transfers between devices, on_device(): lax.all_to_all(sums, 'dom', split_axis=0, concat_axis=0, tiled=True)  6.98 us
    all_to_all x1, starting transfers between devices, on_device(): lax.all_to_all(sums, 'dom', split_axis=0, concat_axis=0, tiled=True)  6.2 us
    pallas_call x1, Pallas kernels, first_mean(): pl.pallas_call(first_mean_kernel, in_specs=in_vmem(3) + in_hbm(2), out_sp...  5.26 us
  transfers between devices with their start and end apart: 12, of which 5 were waited for; matrix products, arithmetic and copies ran while one was open for 0% of the time, Pallas kernels for 25%

profile of v2, /device:TPU:1, one launch (start us, length us, event | category | flops | bytes accessed | tf_op | source)
XLA Modules:
  0.0 106.5 jit_solution(17968311410213876116)
XLA Ops:
  0.6 3.6 %front.1 = (bf16[1024,128]{1,0:T(8,128)(2,1)}, f32[16,2048]{1,0:T(8,128)S(1)}, bf16[160,2048]{1,0:T(8,128)(2,1)}) custom-call(s32[4]{0:T(128)} %hub_hbm.2, s32[24,64]{1,0:T(8,128)} %bitcast.30, s32[1,64]{1,0:T(1,128)} %count_hbm.1, bf16[64,2048]{1,0:T(8,128)(2,1)} %bitcast.27, bf16[64,2048]{1,0:T(8,128)(2,1)} %bitcast.28, bf16[64,256]{1,0:T(8,128)(2,1)} %self_hbm.1, ...), custom_call_target="tpu_custom_call" | custom-call | flops 2147483648 | bytes 1000000 | tf_op jit(solution)/shard_map/front/pallas_call | solution.py:160
  4.2 2.1 %collective-permute-start.2 = (bf16[160,2048]{1,0:T(8,128)(2,1)}, bf16[160,2048]{1,0:T(8,128)(2,1)S(1)}, u32[]{:S(2)}, u32[]{:S(2)}) collective-permute-start(bf16[160,2048]{1,0:T(8,128)(2,1)} %get-tuple-element.46.bundle_hbm.refs_0_), channel_id=1, source_target_pairs={{0,1},{1,2},{2,3},{3,0},{4,5},{5,6},{6,7},{7,4},{8,9},{9,10},{10,1... | collective-permute-start | bytes 1966088 | tf_op jit(solution)/shard_map/ppermute | solution.py:604
  6.3 2.5 %collective-permute-start.1 = (bf16[160,2048]{1,0:T(8,128)(2,1)}, bf16[160,2048]{1,0:T(8,128)(2,1)S(1)}, u32[]{:S(2)}, u32[]{:S(2)}) collective-permute-start(bf16[160,2048]{1,0:T(8,128)(2,1)} %get-tuple-element.46.bundle_hbm.refs_0_), channel_id=1, source_target_pairs={{0,2},{1,3},{2,0},{3,1},{4,6},{5,7},{6,4},{7,5},{8,10},{9,11},{10,... | collective-permute-start | bytes 1966088 | tf_op jit(solution)/shard_map/ppermute | solution.py:604
  8.8 1.2 %collective-permute-start = (bf16[160,2048]{1,0:T(8,128)(2,1)}, bf16[160,2048]{1,0:T(8,128)(2,1)S(1)}, u32[]{:S(2)}, u32[]{:S(2)}) collective-permute-start(bf16[160,2048]{1,0:T(8,128)(2,1)} %get-tuple-element.46.bundle_hbm.refs_0_), channel_id=1, source_target_pairs={{0,3},{1,0},{2,1},{3,2},{4,7},{5,4},{6,5},{7,6},{8,11},{9,8},{10,9... | collective-permute-start | bytes 1966088 | tf_op jit(solution)/shard_map/ppermute | solution.py:604
  9.9 13.2 %all-to-all-start = ((bf16[64,16,128]{2,1,0:T(8,128)(2,1)}), bf16[64,16,128]{2,1,0:T(8,128)(2,1)S(1)}, u32[]{:S(2)}, u32[]{:S(2)}) async-start(bf16[64,16,128]{2,1,0:T(8,128)(2,1)} %bitcast.7), calls=%async_computation | async-start | bytes 524288 | tf_op jit(solution)/shard_map/all_to_all | solution.py:636
  23.8 7.2 %local_sum.1 = (f32[64,2048]{1,0:T(8,128)S(1)}, bf16[2048,2048]{1,0:T(8,128)(2,1)}) custom-call(s32[1]{0:T(128)S(6)} %copy.20.count_ref, s32[128]{0:T(128)} %src_hbm.1, s32[128]{0:T(128)} %dst_hbm.1, bf16[128,128,128]{2,1,0:T(8,128)(2,1)} %tiles_hbm.1, bf16[160,2048]{1,0:T(8,128)(2,1)} %get-tuple-element.46.bundle_hbm.refs_0_), custom_call_target="tpu_custom_call" | custom-call | flops 2147483648 | bytes 13000000 | tf_op jit(solution)/shard_map/local_sum/pallas_call | solution.py:223
  31.0 4.2 %all-to-all-done = bf16[64,16,128]{2,1,0:T(8,128)(2,1)S(1)} async-done(((bf16[64,16,128]{2,1,0:T(8,128)(2,1)}), bf16[64,16,128]{2,1,0:T(8,128)(2,1)S(1)}, u32[]{:S(2)}, u32[]{:S(2)}) %all-to-all-start) | async-done | bytes 262176 | tf_op jit(solution)/shard_map/all_to_all | solution.py:636
  35.1 5.3 %mean_rows.2 = (bf16[64,1024]{1,0:T(8,128)(2,1)S(1)}, bf16[1536,64]{1,0:T(8,128)(2,1)S(1)}, bf16[256,64]{1,0:T(8,128)(2,1)S(1)}, bf16[1024,1536]{1,0:T(8,128)(2,1)S(1)}, bf16[1024,256]{1,0:T(8,128)(2,1)S(1)}) custom-call(bf16[1024,128]{1,0:T(8,128)(2,1)S(1)} %bitcast.25, f32[64,2048]{1,0:T(8,128)S(1)} %get-tuple-element.42.local_ref, ...), custom_call_target="tpu_custom_call" | custom-call | flops 939524096 | bytes 1000000 | tf_op jit(solution)/shard_map/mean_rows/pallas_call | solution.py:307
  40.4 0.4 collective-permute-start.5
  40.8 0.6 collective-permute-start.4
  41.4 1.9 %collective-permute-start.3 = (bf16[64,1024]{1,0:T(8,128)(2,1)S(1)}, bf16[64,1024]{1,0:T(8,128)(2,1)S(1)}, u32[]{:S(2)}, u32[]{:S(2)}) collective-permute-start(bf16[64,1024]{1,0:T(8,128)(2,1)S(1)} %get-tuple-element.45.own_mean), channel_id=1, source_target_pairs={{0,3},{1,0},{2,1},{3,2},{4,7},{5,4},{6,5},{7,6},{8,11},{9,8},{10,9... | collective-permute-start | bytes 393224 | tf_op jit(solution)/shard_map/ppermute | solution.py:604
  43.3 1.2 %mean_rows.3.own_mean = bf16[64,1024]{1,0:T(8,128)(2,1)S(1)} custom-call(bf16[1536,64]{1,0:T(8,128)(2,1)S(1)} %get-tuple-element.51.rows_ref, bf16[256,64]{1,0:T(8,128)(2,1)S(1)} %get-tuple-element.52.hubs_ref, bf16[1024,1536]{1,0:T(8,128)(2,1)S(1)} %get-tuple-element.53.halo_ref, bf16[1024,256]{1,0:T(8,128)(2,1)S(1)} %get-tuple-element.54.hub_ref, ...), custom_call_target="tpu_custom_call" | custom-call | flops 939524096 | bytes 1000000 | tf_op jit(solution)/shard_map/mean_rows/pallas_call | solution.py:325
  44.5 0.5 collective-permute-start.8
  45.0 1.9 %collective-permute-start.7 = (bf16[64,1024]{1,0:T(8,128)(2,1)S(1)}, bf16[64,1024]{1,0:T(8,128)(2,1)S(1)}, u32[]{:S(2)}, u32[]{:S(2)}) collective-permute-start(bf16[64,1024]{1,0:T(8,128)(2,1)S(1)} %mean_rows.3.own_mean), channel_id=1, source_target_pairs={{0,2},{1,3},{2,0},{3,1},{4,6},{5,7},{6,4},{7,5},{8,10},{9,11},{10,... | collective-permute-start | bytes 393224 | tf_op jit(solution)/shard_map/ppermute | solution.py:604
  46.9 2.3 %collective-permute-done.5.refs_6_ = bf16[64,1024]{1,0:T(8,128)(2,1)S(1)} collective-permute-done((bf16[64,1024]{1,0:T(8,128)(2,1)S(1)}, bf16[64,1024]{1,0:T(8,128)(2,1)S(1)}, u32[]{:S(2)}, u32[]{:S(2)}) %collective-permute-start.5) | collective-permute-done | bytes 131104 | tf_op jit(solution)/shard_map/ppermute | solution.py:604
  49.3 0.0 copy-start.5
  49.3 0.2 collective-permute-done.3.refs_4_
  49.5 0.7 copy-done.7
  50.2 5.6 %dense.2 = (bf16[64,1024]{1,0:T(8,128)(2,1)S(1)}, bf16[64,1024]{1,0:T(8,128)(2,1)S(1)}, f32[64,1024]{1,0:T(8,128)S(1)}, f32[64,1536]{1,0:T(8,128)S(1)}, f32[64,2...) custom-call(s32[1]{0:T(128)} %bitcast.mine_ref, ...), custom_call_target="tpu_custom_call" | custom-call | flops 1073741824 | bytes 6000000 | tf_op jit(solution)/shard_map/dense/pallas_call | solution.py:499
  55.8 0.0 copy-start.6
  55.8 0.6 copy-done.4
  56.4 0.0 copy-done.6
  56.5 0.0 copy-done.8
  56.5 5.6 %dense.3 = (bf16[64,1024]{1,0:T(8,128)(2,1)S(1)}, bf16[64,1024]{1,0:T(8,128)(2,1)S(1)}, f32[64,1024]{1,0:T(8,128)S(1)}, bf16[1536,128]{1,0:T(8,128)(2,1)}) custom-call(s32[1]{0:T(128)} %bitcast.mine_ref, bf16[64,1024]{1,0:T(8,128)(2,1)S(1)} %mean_rows.3.own_mean, f32[16,2048]{1,0:T(8,128)S(1)} %get-tuple-element.43.index_ref, ...), custom_call_target="tpu_custom_call" | custom-call | flops 1073741824 | bytes 6000000 | tf_op jit(solution)/shard_map/dense/pallas_call | solution.py:499
  62.1 11.8 %all-to-all-start.1 = ((bf16[64,24,128]{2,1,0:T(8,128)(2,1)}), bf16[64,24,128]{2,1,0:T(8,128)(2,1)S(1)}, u32[]{:S(2)}, u32[]{:S(2)}) async-start(bf16[64,24,128]{2,1,0:T(8,128)(2,1)} %bitcast.10), calls=%async_computation.1 | async-start | bytes 786432 | tf_op jit(solution)/shard_map/all_to_all | solution.py:645
  73.9 4.3 %local_back.1 = (f32[64,2048]{1,0:T(8,128)S(1)}, bf16[64,2048]{1,0:T(8,128)(2,1)}) custom-call(f32[64,1024]{1,0:T(8,128)S(1)} %get-tuple-element.50.ginput0, f32[64,1024]{1,0:T(8,128)S(1)} %get-tuple-element.62.ginput1, bf16[64,1024]{1,0:T(8,128)(2,1)S(1)} %get-tuple-element.63.gmean0, bf16[64,1024]{1,0:T(8,128)(2,1)S(1)} %get-tuple-element.64.gmean1, ...), custom_call_target="tpu_custom_call" | custom-call | flops 2147483648 | bytes 10000000 | tf_op jit(solution)/shard_map/local_back/pallas_call | solution.py:532
  78.2 10.3 %all-to-all-done.1 = bf16[64,24,128]{2,1,0:T(8,128)(2,1)S(1)} async-done(((bf16[64,24,128]{2,1,0:T(8,128)(2,1)}), bf16[64,24,128]{2,1,0:T(8,128)(2,1)S(1)}, u32[]{:S(2)}, u32[]{:S(2)}) %all-to-all-start.1) | async-done | bytes 393248 | tf_op jit(solution)/shard_map/all_to_all | solution.py:645
  88.5 0.7 reduce_grads.1
  89.3 6.2 %all-to-all-start.2 = ((f32[64,4,128]{2,1,0:T(4,128)}), f32[64,4,128]{2,1,0:T(4,128)S(1)}, u32[]{:S(2)}, u32[]{:S(2)}) async-start(f32[64,4,128]{2,1,0:T(4,128)} %bitcast.13), calls=%async_computation.2 | async-start | bytes 262144 | tf_op jit(solution)/shard_map/all_to_all | solution.py:649
  95.5 3.4 %scatter_rows.1 = bf16[64,2048]{1,0:T(8,128)(2,1)} custom-call(bf16[1536,128]{1,0:T(8,128)(2,1)S(1)} %bitcast.24, f32[16,2048]{1,0:T(8,128)S(1)} %get-tuple-element.43.index_ref, f32[64,2048]{1,0:T(8,128)S(1)} %get-tuple-element.72.total_ref), custom_call_target="tpu_custom_call" | custom-call | flops 2147483648 | bytes 2000000 | tf_op jit(solution)/shard_map/scatter_rows/pallas_call | solution.py:591
  98.9 7.0 %all-to-all-done.2 = f32[64,4,128]{2,1,0:T(4,128)S(1)} async-done(((f32[64,4,128]{2,1,0:T(4,128)}), f32[64,4,128]{2,1,0:T(4,128)S(1)}, u32[]{:S(2)}, u32[]{:S(2)}) %all-to-all-start.2) | async-done | bytes 131104 | tf_op jit(solution)/shard_map/all_to_all | solution.py:649
  105.9 0.7 slice_bitcast_fusion
  (20 shorter events, 0.0 us)
Async XLA Ops:
  4.2 36.2 %collective-permute-start.2 = (bf16[160,2048]{1,0:T(8,128)(2,1)}, bf16[160,2048]{1,0:T(8,128)(2,1)S(1)}, u32[]{:S(2)}, u32[]{:S(2)}) collective-permute-start(bf16[160,2048]{1,0:T(8,128)(2,1)} %get-tuple-element.46.bundle_hbm.refs_0_), channel_id=1, source_target_pairs={{0,1},{1,2},{2,3},{3,0},{4,5},{5,6},{6,7},{7,4},{8,9},{9,10},{10,1... | collective-permute-start | bytes 1966088 | tf_op jit(solution)/shard_map/ppermute | solution.py:604
  6.3 34.1 %collective-permute-start.1 = (bf16[160,2048]{1,0:T(8,128)(2,1)}, bf16[160,2048]{1,0:T(8,128)(2,1)S(1)}, u32[]{:S(2)}, u32[]{:S(2)}) collective-permute-start(bf16[160,2048]{1,0:T(8,128)(2,1)} %get-tuple-element.46.bundle_hbm.refs_0_), channel_id=1, source_target_pairs={{0,2},{1,3},{2,0},{3,1},{4,6},{5,7},{6,4},{7,5},{8,10},{9,11},{10,... | collective-permute-start | bytes 1966088 | tf_op jit(solution)/shard_map/ppermute | solution.py:604
  8.8 31.6 %collective-permute-start = (bf16[160,2048]{1,0:T(8,128)(2,1)}, bf16[160,2048]{1,0:T(8,128)(2,1)S(1)}, u32[]{:S(2)}, u32[]{:S(2)}) collective-permute-start(bf16[160,2048]{1,0:T(8,128)(2,1)} %get-tuple-element.46.bundle_hbm.refs_0_), channel_id=1, source_target_pairs={{0,3},{1,0},{2,1},{3,2},{4,7},{5,4},{6,5},{7,6},{8,11},{9,8},{10,9... | collective-permute-start | bytes 1966088 | tf_op jit(solution)/shard_map/ppermute | solution.py:604
  9.9 25.2 %all-to-all-start = ((bf16[64,16,128]{2,1,0:T(8,128)(2,1)}), bf16[64,16,128]{2,1,0:T(8,128)(2,1)S(1)}, u32[]{:S(2)}, u32[]{:S(2)}) async-start(bf16[64,16,128]{2,1,0:T(8,128)(2,1)} %bitcast.7), calls=%async_computation | async-start | bytes 524288 | tf_op jit(solution)/shard_map/all_to_all | solution.py:636
  40.4 9.8 %copy-start = (bf16[160,2048]{1,0:T(8,128)(2,1)}, bf16[160,2048]{1,0:T(8,128)(2,1)S(1)}, u32[]{:S(2)}) copy-start(bf16[160,2048]{1,0:T(8,128)(2,1)S(1)} %collective-permute-done.2.refs_3_) | copy-start | bytes 1966084
  40.4 9.8 %copy-start.1 = (bf16[160,2048]{1,0:T(8,128)(2,1)}, bf16[160,2048]{1,0:T(8,128)(2,1)S(1)}, u32[]{:S(2)}) copy-start(bf16[160,2048]{1,0:T(8,128)(2,1)S(1)} %collective-permute-done.1.refs_2_) | copy-start | bytes 1966084
  40.4 9.7 %copy-start.2 = (bf16[160,2048]{1,0:T(8,128)(2,1)}, bf16[160,2048]{1,0:T(8,128)(2,1)S(1)}, u32[]{:S(2)}) copy-start(bf16[160,2048]{1,0:T(8,128)(2,1)S(1)} %collective-permute-done.refs_1_) | copy-start | bytes 1966084
  40.4 8.8 %collective-permute-start.5 = (bf16[64,1024]{1,0:T(8,128)(2,1)S(1)}, bf16[64,1024]{1,0:T(8,128)(2,1)S(1)}, u32[]{:S(2)}, u32[]{:S(2)}) collective-permute-start(bf16[64,1024]{1,0:T(8,128)(2,1)S(1)} %get-tuple-element.45.own_mean), channel_id=1, source_target_pairs={{0,1},{1,2},{2,3},{3,0},{4,5},{5,6},{6,7},{7,4},{8,9},{9,10},{10,1... | collective-permute-start | bytes 393224 | tf_op jit(solution)/shard_map/ppermute | solution.py:604
  40.8 8.5 %collective-permute-start.4 = (bf16[64,1024]{1,0:T(8,128)(2,1)S(1)}, bf16[64,1024]{1,0:T(8,128)(2,1)S(1)}, u32[]{:S(2)}, u32[]{:S(2)}) collective-permute-start(bf16[64,1024]{1,0:T(8,128)(2,1)S(1)} %get-tuple-element.45.own_mean), channel_id=1, source_target_pairs={{0,2},{1,3},{2,0},{3,1},{4,6},{5,7},{6,4},{7,5},{8,10},{9,11},{10,... | collective-permute-start | bytes 393224 | tf_op jit(solution)/shard_map/ppermute | solution.py:604
  41.4 8.1 %collective-permute-start.3 = (bf16[64,1024]{1,0:T(8,128)(2,1)S(1)}, bf16[64,1024]{1,0:T(8,128)(2,1)S(1)}, u32[]{:S(2)}, u32[]{:S(2)}) collective-permute-start(bf16[64,1024]{1,0:T(8,128)(2,1)S(1)} %get-tuple-element.45.own_mean), channel_id=1, source_target_pairs={{0,3},{1,0},{2,1},{3,2},{4,7},{5,4},{6,5},{7,6},{8,11},{9,8},{10,9... | collective-permute-start | bytes 393224 | tf_op jit(solution)/shard_map/ppermute | solution.py:604
  44.5 11.3 %collective-permute-start.8 = (bf16[64,1024]{1,0:T(8,128)(2,1)S(1)}, bf16[64,1024]{1,0:T(8,128)(2,1)S(1)}, u32[]{:S(2)}, u32[]{:S(2)}) collective-permute-start(bf16[64,1024]{1,0:T(8,128)(2,1)S(1)} %mean_rows.3.own_mean), channel_id=1, source_target_pairs={{0,1},{1,2},{2,3},{3,0},{4,5},{5,6},{6,7},{7,4},{8,9},{9,10},{10,1... | collective-permute-start | bytes 393224 | tf_op jit(solution)/shard_map/ppermute | solution.py:604
  45.0 10.7 %collective-permute-start.7 = (bf16[64,1024]{1,0:T(8,128)(2,1)S(1)}, bf16[64,1024]{1,0:T(8,128)(2,1)S(1)}, u32[]{:S(2)}, u32[]{:S(2)}) collective-permute-start(bf16[64,1024]{1,0:T(8,128)(2,1)S(1)} %mean_rows.3.own_mean), channel_id=1, source_target_pairs={{0,2},{1,3},{2,0},{3,1},{4,6},{5,7},{6,4},{7,5},{8,10},{9,11},{10,... | collective-permute-start | bytes 393224 | tf_op jit(solution)/shard_map/ppermute | solution.py:604
  49.3 0.9 copy-start.3
  49.3 6.5 %collective-permute-start.6 = (bf16[64,1024]{1,0:T(8,128)(2,1)S(1)}, bf16[64,1024]{1,0:T(8,128)(2,1)S(1)}, u32[]{:S(2)}, u32[]{:S(2)}) collective-permute-start(bf16[64,1024]{1,0:T(8,128)(2,1)S(1)} %mean_rows.3.own_mean), channel_id=1, source_target_pairs={{0,3},{1,0},{2,1},{3,2},{4,7},{5,4},{6,5},{7,6},{8,11},{9,8},{10,9... | collective-permute-start | bytes 393224 | tf_op jit(solution)/shard_map/ppermute | solution.py:604
  49.3 0.9 copy-start.5
  49.5 0.7 copy-start.7
  55.8 0.7 copy-start.4
  55.8 0.7 copy-start.6
  55.8 0.7 copy-start.8
  62.1 26.4 %all-to-all-start.1 = ((bf16[64,24,128]{2,1,0:T(8,128)(2,1)}), bf16[64,24,128]{2,1,0:T(8,128)(2,1)S(1)}, u32[]{:S(2)}, u32[]{:S(2)}) async-start(bf16[64,24,128]{2,1,0:T(8,128)(2,1)} %bitcast.10), calls=%async_computation.1 | async-start | bytes 786432 | tf_op jit(solution)/shard_map/all_to_all | solution.py:645
  89.3 16.6 %all-to-all-start.2 = ((f32[64,4,128]{2,1,0:T(4,128)}), f32[64,4,128]{2,1,0:T(4,128)S(1)}, u32[]{:S(2)}, u32[]{:S(2)}) async-start(f32[64,4,128]{2,1,0:T(4,128)} %bitcast.13), calls=%async_computation.2 | async-start | bytes 262144 | tf_op jit(solution)/shard_map/all_to_all | solution.py:649

commit v3 on v2

--- a/solution.py
+++ b/solution.py
@@ -23,11 +23,13 @@
 TILES = 128
 HALO = PEERS * SLOT
 HUB_ALL = PEERS * HUBS
-BUNDLE = 160
+BUNDLE = 144
+WIDTH = 2048 + 128
 PACK = 2 * FIN
 HALF = NODES // 2
 SLOTS = PEERS * ROWS
 CHUNK = 256
+NEAR = HALF // 2
 
 def matmul(left, right):
     return lax.dot_general(
@@ -101,35 +103,27 @@
     return jnp.concatenate([left, right], axis=1)
 
 
-def front_kernel(
-    hub_hbm, send_hbm, count_hbm, feat_hbm, gout_hbm, self_hbm, neigh_hbm, bias_hbm, degree_hbm,
-    wire_ref, index_ref, bundle_hbm,
-    hub_ref, send_ref, count_ref, self_ref, neigh_ref, bias_ref, degree_ref, bundle_ref, sems,
-    out_sem,
+def bundle_kernel(
+    feat_hbm, gout_hbm, self_hbm, neigh_hbm, bias_hbm, bundle_ref,
+    self_ref, neigh_ref, bias_ref, sems,
 ):
-    pairs = [
-        (hub_hbm, hub_ref),
-        (send_hbm, send_ref),
-        (count_hbm, count_ref),
-        (feat_hbm, bundle_ref.at[pl.ds(0, FIN)]),
-        (self_hbm, self_ref),
-        (neigh_hbm, neigh_ref),
-        (bias_hbm, bias_ref),
-        (degree_hbm, degree_ref),
-        (gout_hbm, bundle_ref.at[pl.ds(FIN, FIN)]),
-    ]
-    copies = start_all(pairs, sems)
+    copies = start_all(
+        [
+            (self_hbm, self_ref),
+            (neigh_hbm, neigh_ref),
+            (bias_hbm, bias_ref),
+            (feat_hbm, bundle_ref.at[pl.ds(0, FIN), pl.ds(0, NODES)]),
+            (gout_hbm, bundle_ref.at[pl.ds(FIN, FIN), pl.ds(0, NODES)]),
+        ],
+        sems,
+    )
+    bundle_ref[:, NODES:] = jnp.zeros((BUNDLE, LANES), BF)
     for copy in copies[:3]:
         copy.wait()
-    both = slot_targets(hub_ref, send_ref, count_ref)
-    index_ref[:8] = jnp.broadcast_to(both, (8, 2 * SLOTS))
-    for copy in copies[4:8]:
-        copy.wait()
-    index_ref[8:] = jnp.broadcast_to(degree_ref[...].astype(F32), (8, NODES))
     for i in range(4):
         rows = slice(16 * i, 16 * i + 16)
-        bundle_ref[PACK:PACK + 16, FOUT * i:FOUT * (i + 1)] = self_ref[rows]
-        bundle_ref[PACK:PACK + 16, FOUT * (i + 4):FOUT * (i + 5)] = neigh_ref[rows]
+        bundle_ref[PACK:, FOUT * i:FOUT * (i + 1)] = self_ref[rows]
+        bundle_ref[PACK:, FOUT * (i + 4):FOUT * (i + 5)] = neigh_ref[rows]
     bias = bias_ref[...]
     high = bias.astype(BF).astype(F32)
     middle = (bias - high).astype(BF).astype(F32)
@@ -139,57 +133,89 @@
         place == 0, high, jnp.where(place == 1, middle, jnp.where(place == 2, low, 0.0))
     )
     parts = jnp.concatenate([parts, jnp.zeros((16, LANES - FIN), F32)], axis=1).astype(BF)
-    bundle_ref[PACK + 16:] = jnp.zeros((16, NODES), BF)
-    bundle_ref[PACK + 16:, :LANES] = parts
-    copies[3].wait()
-    copies[8].wait()
-    (outgoing,) = start_all([(bundle_ref, bundle_hbm)], out_sem)
-    target = both.astype(I32)
+    bundle_ref[PACK:, NODES:] = parts
+    for copy in copies[3:]:
+        copy.wait()
+
+
+def bundle(*operands):
+    return pl.pallas_call(
+        bundle_kernel,
+        in_specs=in_hbm(5),
+        out_specs=in_vmem(1)[0],
+        out_shape=pltpu.VMEM((BUNDLE, WIDTH), BF),
+        scratch_shapes=[
+            pltpu.VMEM((FIN, FOUT), BF),
+            pltpu.VMEM((FIN, FOUT), BF),
+            pltpu.VMEM((1, FIN), F32),
+            pltpu.SemaphoreType.DMA((5,)),
+        ],
+        compiler_params=params(),
+        cost_estimate=cost(1000000, 2000000),
+        name="bundle",
+    )(*keep_hbm(*operands))
+
+
+def gather_kernel(
+    hub_hbm, send_hbm, count_hbm, feat_hbm, degree_hbm, wire_ref, index_ref,
+    hub_ref, send_ref, count_ref, feat_ref, degree_ref, sems,
+):
+    copies = start_all(
+        [
+            (hub_hbm, hub_ref),
+            (send_hbm, send_ref),
+            (count_hbm, count_ref),
+            (degree_hbm, degree_ref),
+            (feat_hbm, feat_ref),
+        ],
+        sems,
+    )
+    for copy in copies[:4]:
+        copy.wait()
+    both = slot_targets(hub_ref, send_ref, count_ref)
+    index_ref[:8] = jnp.broadcast_to(both, (8, 2 * SLOTS))
+    index_ref[8:] = jnp.broadcast_to(degree_ref[...].astype(F32), (8, NODES))
+    copies[4].wait()
     step = 256
     total = jnp.zeros((FIN, 2 * SLOTS), F32)
-    node = iota((step, 2 * SLOTS), 0)
+    node = iota((step, 2 * SLOTS), 0).astype(F32).astype(BF)
     for k in range(NODES // step):
-        hot = (node == target - k * step).astype(F32).astype(BF)
-        total += matmul(bundle_ref[:FIN, k * step:(k + 1) * step], hot)
+        target = (both - float(k * step)).astype(BF)
+        hot = jnp.where(node == target, jnp.ones((), BF), jnp.zeros((), BF))
+        total += matmul(feat_ref[:, k * step:(k + 1) * step], hot)
     stacked = jnp.concatenate([total[:, :SLOTS], total[:, SLOTS:]], axis=0)
     wire_ref[...] = stacked.T.astype(BF)
-    outgoing.wait()
-
-
-def front(*operands):
-    return pl.pallas_call(
-        front_kernel,
-        in_specs=in_hbm(9),
-        out_specs=in_vmem(2) + in_hbm(1),
+
+
+def gather_rows(*operands):
+    return pl.pallas_call(
+        gather_kernel,
+        in_specs=in_hbm(5),
+        out_specs=in_vmem(2),
         out_shape=[
             jax.ShapeDtypeStruct((SLOTS, LANES), BF),
             pltpu.VMEM((16, NODES), F32),
-            pltpu.HBM((BUNDLE, NODES), BF),
         ],
         scratch_shapes=[
             pltpu.SMEM((HUBS,), I32),
             pltpu.VMEM((SLOT, PEERS), I32),
             pltpu.VMEM((1, PEERS), I32),
-            pltpu.VMEM((FIN, FOUT), BF),
-            pltpu.VMEM((FIN, FOUT), BF),
-            pltpu.VMEM((1, FIN), F32),
+            pltpu.VMEM((FIN, NODES), BF),
             pltpu.VMEM((1, NODES), I32),
-            pltpu.VMEM((BUNDLE, NODES), BF),
-            pltpu.SemaphoreType.DMA((9,)),
-            pltpu.SemaphoreType.DMA((1,)),
+            pltpu.SemaphoreType.DMA((5,)),
         ],
         compiler_params=params(),
         cost_estimate=cost(2 * 2 * SLOTS * NODES * 256, 1000000),
-        name="front",
+        name="gather_rows",
     )(*keep_hbm(*operands))
 
 
 def local_kernel(
-    count_ref, src_hbm, dst_hbm, tiles_hbm, bundle_hbm, sum_ref, adj_hbm,
+    count_ref, src_hbm, dst_hbm, tiles_hbm, feat_hbm, sum_ref, adj_hbm,
     src_ref, dst_ref, feat_ref, tiles_ref, adj_ref, sems, tile_sems, out_sems,
 ):
     small = start_all(
-        [(src_hbm, src_ref), (dst_hbm, dst_ref), (bundle_hbm.at[pl.ds(0, FIN)], feat_ref)], sems
+        [(src_hbm, src_ref), (dst_hbm, dst_ref), (feat_hbm, feat_ref)], sems
     )
     groups = tile_sems.shape[0]
     group = TILES // groups
@@ -219,7 +245,7 @@
         copy.wait()
 
 
-def local_sum(src, dst, count, tiles, packed):
+def local_sum(src, dst, count, tiles, feat):
     return pl.pallas_call(
         local_kernel,
         in_specs=[pl.BlockSpec(memory_space=pltpu.SMEM)] + in_hbm(4),
@@ -241,37 +267,52 @@
         compiler_params=params(),
         cost_estimate=cost(2 * NODES * NODES * 256, 13000000),
         name="local_sum",
-    )(count, *keep_hbm(src, dst, tiles, packed))
-
-
-def adjacency_copies(part, pieces, halo_hbm, hub_hbm, halo_ref, hub_ref, sems):
-    piece = HALF // pieces
+    )(count, *keep_hbm(src, dst, tiles, feat))
+
+
+def adjacency_copies(start, rows, pieces, halo_hbm, hub_hbm, halo_ref, hub_ref, sems):
+    piece = rows // pieces
     pairs = []
     for i in range(pieces):
-        there = pl.ds(part * HALF + i * piece, piece)
+        there = pl.ds(start + i * piece, piece)
         pairs.append((halo_hbm.at[there], halo_ref.at[pl.ds(i * piece, piece)]))
-    pairs.append((hub_hbm.at[pl.ds(part * HALF, HALF)], hub_ref))
+    pairs.append((hub_hbm.at[pl.ds(start, rows)], hub_ref))
     return start_all(pairs, sems)
 
 
-def mean_half(part, rows, hubs, halo_ref, hub_ref, local_ref, index_ref, mean_ref, ready):
-    chunk = 512
-    for i in range(HALF // chunk):
-        ready(i)
-        here = slice(i * chunk, (i + 1) * chunk)
-        whole = slice(part * HALF + i * chunk, part * HALF + (i + 1) * chunk)
-        total = matmul(halo_ref[here], rows) + matmul(hub_ref[here], hubs)
-        total = total.T + local_ref[:, whole]
-        mean_ref[:, here] = (total / index_ref[8:9, whole]).astype(BF)
+def mean_part(start, column, rows, hubs, halo, hub, local_ref, index_ref, mean_ref):
+    count = halo.shape[0]
+    total = matmul(halo, rows) + matmul(hub, hubs)
+    there = slice(start, start + count)
+    total = total.T + local_ref[:, there]
+    mean_ref[:, column:column + count] = (total / index_ref[8:9, there]).astype(BF)
+
+
+def half_copies(part, halo_hbm, hub_hbm, halo_ref, hub_ref, sems):
+    return [
+        adjacency_copies(
+            part * HALF + i * NEAR, NEAR, 1,
+            halo_hbm, hub_hbm, halo_ref.at[i], hub_ref.at[i], sems.at[i],
+        )
+        for i in range(2)
+    ]
+
+
+def mean_half(part, copies, rows, hubs, halo_ref, hub_ref, local_ref, index_ref, mean_ref):
+    for i in range(2):
+        for copy in copies[i]:
+            copy.wait()
+        mean_part(
+            part * HALF + i * NEAR, i * NEAR, rows, hubs, halo_ref[i], hub_ref[i],
+            local_ref, index_ref, mean_ref,
+        )
 
 
 def first_mean_kernel(
-    wire_ref, local_ref, index_ref, halo_hbm, hub_hbm,
-    mean_ref, rows_ref, hubs_ref, later_halo, later_hub,
-    halo_ref, hub_ref, sems, later_sems,
+    wire_ref, local_ref, index_ref, halo_hbm, hub_hbm, mean_ref, rows_ref, hubs_ref,
+    halo_ref, hub_ref, sems,
 ):
-    copies = adjacency_copies(0, 2, halo_hbm, hub_hbm, halo_ref, hub_ref, sems)
-    later = []
+    copies = half_copies(0, halo_hbm, hub_hbm, halo_ref, hub_ref, sems)
     wire = wire_ref[...].astype(F32).reshape(PEERS, ROWS, LANES)
     left = wire[:, :, :FIN]
     right = wire[:, :, FIN:]
@@ -279,72 +320,94 @@
     rows_ref[...] = rows.reshape(HALO, FIN).astype(BF)
     owned = right[:, 8:].reshape(PEERS * 8, FIN).astype(BF)
     hubs_ref[...] = matmul(pick_hubs(), owned).astype(BF)
-    copies[-1].wait()
-
-    def ready(i):
-        copies[i].wait()
-        if i:
-            later.extend(
-                adjacency_copies(1, 2, halo_hbm, hub_hbm, later_halo, later_hub, later_sems)
-            )
-
     mean_half(
-        0, rows_ref[...], hubs_ref[...], halo_ref, hub_ref, local_ref, index_ref, mean_ref, ready
-    )
-    for copy in later:
-        copy.wait()
-
-
-def later_mean_kernel(rows_ref, hubs_ref, halo_ref, hub_ref, local_ref, index_ref, mean_ref):
-    mean_half(
-        1, rows_ref[...], hubs_ref[...], halo_ref, hub_ref, local_ref, index_ref, mean_ref,
-        lambda i: None,
-    )
+        0, copies, rows_ref[...], hubs_ref[...], halo_ref, hub_ref, local_ref, index_ref, mean_ref
+    )
+
+
+HALF_SCRATCH = [
+    pltpu.VMEM((2, NEAR, HALO), BF),
+    pltpu.VMEM((2, NEAR, HUB_ALL), BF),
+    pltpu.SemaphoreType.DMA((2, 2)),
+]
 
 
 def first_mean(wire, halo_adj, hub_adj, local, index):
-    shapes = [(FIN, HALF), (HALO, FIN), (HUB_ALL, FIN), (HALF, HALO), (HALF, HUB_ALL)]
+    shapes = [(FIN, HALF), (HALO, FIN), (HUB_ALL, FIN)]
     return pl.pallas_call(
         first_mean_kernel,
         in_specs=in_vmem(3) + in_hbm(2),
         out_specs=in_vmem(len(shapes)),
         out_shape=[pltpu.VMEM(shape, BF) for shape in shapes],
-        scratch_shapes=[
-            pltpu.VMEM((HALF, HALO), BF),
-            pltpu.VMEM((HALF, HUB_ALL), BF),
-            pltpu.SemaphoreType.DMA((3,)),
-            pltpu.SemaphoreType.DMA((3,)),
-        ],
+        scratch_shapes=HALF_SCRATCH,
         compiler_params=params(),
         cost_estimate=cost(HALF * (HALO + HUB_ALL) * 512, 1000000),
         name="mean_rows",
     )(wire, local, index, *keep_hbm(halo_adj, hub_adj))
 
 
-def later_mean(known, local, index):
+def later_mean_kernel(mine_ref, rows_ref, hubs_ref, local_ref, index_ref, *refs):
+    halo_hbm, hub_hbm, bundles = refs[0], refs[1], refs[2:6]
+    mean_ref, weight_ref, bias_ref, back_ref, value_ref = refs[6:11]
+    halo_ref, hub_ref, sems, pack_ref, pack_sems, value_sems = refs[11:]
+    copies = half_copies(1, halo_hbm, hub_hbm, halo_ref, hub_ref, sems)
+    packs = start_all(
+        [(bundles[k].at[pl.ds(PACK, 16)], pack_ref.at[k]) for k in range(FEATS)], pack_sems
+    )
+    values = value_copies(0, bundles, value_ref, value_sems)
+    mean_half(
+        1, copies, rows_ref[...], hubs_ref[...], halo_ref, hub_ref, local_ref, index_ref, mean_ref
+    )
+    for copy in packs:
+        copy.wait()
+    prepare_weights(mine_ref[0], pack_ref, weight_ref, bias_ref, back_ref)
+    for copy in values:
+        copy.wait()
+
+
+def later_mean(mine, known, local, index, halo_adj, hub_adj, bundles):
     return pl.pallas_call(
         later_mean_kernel,
-        in_specs=in_vmem(6),
-        out_specs=in_vmem(1)[0],
-        out_shape=pltpu.VMEM((FIN, HALF), BF),
+        in_specs=[pl.BlockSpec(memory_space=pltpu.SMEM)]
+        + in_vmem(4)
+        + in_hbm(2)
+        + [pl.BlockSpec(memory_space=pl.ANY)]
+        + in_hbm(FEATS - 1),
+        out_specs=in_vmem(5),
+        out_shape=[
+            pltpu.VMEM((FIN, HALF), BF),
+            pltpu.VMEM((FEATS, FOUT, PACK), BF),
+            pltpu.VMEM((FOUT, LANES), F32),
+            pltpu.VMEM((PACK, FOUT), BF),
+            pltpu.VMEM((FEATS, PACK, HALF), BF),
+        ],
+        scratch_shapes=HALF_SCRATCH
+        + [
+            pltpu.VMEM((FEATS, 16, WIDTH), BF),
+            pltpu.SemaphoreType.DMA((FEATS,)),
+            pltpu.SemaphoreType.DMA((FEATS,)),
+        ],
         compiler_params=params(),
         cost_estimate=cost(HALF * (HALO + HUB_ALL) * 512, 1000000),
         name="mean_rows",
-    )(*known, local, index)
+    )(
+        mine, *known, local, index, *keep_hbm(halo_adj, hub_adj),
+        bundles[0], *keep_hbm(*bundles[1:]),
+    )
 
 
 def prepare_weights(mine, packs, weight_ref, bias_ref, back_ref):
     eye = iota((FIN, FIN), 0) == iota((FIN, FIN), 1)
     for k in range(FEATS):
         pieces = [
-            packs[k, :16, FOUT * i:FOUT * (i + 1)].astype(F32) for i in range(8)
+            packs[k, :, FOUT * i:FOUT * (i + 1)].astype(F32) for i in range(8)
         ]
         turned = jnp.concatenate(pieces, axis=0).T.astype(BF)
         for b in range(FEATS):
             place = lax.rem(b - mine + FEATS, FEATS)
             rows = pl.ds(pl.multiple_of(place * FIN, FIN), FIN)
             weight_ref[k, rows, :] = turned[b * FIN:(b + 1) * FIN]
-        parts = packs[k, 16:, :LANES].astype(F32)
+        parts = packs[k, :, NODES:].astype(F32)
         row = parts[0:1, :FIN] + parts[1:2, :FIN] + parts[2:3, :FIN]
         column = jnp.sum(jnp.where(eye, row, 0.0), axis=1, keepdims=True)
         bias_ref[k * FIN:(k + 1) * FIN, :] = jnp.broadcast_to(column, (FIN, LANES))
@@ -382,12 +445,8 @@
     )
 
 
-def mean_copies(means, mean_ref, sems):
-    return start_all([(means[k], mean_ref.at[k]) for k in range(FEATS - 1)], sems)
-
-
 def dense_half(
-    part, own_mean, mean_ref, value_ref, weight_ref, bias_ref, back_ref, index_ref, copies,
+    part, means, value_ref, weight_ref, bias_ref, back_ref, index_ref, copies,
     halo_ref, hub_ref, out_ref, gmean_ref, ginput_ref, gpre_ref,
 ):
     chunk = CHUNK
@@ -396,10 +455,9 @@
         whole = slice(part * HALF + i * chunk, part * HALF + (i + 1) * chunk)
         pre = jnp.tile(bias_ref[...], (1, chunk // LANES))
         for k in range(FEATS):
-            mean = mean_ref[k - 1, :, here] if k else own_mean[:, here]
-            both = jnp.concatenate([value_ref[k, :FIN, here], mean], axis=0)
+            both = jnp.concatenate([value_ref[k, :FIN, here], means[k][:, here]], axis=0)
             pre = pre + matmul(weight_ref[k], both).astype(BF).astype(F32)
-        sigma = 1.0 / (1.0 + jnp.exp(-pre))
+        sigma = 0.5 * jnp.tanh(0.5 * pre) + 0.5
         out_ref[:, here] = (pre[:FIN] * sigma[:FIN]).astype(BF)
         slope = sigma * (1.0 + pre * (1.0 - sigma))
         gout = jnp.concatenate([value_ref[k, FIN:, here] for k in range(FEATS)], axis=0)
@@ -408,7 +466,7 @@
         back = matmul(back_ref[...], gpre)
         ginput_ref[:, here] = back[:FIN]
         gmean_ref[:, here] = (back[FIN:] / index_ref[8:9, whole]).astype(BF)
-    left = jnp.concatenate([value_ref[0, :FIN], own_mean[...], jnp.ones((16, HALF), BF)], axis=0)
+    left = jnp.concatenate([value_ref[0, :FIN], means[0][...], jnp.ones((16, HALF), BF)], axis=0)
     grads = matmul_nt(left, gpre_ref[...])
     for copy in copies:
         copy.wait()
@@ -417,44 +475,31 @@
     return halos, hubs, grads
 
 
-def first_dense_kernel(mine_ref, own_mean, index_ref, *refs):
-    bundles, means, halo_hbm, hub_hbm = refs[:4], refs[4:7], refs[7], refs[8]
-    out_ref, gmean_ref, ginput_ref, halo_acc, hub_acc, grad_acc = refs[9:15]
-    weight_ref, bias_ref, back_ref, later_ref = refs[15:19]
-    gpre_ref, halo_ref, hub_ref, pack_ref, value_ref, mean_ref = refs[19:25]
-    pack_sems, value_sems, mean_sems, sems, later_sems = refs[25:]
-    packs = start_all(
-        [(bundles[k].at[pl.ds(PACK, 32)], pack_ref.at[k]) for k in range(FEATS)], pack_sems
-    )
-    ready = value_copies(0, bundles, value_ref, value_sems)
-    ready = ready + mean_copies(means, mean_ref, mean_sems)
-    copies = adjacency_copies(0, 4, halo_hbm, hub_hbm, halo_ref, hub_ref, sems)
+def first_dense_kernel(*refs):
+    means, index_ref = refs[:4], refs[4]
+    weight_ref, bias_ref, back_ref, value_ref = refs[5:9]
+    bundles, halo_hbm, hub_hbm = refs[9:13], refs[13], refs[14]
+    out_ref, gmean_ref, ginput_ref, halo_acc, hub_acc, grad_acc, later_ref = refs[15:22]
+    gpre_ref, halo_ref, hub_ref, sems, later_sems = refs[22:]
+    copies = adjacency_copies(0, HALF, 4, halo_hbm, hub_hbm, halo_ref, hub_ref, sems)
     later = value_copies(1, bundles, later_ref, later_sems)
-    for copy in packs:
-        copy.wait()
-    prepare_weights(mine_ref[0], pack_ref, weight_ref, bias_ref, back_ref)
-    for copy in ready:
-        copy.wait()
     halo_acc[...], hub_acc[...], grad_acc[...] = dense_half(
-        0, own_mean, mean_ref, value_ref, weight_ref, bias_ref, back_ref, index_ref, copies,
+        0, means, value_ref, weight_ref, bias_ref, back_ref, index_ref, copies,
         halo_ref, hub_ref, out_ref, gmean_ref, ginput_ref, gpre_ref,
     )
     for copy in later:
         copy.wait()
 
 
-def later_dense_kernel(mine_ref, own_mean, index_ref, *refs):
-    held_halo, held_hub, held_grad, weight_ref, bias_ref, back_ref, value_ref = refs[:7]
-    means, halo_hbm, hub_hbm = refs[7:10], refs[10], refs[11]
-    out_ref, gmean_ref, ginput_ref, wire_ref = refs[12:16]
-    gpre_ref, halo_ref, hub_ref, halo_acc, hub_acc, grad_acc, mean_ref = refs[16:23]
-    mean_sems, sems = refs[23:]
-    ready = mean_copies(means, mean_ref, mean_sems)
-    copies = adjacency_copies(1, 4, halo_hbm, hub_hbm, halo_ref, hub_ref, sems)
-    for copy in ready:
-        copy.wait()
+def later_dense_kernel(mine_ref, *refs):
+    means, index_ref = refs[:4], refs[4]
+    weight_ref, bias_ref, back_ref, value_ref = refs[5:9]
+    held_halo, held_hub, held_grad, halo_hbm, hub_hbm = refs[9:14]
+    out_ref, gmean_ref, ginput_ref, wire_ref = refs[14:18]
+    gpre_ref, halo_ref, hub_ref, halo_acc, hub_acc, grad_acc, sems = refs[18:]
+    copies = adjacency_copies(HALF, HALF, 4, halo_hbm, hub_hbm, halo_ref, hub_ref, sems)
     halos, hubs, grads = dense_half(
-        1, own_mean, mean_ref, value_ref, weight_ref, bias_ref, back_ref, index_ref, copies,
+        1, means, value_ref, weight_ref, bias_ref, back_ref, index_ref, copies,
         halo_ref, hub_ref, out_ref, gmean_ref, ginput_ref, gpre_ref,
     )
     halo_acc[...] = held_halo[...] + halos
@@ -464,50 +509,48 @@
 
 
 ACCUMULATORS = [(FIN, HALO), (FIN, HUB_ALL), (PACK + 16, FOUT)]
-
-
-def dense(part, mine, bundles, means, index, halo_adj, hub_adj, held):
-    out_shape = [
-        jax.ShapeDtypeStruct((FIN, HALF), BF),
-        jax.ShapeDtypeStruct((FIN, HALF), BF),
-        jax.ShapeDtypeStruct((FIN, HALF), F32),
-    ]
-    scratch = [
-        pltpu.VMEM((FOUT, HALF), BF),
-        pltpu.VMEM((HALF, HALO), BF),
-        pltpu.VMEM((HALF, HUB_ALL), BF),
-    ]
-    remote = pltpu.VMEM((FEATS - 1, FIN, HALF), BF)
-    value = pltpu.VMEM((FEATS, PACK, HALF), BF)
-    if part == 0:
-        out_shape += [pltpu.VMEM(shape, F32) for shape in ACCUMULATORS]
-        out_shape += [
-            pltpu.VMEM((FEATS, FOUT, PACK), BF),
-            pltpu.VMEM((FOUT, LANES), F32),
-            pltpu.VMEM((PACK, FOUT), BF),
-            value,
-        ]
-        scratch += [pltpu.VMEM((FEATS, 32, NODES), BF), value, remote]
-        counts = [4, 4, 3, 5, 4]
-        far = keep_hbm(*bundles, *means[1:], halo_adj, hub_adj)
-    else:
-        out_shape += [jax.ShapeDtypeStruct((PEERS * WIDE, LANES), BF)]
-        scratch += [pltpu.VMEM(shape, F32) for shape in ACCUMULATORS] + [remote]
-        counts = [3, 5]
-        far = keep_hbm(*means[1:], halo_adj, hub_adj)
-    scratch += [pltpu.SemaphoreType.DMA((count,)) for count in counts]
-    return pl.pallas_call(
-        later_dense_kernel if part else first_dense_kernel,
-        in_specs=[pl.BlockSpec(memory_space=pltpu.SMEM)]
-        + in_vmem(2 + len(held))
-        + in_hbm(len(far)),
+HALVES = [
+    jax.ShapeDtypeStruct((FIN, HALF), BF),
+    jax.ShapeDtypeStruct((FIN, HALF), BF),
+    jax.ShapeDtypeStruct((FIN, HALF), F32),
+]
+ADJACENCY = [
+    pltpu.VMEM((FOUT, HALF), BF),
+    pltpu.VMEM((HALF, HALO), BF),
+    pltpu.VMEM((HALF, HUB_ALL), BF),
+]
+
+
+def first_dense(means, index, weights, value, bundles, halo_adj, hub_adj):
+    out_shape = HALVES + [pltpu.VMEM(shape, F32) for shape in ACCUMULATORS]
+    out_shape += [pltpu.VMEM((FEATS, PACK, HALF), BF)]
+    return pl.pallas_call(
+        first_dense_kernel,
+        in_specs=in_vmem(9) + [pl.BlockSpec(memory_space=pl.ANY)] + in_hbm(FEATS + 1),
         out_specs=in_vmem(len(out_shape)),
         out_shape=out_shape,
-        scratch_shapes=scratch,
+        scratch_shapes=ADJACENCY
+        + [pltpu.SemaphoreType.DMA((5,)), pltpu.SemaphoreType.DMA((FEATS,))],
         compiler_params=params(),
         cost_estimate=cost(NODES * 2048 * 256, 6000000),
         name="dense",
-    )(mine, means[0], index, *held, *far)
+    )(*means, index, *weights, value, bundles[0], *keep_hbm(*bundles[1:], halo_adj, hub_adj))
+
+
+def later_dense(mine, means, index, weights, value, held, halo_adj, hub_adj):
+    out_shape = HALVES + [jax.ShapeDtypeStruct((PEERS * WIDE, LANES), BF)]
+    return pl.pallas_call(
+        later_dense_kernel,
+        in_specs=[pl.BlockSpec(memory_space=pltpu.SMEM)] + in_vmem(12) + in_hbm(2),
+        out_specs=in_vmem(len(out_shape)),
+        out_shape=out_shape,
+        scratch_shapes=ADJACENCY
+        + [pltpu.VMEM(shape, F32) for shape in ACCUMULATORS]
+        + [pltpu.SemaphoreType.DMA((5,))],
+        compiler_params=params(),
+        cost_estimate=cost(NODES * 2048 * 256, 6000000),
+        name="dense",
+    )(mine, *means, index, *weights, value, *held, *keep_hbm(halo_adj, hub_adj))
 
 
 def back_kernel(
@@ -629,19 +672,25 @@
     mine = lax.axis_index("feat").astype(I32).reshape(1)
     degree = degree.reshape(1, NODES)
     send = jnp.transpose(send_rows[0])
-    wire, index, packed = front(
-        hub_local, send, send_count, feat, gout, w_self, w_neigh, bias.reshape(1, FIN), degree
-    )
+    packed = bundle(feat, gout, w_self, w_neigh, bias.reshape(1, FIN))
+    packed, feat = lax.optimization_barrier((packed, feat))
     bundles = from_feat(packed)
+    wire, index = gather_rows(hub_local, send, send_count, feat, degree)
     arrived = lax.all_to_all(wire, "dom", split_axis=0, concat_axis=0, tiled=True)
-    local, adj = local_sum(tile_src, tile_dst, tile_count, tiles, packed)
+    local, adj = local_sum(tile_src, tile_dst, tile_count, tiles, feat)
     mean, *known = first_mean(arrived, halo_adj, hub_adj, local, index)
     mean, bundles = lax.optimization_barrier((mean, bundles))
     first = from_feat(mean)
-    mean = later_mean(known, local, index)
+    mean, *weights, value = later_mean(
+        mine, known, local, index, halo_adj, hub_adj, bundles
+    )
     second = from_feat(mean)
-    out0, gmean0, ginput0, *held = dense(0, mine, bundles, first, index, halo_adj, hub_adj, [])
-    out1, gmean1, ginput1, wire = dense(1, mine, bundles, second, index, halo_adj, hub_adj, held)
+    out0, gmean0, ginput0, *held, value = first_dense(
+        first, index, weights, value, bundles, halo_adj, hub_adj
+    )
+    out1, gmean1, ginput1, wire = later_dense(
+        mine, second, index, weights, value, held, halo_adj, hub_adj
+    )
     returned = lax.all_to_all(wire, "dom", split_axis=0, concat_axis=0, tiled=True)
     total, out = local_back([ginput0, ginput1], [gmean0, gmean1], [out0, out1], adj)
     returned, total = lax.optimization_barrier((returned, total))

time: 107 us -> 103 us (0.963)
  waiting for transfers between devices: 24 us -> 22 us
  local copies, waits for them, and re-layouts: 2.03 us -> 0.67 us
    all_to_all x2, starting transfers between devices: 25 us -> 22.3 us  [on_device(): lax.all_to_all(wire, 'dom', split_axis=0, concat_axis=0, tiled=True)]
    ppermute x9, starting transfers between devices: 11 us -> 13 us  [from_feat(): lax.ppermute(value, 'feat', [(j, (j - k) % FEATS) for j in range(FEATS)])]
    ppermute x9, waiting for transfers between devices: 2.56 us -> 1.1 us  [from_feat(): lax.ppermute(value, 'feat', [(j, (j - k) % FEATS) for j in range(FEATS)])]
    unnamed x18 -> x4, local copies, waits for them, and re-layouts: 1.37 us -> 0.01 us
    pallas_call x1, Pallas kernels: 5.26 us -> 3.94 us  [first_mean(): pl.pallas_call(first_mean_kernel, in_specs=in_vmem(3) + in_hbm(2), out_sp...]
    pallas_call x4 -> x5, Pallas kernels: 15.9 us -> 16.8 us  [the longest x1 5.24 us: later_dense(): pl.pallas_call(later_dense_kernel, in_specs=[pl.BlockSpec(memory_space=pl...]
  transfers between devices with their start and end apart: 12 -> 12, of which waited for: 5 -> 4; matrix products, arithmetic and copies ran while one was open for 0% -> 0% of each run, Pallas kernels for 25% -> 29%
where the time goes in v3:
time: 103 us; the launch traced here: 102 us
  starting transfers between devices  41.5 us (40%)
  Pallas kernels  36.8 us (36%)
  waiting for transfers between devices  22 us (21%)
  between operations  1.43 us (1%)
    all_to_all x2, starting transfers between devices, on_device(): lax.all_to_all(wire, 'dom', split_axis=0, concat_axis=0, tiled=True)  22.3 us
    all_to_all x2, waiting for transfers between devices, on_device(): lax.all_to_all(wire, 'dom', split_axis=0, concat_axis=0, tiled=True)  13.9 us
    ppermute x9, starting transfers between devices, from_feat(): lax.ppermute(value, 'feat', [(j, (j - k) % FEATS) for j in range(FEATS)])  13 us
    pallas_call x1, Pallas kernels, local_sum(): pl.pallas_call(local_kernel, in_specs=[pl.BlockSpec(memory_space=pltpu.SM...  7.78 us
    all_to_all x1, waiting for transfers between devices, on_device(): lax.all_to_all(sums, 'dom', split_axis=0, concat_axis=0, tiled=True)  6.98 us
    all_to_all x1, starting transfers between devices, on_device(): lax.all_to_all(sums, 'dom', split_axis=0, concat_axis=0, tiled=True)  6.2 us
    pallas_call x1, Pallas kernels, later_dense(): pl.pallas_call(later_dense_kernel, in_specs=[pl.BlockSpec(memory_space=pl...  5.24 us
    pallas_call x1, Pallas kernels, local_back(): pl.pallas_call(back_kernel, in_specs=in_vmem(6) + in_hbm(1), out_specs=in...  4.26 us
  transfers between devices with their start and end apart: 12, of which 4 were waited for; matrix products, arithmetic and copies ran while one was open for 0% of the time, Pallas kernels for 29%

profile of v3, /device:TPU:1, one launch (start us, length us, event | category | flops | bytes accessed | tf_op | source)
XLA Modules:
  0.0 102.4 jit_solution(10920921935601541366)
XLA Ops:
  0.6 1.1 %bundle.1.refs_2_.refs_9_ = bf16[144,2176]{1,0:T(8,128)(2,1)S(1)} custom-call(bf16[64,2048]{1,0:T(8,128)(2,1)} %bitcast.28, bf16[64,2048]{1,0:T(8,128)(2,1)} %bitcast.27, bf16[64,256]{1,0:T(8,128)(2,1)} %self_hbm.1, bf16[64,256]{1,0:T(8,128)(2,1)} %neigh_hbm.1, f32[1,64]{1,0:T(1,128)} %bitcast.31), custom_call_target="tpu_custom_call" | custom-call | flops 1000000 | bytes 2000000 | tf_op jit(solution)/shard_map/bundle/pallas_call | solution.py:142
  1.8 2.1 %collective-permute-start.2 = (bf16[144,2176]{1,0:T(8,128)(2,1)S(1)}, bf16[144,2176]{1,0:T(8,128)(2,1)S(1)}, u32[]{:S(2)}, u32[]{:S(2)}) collective-permute-start(bf16[144,2176]{1,0:T(8,128)(2,1)S(1)} %bundle.1.refs_2_.refs_9_), channel_id=1, source_target_pairs={{0,1},{1,2},{2,3},{3,0},{4,5},{5,6},{6,7},{7,4},{8,9},{9,10},{10,1... | collective-permute-start | bytes 1880072 | tf_op jit(solution)/shard_map/ppermute | solution.py:647
  3.9 2.5 %collective-permute-start.1 = (bf16[144,2176]{1,0:T(8,128)(2,1)S(1)}, bf16[144,2176]{1,0:T(8,128)(2,1)S(1)}, u32[]{:S(2)}, u32[]{:S(2)}) collective-permute-start(bf16[144,2176]{1,0:T(8,128)(2,1)S(1)} %bundle.1.refs_2_.refs_9_), channel_id=1, source_target_pairs={{0,2},{1,3},{2,0},{3,1},{4,6},{5,7},{6,4},{7,5},{8,10},{9,11},{10,... | collective-permute-start | bytes 1880072 | tf_op jit(solution)/shard_map/ppermute | solution.py:647
  6.3 1.2 %collective-permute-start = (bf16[144,2176]{1,0:T(8,128)(2,1)S(1)}, bf16[144,2176]{1,0:T(8,128)(2,1)}, u32[]{:S(2)}, u32[]{:S(2)}) collective-permute-start(bf16[144,2176]{1,0:T(8,128)(2,1)S(1)} %bundle.1.refs_2_.refs_9_), channel_id=1, source_target_pairs={{0,3},{1,0},{2,1},{3,2},{4,7},{5,4},{6,5},{7,6},{8,11},{9,8},{10,9... | collective-permute-start | bytes 1880072 | tf_op jit(solution)/shard_map/ppermute | solution.py:647
  7.5 3.4 %gather_rows.1 = (bf16[1024,128]{1,0:T(8,128)(2,1)}, f32[16,2048]{1,0:T(8,128)S(1)}) custom-call(s32[4]{0:T(128)} %hub_hbm.2, s32[24,64]{1,0:T(8,128)} %bitcast.33, s32[1,64]{1,0:T(1,128)} %count_hbm.1, bf16[64,2048]{1,0:T(8,128)(2,1)} %bitcast.29, s32[1,2048]{1,0:T(1,128)} %bitcast.34), custom_call_target="tpu_custom_call" | custom-call | flops 2147483648 | bytes 1000000 | tf_op jit(solution)/shard_map/gather_rows/pallas_call | solution.py:191
  10.9 13.2 %all-to-all-start = ((bf16[64,16,128]{2,1,0:T(8,128)(2,1)}), bf16[64,16,128]{2,1,0:T(8,128)(2,1)S(1)}, u32[]{:S(2)}, u32[]{:S(2)}) async-start(bf16[64,16,128]{2,1,0:T(8,128)(2,1)} %bitcast.6), calls=%async_computation | async-start | bytes 524288 | tf_op jit(solution)/shard_map/all_to_all | solution.py:679
  24.7 7.8 %local_sum.1 = (f32[64,2048]{1,0:T(8,128)S(1)}, bf16[2048,2048]{1,0:T(8,128)(2,1)}) custom-call(s32[1]{0:T(128)S(6)} %copy.20.count_ref, s32[128]{0:T(128)} %src_hbm.1, s32[128]{0:T(128)} %dst_hbm.1, bf16[128,128,128]{2,1,0:T(8,128)(2,1)} %tiles_hbm.1, bf16[64,2048]{1,0:T(8,128)(2,1)} %bitcast.30), custom_call_target="tpu_custom_call" | custom-call | flops 2147483648 | bytes 13000000 | tf_op jit(solution)/shard_map/local_sum/pallas_call | solution.py:249
  32.5 3.6 %all-to-all-done = bf16[64,16,128]{2,1,0:T(8,128)(2,1)S(1)} async-done(((bf16[64,16,128]{2,1,0:T(8,128)(2,1)}), bf16[64,16,128]{2,1,0:T(8,128)(2,1)S(1)}, u32[]{:S(2)}, u32[]{:S(2)}) %all-to-all-start) | async-done | bytes 262176 | tf_op jit(solution)/shard_map/all_to_all | solution.py:679
  36.1 3.9 %mean_rows.2 = (bf16[64,1024]{1,0:T(8,128)(2,1)S(1)}, bf16[1536,64]{1,0:T(8,128)(2,1)S(1)}, bf16[256,64]{1,0:T(8,128)(2,1)S(1)}) custom-call(bf16[1024,128]{1,0:T(8,128)(2,1)S(1)} %bitcast.25, f32[64,2048]{1,0:T(8,128)S(1)} %get-tuple-element.43.local_ref, f32[16,2048]{1,0:T(8,128)S(1)} %get-tuple-element.44.index_ref.refs_4_, bf16[2048,1536]{1,0:T(8,128)(2,1)} %refs_12_.1, ...), custom_call_target="tpu_custom_call" | custom-call | flops 939524096 | bytes 1000000 | tf_op jit(solution)/shard_map/mean_rows/pallas_call | solution.py:337
  40.0 0.0 collective-permute-done.1.refs_4_.refs_11_
  40.0 0.0 collective-permute-done.refs_3_.refs_10_
  40.1 0.4 collective-permute-start.5
  40.4 0.6 collective-permute-start.4
  41.0 1.9 %collective-permute-start.3 = (bf16[64,1024]{1,0:T(8,128)(2,1)S(1)}, bf16[64,1024]{1,0:T(8,128)(2,1)S(1)}, u32[]{:S(2)}, u32[]{:S(2)}) collective-permute-start(bf16[64,1024]{1,0:T(8,128)(2,1)S(1)} %get-tuple-element.47.refs_0_), channel_id=1, source_target_pairs={{0,3},{1,0},{2,1},{3,2},{4,7},{5,4},{6,5},{7,6},{8,11},{9,8},{10,9... | collective-permute-start | bytes 393224 | tf_op jit(solution)/shard_map/ppermute | solution.py:647
  42.9 4.1 %mean_rows.3 = (bf16[64,1024]{1,0:T(8,128)(2,1)S(1)}, bf16[4,256,128]{2,1,0:T(8,128)(2,1)S(1)}, f32[256,128]{1,0:T(8,128)S(1)}, bf16[128,256]{1,0:T(8,128)(2,1)S(1)}, bf16[4,128,1024]{2,1,0:T(8,128)(2,1)S(1)}) custom-call(s32[1]{0:T(128)} %bitcast.8.mine_ref, bf16[1536,64]{1,0:T(8,128)(2,1)S(1)} %get-tuple-element.48.rows_ref, ...), custom_call_target="tpu_custom_call" | custom-call | flops 939524096 | bytes 1000000 | tf_op jit(solution)/shard_map/mean_rows/pallas_call | solution.py:369
  47.1 0.5 collective-permute-start.8
  47.6 1.9 %collective-permute-start.7 = (bf16[64,1024]{1,0:T(8,128)(2,1)S(1)}, bf16[64,1024]{1,0:T(8,128)(2,1)S(1)}, u32[]{:S(2)}, u32[]{:S(2)}) collective-permute-start(bf16[64,1024]{1,0:T(8,128)(2,1)S(1)} %get-tuple-element.59.refs_0_), channel_id=1, source_target_pairs={{0,2},{1,3},{2,0},{3,1},{4,6},{5,7},{6,4},{7,5},{8,10},{9,11},{10,... | collective-permute-start | bytes 393224 | tf_op jit(solution)/shard_map/ppermute | solution.py:647
  49.5 0.0 collective-permute-done.5.refs_3_
  49.5 2.0 %collective-permute-start.6 = (bf16[64,1024]{1,0:T(8,128)(2,1)S(1)}, bf16[64,1024]{1,0:T(8,128)(2,1)S(1)}, u32[]{:S(2)}, u32[]{:S(2)}) collective-permute-start(bf16[64,1024]{1,0:T(8,128)(2,1)S(1)} %get-tuple-element.59.refs_0_), channel_id=1, source_target_pairs={{0,3},{1,0},{2,1},{3,2},{4,7},{5,4},{6,5},{7,6},{8,11},{9,8},{10,9... | collective-permute-start | bytes 393224 | tf_op jit(solution)/shard_map/ppermute | solution.py:647
  51.5 0.0 collective-permute-done.4.refs_2_
  51.5 2.9 %dense.2 = (bf16[64,1024]{1,0:T(8,128)(2,1)S(1)}, bf16[64,1024]{1,0:T(8,128)(2,1)S(1)}, f32[64,1024]{1,0:T(8,128)S(1)}, f32[64,1536]{1,0:T(8,128)S(1)}, f32[64,2...) custom-call(bf16[64,1024]{1,0:T(8,128)(2,1)S(1)} %get-tuple-element.47.refs_0_, ...), custom_call_target="tpu_custom_call" | custom-call | flops 1073741824 | bytes 6000000 | tf_op jit(solution)/shard_map/dense/pallas_call | solution.py:527
  54.4 0.0 collective-permute-done.7.refs_2_
  54.4 1.0 %collective-permute-done.6.refs_1_ = bf16[64,1024]{1,0:T(8,128)(2,1)S(1)} collective-permute-done((bf16[64,1024]{1,0:T(8,128)(2,1)S(1)}, bf16[64,1024]{1,0:T(8,128)(2,1)S(1)}, u32[]{:S(2)}, u32[]{:S(2)}) %collective-permute-start.6) | collective-permute-done | bytes 131104 | tf_op jit(solution)/shard_map/ppermute | solution.py:647
  55.5 5.2 %dense.3 = (bf16[64,1024]{1,0:T(8,128)(2,1)S(1)}, bf16[64,1024]{1,0:T(8,128)(2,1)S(1)}, f32[64,1024]{1,0:T(8,128)S(1)}, bf16[1536,128]{1,0:T(8,128)(2,1)}) custom-call(s32[1]{0:T(128)} %bitcast.8.mine_ref, bf16[64,1024]{1,0:T(8,128)(2,1)S(1)} %get-tuple-element.59.refs_0_, bf16[64,1024]{1,0:T(8,128)(2,1)S(1)} %collective-permute-done.6.refs_1_, ...), custom_call_target="tpu_custom_call" | custom-call | flops 1073741824 | bytes 6000000 | tf_op jit(solution)/shard_map/dense/pallas_call | solution.py:542
  60.7 9.1 %all-to-all-start.1 = ((bf16[64,24,128]{2,1,0:T(8,128)(2,1)}), bf16[64,24,128]{2,1,0:T(8,128)(2,1)S(1)}, u32[]{:S(2)}, u32[]{:S(2)}) async-start(bf16[64,24,128]{2,1,0:T(8,128)(2,1)} %bitcast.10), calls=%async_computation.1 | async-start | bytes 786432 | tf_op jit(solution)/shard_map/all_to_all | solution.py:694
  69.9 4.3 %local_back.1 = (f32[64,2048]{1,0:T(8,128)S(1)}, bf16[64,2048]{1,0:T(8,128)(2,1)}) custom-call(f32[64,1024]{1,0:T(8,128)S(1)} %get-tuple-element.58.ginput0, f32[64,1024]{1,0:T(8,128)S(1)} %get-tuple-element.64.ginput1, bf16[64,1024]{1,0:T(8,128)(2,1)S(1)} %get-tuple-element.65.gmean0, bf16[64,1024]{1,0:T(8,128)(2,1)S(1)} %get-tuple-element.66.gmean1, ...), custom_call_target="tpu_custom_call" | custom-call | flops 2147483648 | bytes 10000000 | tf_op jit(solution)/shard_map/local_back/pallas_call | solution.py:575
  74.1 10.3 %all-to-all-done.1 = bf16[64,24,128]{2,1,0:T(8,128)(2,1)S(1)} async-done(((bf16[64,24,128]{2,1,0:T(8,128)(2,1)}), bf16[64,24,128]{2,1,0:T(8,128)(2,1)S(1)}, u32[]{:S(2)}, u32[]{:S(2)}) %all-to-all-start.1) | async-done | bytes 393248 | tf_op jit(solution)/shard_map/all_to_all | solution.py:694
  84.5 0.7 reduce_grads.1
  85.2 6.2 %all-to-all-start.2 = ((f32[64,4,128]{2,1,0:T(4,128)}), f32[64,4,128]{2,1,0:T(4,128)S(1)}, u32[]{:S(2)}, u32[]{:S(2)}) async-start(f32[64,4,128]{2,1,0:T(4,128)} %bitcast.13), calls=%async_computation.2 | async-start | bytes 262144 | tf_op jit(solution)/shard_map/all_to_all | solution.py:698
  91.4 3.4 %scatter_rows.1 = bf16[64,2048]{1,0:T(8,128)(2,1)} custom-call(bf16[1536,128]{1,0:T(8,128)(2,1)S(1)} %bitcast.24, f32[16,2048]{1,0:T(8,128)S(1)} %get-tuple-element.44.index_ref.refs_4_, f32[64,2048]{1,0:T(8,128)S(1)} %get-tuple-element.74.total_ref), custom_call_target="tpu_custom_call" | custom-call | flops 2147483648 | bytes 2000000 | tf_op jit(solution)/shard_map/scatter_rows/pallas_call | solution.py:634
  94.8 7.0 %all-to-all-done.2 = f32[64,4,128]{2,1,0:T(4,128)S(1)} async-done(((f32[64,4,128]{2,1,0:T(4,128)}), f32[64,4,128]{2,1,0:T(4,128)S(1)}, u32[]{:S(2)}, u32[]{:S(2)}) %all-to-all-start.2) | async-done | bytes 131104 | tf_op jit(solution)/shard_map/all_to_all | solution.py:698
  101.8 0.7 slice_bitcast_fusion
  (7 shorter events, 0.0 us)
Async XLA Ops:
  1.8 38.2 %collective-permute-start.2 = (bf16[144,2176]{1,0:T(8,128)(2,1)S(1)}, bf16[144,2176]{1,0:T(8,128)(2,1)S(1)}, u32[]{:S(2)}, u32[]{:S(2)}) collective-permute-start(bf16[144,2176]{1,0:T(8,128)(2,1)S(1)} %bundle.1.refs_2_.refs_9_), channel_id=1, source_target_pairs={{0,1},{1,2},{2,3},{3,0},{4,5},{5,6},{6,7},{7,4},{8,9},{9,10},{10,1... | collective-permute-start | bytes 1880072 | tf_op jit(solution)/shard_map/ppermute | solution.py:647
  3.9 36.1 %collective-permute-start.1 = (bf16[144,2176]{1,0:T(8,128)(2,1)S(1)}, bf16[144,2176]{1,0:T(8,128)(2,1)S(1)}, u32[]{:S(2)}, u32[]{:S(2)}) collective-permute-start(bf16[144,2176]{1,0:T(8,128)(2,1)S(1)} %bundle.1.refs_2_.refs_9_), channel_id=1, source_target_pairs={{0,2},{1,3},{2,0},{3,1},{4,6},{5,7},{6,4},{7,5},{8,10},{9,11},{10,... | collective-permute-start | bytes 1880072 | tf_op jit(solution)/shard_map/ppermute | solution.py:647
  6.3 33.7 %collective-permute-start = (bf16[144,2176]{1,0:T(8,128)(2,1)S(1)}, bf16[144,2176]{1,0:T(8,128)(2,1)}, u32[]{:S(2)}, u32[]{:S(2)}) collective-permute-start(bf16[144,2176]{1,0:T(8,128)(2,1)S(1)} %bundle.1.refs_2_.refs_9_), channel_id=1, source_target_pairs={{0,3},{1,0},{2,1},{3,2},{4,7},{5,4},{6,5},{7,6},{8,11},{9,8},{10,9... | collective-permute-start | bytes 1880072 | tf_op jit(solution)/shard_map/ppermute | solution.py:647
  10.9 25.2 %all-to-all-start = ((bf16[64,16,128]{2,1,0:T(8,128)(2,1)}), bf16[64,16,128]{2,1,0:T(8,128)(2,1)S(1)}, u32[]{:S(2)}, u32[]{:S(2)}) async-start(bf16[64,16,128]{2,1,0:T(8,128)(2,1)} %bitcast.6), calls=%async_computation | async-start | bytes 524288 | tf_op jit(solution)/shard_map/all_to_all | solution.py:679
  40.0 2.9 %copy-start = (bf16[144,2176]{1,0:T(8,128)(2,1)}, bf16[144,2176]{1,0:T(8,128)(2,1)S(1)}, u32[]{:S(2)}) copy-start(bf16[144,2176]{1,0:T(8,128)(2,1)S(1)} %collective-permute-done.2.refs_5_.refs_12_) | copy-start | bytes 1880068
  40.0 2.9 %copy-start.1 = (bf16[144,2176]{1,0:T(8,128)(2,1)}, bf16[144,2176]{1,0:T(8,128)(2,1)S(1)}, u32[]{:S(2)}) copy-start(bf16[144,2176]{1,0:T(8,128)(2,1)S(1)} %collective-permute-done.1.refs_4_.refs_11_) | copy-start | bytes 1880068
  40.1 9.4 %collective-permute-start.5 = (bf16[64,1024]{1,0:T(8,128)(2,1)S(1)}, bf16[64,1024]{1,0:T(8,128)(2,1)S(1)}, u32[]{:S(2)}, u32[]{:S(2)}) collective-permute-start(bf16[64,1024]{1,0:T(8,128)(2,1)S(1)} %get-tuple-element.47.refs_0_), channel_id=1, source_target_pairs={{0,1},{1,2},{2,3},{3,0},{4,5},{5,6},{6,7},{7,4},{8,9},{9,10},{10,1... | collective-permute-start | bytes 393224 | tf_op jit(solution)/shard_map/ppermute | solution.py:647
  40.4 11.0 %collective-permute-start.4 = (bf16[64,1024]{1,0:T(8,128)(2,1)S(1)}, bf16[64,1024]{1,0:T(8,128)(2,1)S(1)}, u32[]{:S(2)}, u32[]{:S(2)}) collective-permute-start(bf16[64,1024]{1,0:T(8,128)(2,1)S(1)} %get-tuple-element.47.refs_0_), channel_id=1, source_target_pairs={{0,2},{1,3},{2,0},{3,1},{4,6},{5,7},{6,4},{7,5},{8,10},{9,11},{10,... | collective-permute-start | bytes 393224 | tf_op jit(solution)/shard_map/ppermute | solution.py:647
  41.0 10.4 %collective-permute-start.3 = (bf16[64,1024]{1,0:T(8,128)(2,1)S(1)}, bf16[64,1024]{1,0:T(8,128)(2,1)S(1)}, u32[]{:S(2)}, u32[]{:S(2)}) collective-permute-start(bf16[64,1024]{1,0:T(8,128)(2,1)S(1)} %get-tuple-element.47.refs_0_), channel_id=1, source_target_pairs={{0,3},{1,0},{2,1},{3,2},{4,7},{5,4},{6,5},{7,6},{8,11},{9,8},{10,9... | collective-permute-start | bytes 393224 | tf_op jit(solution)/shard_map/ppermute | solution.py:647
  47.1 7.3 %collective-permute-start.8 = (bf16[64,1024]{1,0:T(8,128)(2,1)S(1)}, bf16[64,1024]{1,0:T(8,128)(2,1)S(1)}, u32[]{:S(2)}, u32[]{:S(2)}) collective-permute-start(bf16[64,1024]{1,0:T(8,128)(2,1)S(1)} %get-tuple-element.59.refs_0_), channel_id=1, source_target_pairs={{0,1},{1,2},{2,3},{3,0},{4,5},{5,6},{6,7},{7,4},{8,9},{9,10},{10,1... | collective-permute-start | bytes 393224 | tf_op jit(solution)/shard_map/ppermute | solution.py:647
  47.6 6.8 %collective-permute-start.7 = (bf16[64,1024]{1,0:T(8,128)(2,1)S(1)}, bf16[64,1024]{1,0:T(8,128)(2,1)S(1)}, u32[]{:S(2)}, u32[]{:S(2)}) collective-permute-start(bf16[64,1024]{1,0:T(8,128)(2,1)S(1)} %get-tuple-element.59.refs_0_), channel_id=1, source_target_pairs={{0,2},{1,3},{2,0},{3,1},{4,6},{5,7},{6,4},{7,5},{8,10},{9,11},{10,... | collective-permute-start | bytes 393224 | tf_op jit(solution)/shard_map/ppermute | solution.py:647
  49.5 6.0 %collective-permute-start.6 = (bf16[64,1024]{1,0:T(8,128)(2,1)S(1)}, bf16[64,1024]{1,0:T(8,128)(2,1)S(1)}, u32[]{:S(2)}, u32[]{:S(2)}) collective-permute-start(bf16[64,1024]{1,0:T(8,128)(2,1)S(1)} %get-tuple-element.59.refs_0_), channel_id=1, source_target_pairs={{0,3},{1,0},{2,1},{3,2},{4,7},{5,4},{6,5},{7,6},{8,11},{9,8},{10,9... | collective-permute-start | bytes 393224 | tf_op jit(solution)/shard_map/ppermute | solution.py:647
  60.7 23.8 %all-to-all-start.1 = ((bf16[64,24,128]{2,1,0:T(8,128)(2,1)}), bf16[64,24,128]{2,1,0:T(8,128)(2,1)S(1)}, u32[]{:S(2)}, u32[]{:S(2)}) async-start(bf16[64,24,128]{2,1,0:T(8,128)(2,1)} %bitcast.10), calls=%async_computation.1 | async-start | bytes 786432 | tf_op jit(solution)/shard_map/all_to_all | solution.py:694
  85.2 16.6 %all-to-all-start.2 = ((f32[64,4,128]{2,1,0:T(4,128)}), f32[64,4,128]{2,1,0:T(4,128)S(1)}, u32[]{:S(2)}, u32[]{:S(2)}) async-start(f32[64,4,128]{2,1,0:T(4,128)} %bitcast.13), calls=%async_computation.2 | async-start | bytes 262144 | tf_op jit(solution)/shard_map/all_to_all | solution.py:698

commit v4 on v3

--- a/solution.py
+++ b/solution.py
@@ -26,10 +26,10 @@
 BUNDLE = 144
 WIDTH = 2048 + 128
 PACK = 2 * FIN
-HALF = NODES // 2
+SIZES = (1280, 768)
+STARTS = (0, 1280)
 SLOTS = PEERS * ROWS
 CHUNK = 256
-NEAR = HALF // 2
 
 def matmul(left, right):
     return lax.dot_general(
@@ -289,9 +289,10 @@
 
 
 def half_copies(part, halo_hbm, hub_hbm, halo_ref, hub_ref, sems):
+    near = SIZES[part] // 2
     return [
         adjacency_copies(
-            part * HALF + i * NEAR, NEAR, 1,
+            STARTS[part] + i * near, near, 1,
             halo_hbm, hub_hbm, halo_ref.at[i], hub_ref.at[i], sems.at[i],
         )
         for i in range(2)
@@ -299,11 +300,12 @@
 
 
 def mean_half(part, copies, rows, hubs, halo_ref, hub_ref, local_ref, index_ref, mean_ref):
+    near = SIZES[part] // 2
     for i in range(2):
         for copy in copies[i]:
             copy.wait()
         mean_part(
-            part * HALF + i * NEAR, i * NEAR, rows, hubs, halo_ref[i], hub_ref[i],
+            STARTS[part] + i * near, i * near, rows, hubs, halo_ref[i], hub_ref[i],
             local_ref, index_ref, mean_ref,
         )
 
@@ -325,23 +327,25 @@
     )
 
 
-HALF_SCRATCH = [
-    pltpu.VMEM((2, NEAR, HALO), BF),
-    pltpu.VMEM((2, NEAR, HUB_ALL), BF),
-    pltpu.SemaphoreType.DMA((2, 2)),
-]
+def half_scratch(part):
+    near = SIZES[part] // 2
+    return [
+        pltpu.VMEM((2, near, HALO), BF),
+        pltpu.VMEM((2, near, HUB_ALL), BF),
+        pltpu.SemaphoreType.DMA((2, 2)),
+    ]
 
 
 def first_mean(wire, halo_adj, hub_adj, local, index):
-    shapes = [(FIN, HALF), (HALO, FIN), (HUB_ALL, FIN)]
+    shapes = [(FIN, SIZES[0]), (HALO, FIN), (HUB_ALL, FIN)]
     return pl.pallas_call(
         first_mean_kernel,
         in_specs=in_vmem(3) + in_hbm(2),
         out_specs=in_vmem(len(shapes)),
         out_shape=[pltpu.VMEM(shape, BF) for shape in shapes],
-        scratch_shapes=HALF_SCRATCH,
-        compiler_params=params(),
-        cost_estimate=cost(HALF * (HALO + HUB_ALL) * 512, 1000000),
+        scratch_shapes=half_scratch(0),
+        compiler_params=params(),
+        cost_estimate=cost(1024 * (HALO + HUB_ALL) * 512, 1000000),
         name="mean_rows",
     )(wire, local, index, *keep_hbm(halo_adj, hub_adj))
 
@@ -375,20 +379,20 @@
         + in_hbm(FEATS - 1),
         out_specs=in_vmem(5),
         out_shape=[
-            pltpu.VMEM((FIN, HALF), BF),
+            pltpu.VMEM((FIN, SIZES[1]), BF),
             pltpu.VMEM((FEATS, FOUT, PACK), BF),
             pltpu.VMEM((FOUT, LANES), F32),
             pltpu.VMEM((PACK, FOUT), BF),
-            pltpu.VMEM((FEATS, PACK, HALF), BF),
-        ],
-        scratch_shapes=HALF_SCRATCH
+            pltpu.VMEM((FEATS, PACK, SIZES[0]), BF),
+        ],
+        scratch_shapes=half_scratch(1)
         + [
             pltpu.VMEM((FEATS, 16, WIDTH), BF),
             pltpu.SemaphoreType.DMA((FEATS,)),
             pltpu.SemaphoreType.DMA((FEATS,)),
         ],
         compiler_params=params(),
-        cost_estimate=cost(HALF * (HALO + HUB_ALL) * 512, 1000000),
+        cost_estimate=cost(1024 * (HALO + HUB_ALL) * 512, 1000000),
         name="mean_rows",
     )(
         mine, *known, local, index, *keep_hbm(halo_adj, hub_adj),
@@ -439,7 +443,7 @@
 
 
 def value_copies(part, bundles, value_ref, sems):
-    own = pl.ds(part * HALF, HALF)
+    own = pl.ds(STARTS[part], SIZES[part])
     return start_all(
         [(bundles[k].at[pl.ds(0, PACK), own], value_ref.at[k]) for k in range(FEATS)], sems
     )
@@ -450,9 +454,9 @@
     halo_ref, hub_ref, out_ref, gmean_ref, ginput_ref, gpre_ref,
 ):
     chunk = CHUNK
-    for i in range(HALF // chunk):
+    for i in range(SIZES[part] // chunk):
         here = slice(i * chunk, (i + 1) * chunk)
-        whole = slice(part * HALF + i * chunk, part * HALF + (i + 1) * chunk)
+        whole = slice(STARTS[part] + i * chunk, STARTS[part] + (i + 1) * chunk)
         pre = jnp.tile(bias_ref[...], (1, chunk // LANES))
         for k in range(FEATS):
             both = jnp.concatenate([value_ref[k, :FIN, here], means[k][:, here]], axis=0)
@@ -466,7 +470,8 @@
         back = matmul(back_ref[...], gpre)
         ginput_ref[:, here] = back[:FIN]
         gmean_ref[:, here] = (back[FIN:] / index_ref[8:9, whole]).astype(BF)
-    left = jnp.concatenate([value_ref[0, :FIN], means[0][...], jnp.ones((16, HALF), BF)], axis=0)
+    ones = jnp.ones((16, SIZES[part]), BF)
+    left = jnp.concatenate([value_ref[0, :FIN], means[0][...], ones], axis=0)
     grads = matmul_nt(left, gpre_ref[...])
     for copy in copies:
         copy.wait()
@@ -481,7 +486,7 @@
     bundles, halo_hbm, hub_hbm = refs[9:13], refs[13], refs[14]
     out_ref, gmean_ref, ginput_ref, halo_acc, hub_acc, grad_acc, later_ref = refs[15:22]
     gpre_ref, halo_ref, hub_ref, sems, later_sems = refs[22:]
-    copies = adjacency_copies(0, HALF, 4, halo_hbm, hub_hbm, halo_ref, hub_ref, sems)
+    copies = adjacency_copies(STARTS[0], SIZES[0], 4, halo_hbm, hub_hbm, halo_ref, hub_ref, sems)
     later = value_copies(1, bundles, later_ref, later_sems)
     halo_acc[...], hub_acc[...], grad_acc[...] = dense_half(
         0, means, value_ref, weight_ref, bias_ref, back_ref, index_ref, copies,
@@ -497,7 +502,7 @@
     held_halo, held_hub, held_grad, halo_hbm, hub_hbm = refs[9:14]
     out_ref, gmean_ref, ginput_ref, wire_ref = refs[14:18]
     gpre_ref, halo_ref, hub_ref, halo_acc, hub_acc, grad_acc, sems = refs[18:]
-    copies = adjacency_copies(HALF, HALF, 4, halo_hbm, hub_hbm, halo_ref, hub_ref, sems)
+    copies = adjacency_copies(STARTS[1], SIZES[1], 4, halo_hbm, hub_hbm, halo_ref, hub_ref, sems)
     halos, hubs, grads = dense_half(
         1, means, value_ref, weight_ref, bias_ref, back_ref, index_ref, copies,
         halo_ref, hub_ref, out_ref, gmean_ref, ginput_ref, gpre_ref,
@@ -509,27 +514,31 @@
 
 
 ACCUMULATORS = [(FIN, HALO), (FIN, HUB_ALL), (PACK + 16, FOUT)]
-HALVES = [
-    jax.ShapeDtypeStruct((FIN, HALF), BF),
-    jax.ShapeDtypeStruct((FIN, HALF), BF),
-    jax.ShapeDtypeStruct((FIN, HALF), F32),
-]
-ADJACENCY = [
-    pltpu.VMEM((FOUT, HALF), BF),
-    pltpu.VMEM((HALF, HALO), BF),
-    pltpu.VMEM((HALF, HUB_ALL), BF),
-]
+def halves(part):
+    return [
+        jax.ShapeDtypeStruct((FIN, SIZES[part]), BF),
+        jax.ShapeDtypeStruct((FIN, SIZES[part]), BF),
+        jax.ShapeDtypeStruct((FIN, SIZES[part]), F32),
+    ]
+
+
+def adjacency_scratch(part):
+    return [
+        pltpu.VMEM((FOUT, SIZES[part]), BF),
+        pltpu.VMEM((SIZES[part], HALO), BF),
+        pltpu.VMEM((SIZES[part], HUB_ALL), BF),
+    ]
 
 
 def first_dense(means, index, weights, value, bundles, halo_adj, hub_adj):
-    out_shape = HALVES + [pltpu.VMEM(shape, F32) for shape in ACCUMULATORS]
-    out_shape += [pltpu.VMEM((FEATS, PACK, HALF), BF)]
+    out_shape = halves(0) + [pltpu.VMEM(shape, F32) for shape in ACCUMULATORS]
+    out_shape += [pltpu.VMEM((FEATS, PACK, SIZES[1]), BF)]
     return pl.pallas_call(
         first_dense_kernel,
         in_specs=in_vmem(9) + [pl.BlockSpec(memory_space=pl.ANY)] + in_hbm(FEATS + 1),
         out_specs=in_vmem(len(out_shape)),
         out_shape=out_shape,
-        scratch_shapes=ADJACENCY
+        scratch_shapes=adjacency_scratch(0)
         + [pltpu.SemaphoreType.DMA((5,)), pltpu.SemaphoreType.DMA((FEATS,))],
         compiler_params=params(),
         cost_estimate=cost(NODES * 2048 * 256, 6000000),
@@ -538,13 +547,13 @@
 
 
 def later_dense(mine, means, index, weights, value, held, halo_adj, hub_adj):
-    out_shape = HALVES + [jax.ShapeDtypeStruct((PEERS * WIDE, LANES), BF)]
+    out_shape = halves(1) + [jax.ShapeDtypeStruct((PEERS * WIDE, LANES), BF)]
     return pl.pallas_call(
         later_dense_kernel,
         in_specs=[pl.BlockSpec(memory_space=pltpu.SMEM)] + in_vmem(12) + in_hbm(2),
         out_specs=in_vmem(len(out_shape)),
         out_shape=out_shape,
-        scratch_shapes=ADJACENCY
+        scratch_shapes=adjacency_scratch(1)
         + [pltpu.VMEM(shape, F32) for shape in ACCUMULATORS]
         + [pltpu.SemaphoreType.DMA((5,))],
         compiler_params=params(),
@@ -556,18 +565,18 @@
 def back_kernel(
     ginput0, ginput1, gmean0, gmean1, out0, out1, adj_hbm, total_ref, out_ref, adj_ref, sems
 ):
-    chunk = 512
+    chunk = 256
     here = [pl.ds(i * chunk, chunk) for i in range(NODES // chunk)]
     blocks = start_all([(adj_hbm.at[:, i], adj_ref.at[:, i]) for i in here], sems)
-    out_ref[:, :HALF] = out0[...]
-    out_ref[:, HALF:] = out1[...]
+    out_ref[:, :SIZES[0]] = out0[...]
+    out_ref[:, SIZES[0]:] = out1[...]
     for i in range(NODES // chunk):
         blocks[i].wait()
         here = slice(i * chunk, (i + 1) * chunk)
-        total = matmul(gmean0[...], adj_ref[:HALF, here])
-        total = total + matmul(gmean1[...], adj_ref[HALF:, here])
-        half = ginput0 if i * chunk < HALF else ginput1
-        start = i * chunk % HALF
+        total = matmul(gmean0[...], adj_ref[:SIZES[0], here])
+        total = total + matmul(gmean1[...], adj_ref[SIZES[0]:, here])
+        half = ginput0 if i * chunk < SIZES[0] else ginput1
+        start = i * chunk % SIZES[0]
         total_ref[:, here] = total + half[:, start:start + chunk]
 
 
@@ -582,7 +591,7 @@
         ],
         scratch_shapes=[
             pltpu.VMEM((NODES, NODES), BF),
-            pltpu.SemaphoreType.DMA((4,)),
+            pltpu.SemaphoreType.DMA((8,)),
         ],
         compiler_params=params(),
         cost_estimate=cost(2 * NODES * NODES * 256, 10000000),

time: 103 us -> 102 us (level)
  starting transfers between devices: 41.5 us -> 39.7 us
    ppermute x9, starting transfers between devices: 13 us -> 11.7 us  [from_feat(): lax.ppermute(value, 'feat', [(j, (j - k) % FEATS) for j in range(FEATS)])]
  transfers between devices with their start and end apart: 12 -> 12, of which waited for: 4 -> 6; matrix products, arithmetic and copies ran while one was open for 0% -> 0% of each run, Pallas kernels for 29% -> 30%
where the time goes in v4:
time: 102 us; the launch traced here: 101 us
  starting transfers between devices  39.7 us (39%)
  Pallas kernels  36.7 us (36%)
  waiting for transfers between devices  22.8 us (22%)
  between operations  1.41 us (1%)
    all_to_all x2, starting transfers between devices, on_device(): lax.all_to_all(wire, 'dom', split_axis=0, concat_axis=0, tiled=True)  21.9 us
    all_to_all x2, waiting for transfers between devices, on_device(): lax.all_to_all(wire, 'dom', split_axis=0, concat_axis=0, tiled=True)  13.8 us
    ppermute x9, starting transfers between devices, from_feat(): lax.ppermute(value, 'feat', [(j, (j - k) % FEATS) for j in range(FEATS)])  11.7 us
    pallas_call x1, Pallas kernels, local_sum(): pl.pallas_call(local_kernel, in_specs=[pl.BlockSpec(memory_space=pltpu.SM...  7.05 us
    all_to_all x1, waiting for transfers between devices, on_device(): lax.all_to_all(sums, 'dom', split_axis=0, concat_axis=0, tiled=True)  6.98 us
    all_to_all x1, starting transfers between devices, on_device(): lax.all_to_all(sums, 'dom', split_axis=0, concat_axis=0, tiled=True)  6.2 us
    pallas_call x1, Pallas kernels, local_back(): pl.pallas_call(back_kernel, in_specs=in_vmem(6) + in_hbm(1), out_specs=in...  5.09 us
    pallas_call x1, Pallas kernels, first_mean(): pl.pallas_call(first_mean_kernel, in_specs=in_vmem(3) + in_hbm(2), out_sp...  4.55 us
  transfers between devices with their start and end apart: 12, of which 6 were waited for; matrix products, arithmetic and copies ran while one was open for 0% of the time, Pallas kernels for 30%

profile of v4, /device:TPU:1, one launch (start us, length us, event | category | flops | bytes accessed | tf_op | source)
XLA Modules:
  0.0 101.3 jit_solution(15589465713209766087)
XLA Ops:
  0.6 1.1 %bundle.1.refs_2_.refs_9_ = bf16[144,2176]{1,0:T(8,128)(2,1)S(1)} custom-call(bf16[64,2048]{1,0:T(8,128)(2,1)} %bitcast.28, bf16[64,2048]{1,0:T(8,128)(2,1)} %bitcast.27, bf16[64,256]{1,0:T(8,128)(2,1)} %self_hbm.1, bf16[64,256]{1,0:T(8,128)(2,1)} %neigh_hbm.1, f32[1,64]{1,0:T(1,128)} %bitcast.31), custom_call_target="tpu_custom_call" | custom-call | flops 1000000 | bytes 2000000 | tf_op jit(solution)/shard_map/bundle/pallas_call | solution.py:142
  1.8 2.1 %collective-permute-start.2 = (bf16[144,2176]{1,0:T(8,128)(2,1)S(1)}, bf16[144,2176]{1,0:T(8,128)(2,1)S(1)}, u32[]{:S(2)}, u32[]{:S(2)}) collective-permute-start(bf16[144,2176]{1,0:T(8,128)(2,1)S(1)} %bundle.1.refs_2_.refs_9_), channel_id=1, source_target_pairs={{0,1},{1,2},{2,3},{3,0},{4,5},{5,6},{6,7},{7,4},{8,9},{9,10},{10,1... | collective-permute-start | bytes 1880072 | tf_op jit(solution)/shard_map/ppermute | solution.py:656
  3.9 2.5 %collective-permute-start.1 = (bf16[144,2176]{1,0:T(8,128)(2,1)S(1)}, bf16[144,2176]{1,0:T(8,128)(2,1)}, u32[]{:S(2)}, u32[]{:S(2)}) collective-permute-start(bf16[144,2176]{1,0:T(8,128)(2,1)S(1)} %bundle.1.refs_2_.refs_9_), channel_id=1, source_target_pairs={{0,2},{1,3},{2,0},{3,1},{4,6},{5,7},{6,4},{7,5},{8,10},{9,11},{10,... | collective-permute-start | bytes 1880072 | tf_op jit(solution)/shard_map/ppermute | solution.py:656
  6.3 1.2 %collective-permute-start = (bf16[144,2176]{1,0:T(8,128)(2,1)S(1)}, bf16[144,2176]{1,0:T(8,128)(2,1)}, u32[]{:S(2)}, u32[]{:S(2)}) collective-permute-start(bf16[144,2176]{1,0:T(8,128)(2,1)S(1)} %bundle.1.refs_2_.refs_9_), channel_id=1, source_target_pairs={{0,3},{1,0},{2,1},{3,2},{4,7},{5,4},{6,5},{7,6},{8,11},{9,8},{10,9... | collective-permute-start | bytes 1880072 | tf_op jit(solution)/shard_map/ppermute | solution.py:656
  7.5 3.4 %gather_rows.1 = (bf16[1024,128]{1,0:T(8,128)(2,1)}, f32[16,2048]{1,0:T(8,128)S(1)}) custom-call(s32[4]{0:T(128)} %hub_hbm.2, s32[24,64]{1,0:T(8,128)} %bitcast.33, s32[1,64]{1,0:T(1,128)} %count_hbm.1, bf16[64,2048]{1,0:T(8,128)(2,1)} %bitcast.29, s32[1,2048]{1,0:T(1,128)} %bitcast.34), custom_call_target="tpu_custom_call" | custom-call | flops 2147483648 | bytes 1000000 | tf_op jit(solution)/shard_map/gather_rows/pallas_call | solution.py:191
  10.9 13.2 %all-to-all-start = ((bf16[64,16,128]{2,1,0:T(8,128)(2,1)}), bf16[64,16,128]{2,1,0:T(8,128)(2,1)S(1)}, u32[]{:S(2)}, u32[]{:S(2)}) async-start(bf16[64,16,128]{2,1,0:T(8,128)(2,1)} %bitcast.6), calls=%async_computation | async-start | bytes 524288 | tf_op jit(solution)/shard_map/all_to_all | solution.py:688
  24.7 7.1 %local_sum.1 = (f32[64,2048]{1,0:T(8,128)S(1)}, bf16[2048,2048]{1,0:T(8,128)(2,1)}) custom-call(s32[1]{0:T(128)S(6)} %copy.20.count_ref, s32[128]{0:T(128)} %src_hbm.1, s32[128]{0:T(128)} %dst_hbm.1, bf16[128,128,128]{2,1,0:T(8,128)(2,1)} %tiles_hbm.1, bf16[64,2048]{1,0:T(8,128)(2,1)} %bitcast.30), custom_call_target="tpu_custom_call" | custom-call | flops 2147483648 | bytes 13000000 | tf_op jit(solution)/shard_map/local_sum/pallas_call | solution.py:249
  31.8 4.3 %all-to-all-done = bf16[64,16,128]{2,1,0:T(8,128)(2,1)S(1)} async-done(((bf16[64,16,128]{2,1,0:T(8,128)(2,1)}), bf16[64,16,128]{2,1,0:T(8,128)(2,1)S(1)}, u32[]{:S(2)}, u32[]{:S(2)}) %all-to-all-start) | async-done | bytes 262176 | tf_op jit(solution)/shard_map/all_to_all | solution.py:688
  36.1 4.6 %mean_rows.2 = (bf16[64,1280]{1,0:T(8,128)(2,1)S(1)}, bf16[1536,64]{1,0:T(8,128)(2,1)S(1)}, bf16[256,64]{1,0:T(8,128)(2,1)S(1)}) custom-call(bf16[1024,128]{1,0:T(8,128)(2,1)S(1)} %bitcast.25, f32[64,2048]{1,0:T(8,128)S(1)} %get-tuple-element.43.local_ref, f32[16,2048]{1,0:T(8,128)S(1)} %get-tuple-element.44.index_ref.refs_4_, bf16[2048,1536]{1,0:T(8,128)(2,1)} %refs_12_.1, ...), custom_call_target="tpu_custom_call" | custom-call | flops 939524096 | bytes 1000000 | tf_op jit(solution)/shard_map/mean_rows/pallas_call | solution.py:341
  40.6 0.0 collective-permute-done.2.refs_5_.refs_12_
  40.6 0.0 collective-permute-done.1.refs_4_.refs_11_
  40.7 0.4 collective-permute-start.5
  41.1 0.6 collective-permute-start.4
  41.6 1.9 %collective-permute-start.3 = (bf16[64,1280]{1,0:T(8,128)(2,1)S(1)}, bf16[64,1280]{1,0:T(8,128)(2,1)S(1)}, u32[]{:S(2)}, u32[]{:S(2)}) collective-permute-start(bf16[64,1280]{1,0:T(8,128)(2,1)S(1)} %get-tuple-element.47.refs_0_), channel_id=1, source_target_pairs={{0,3},{1,0},{2,1},{3,2},{4,7},{5,4},{6,5},{7,6},{8,11},{9,8},{10,9... | collective-permute-start | bytes 491528 | tf_op jit(solution)/shard_map/ppermute | solution.py:656
  43.5 3.5 %mean_rows.3 = (bf16[64,768]{1,0:T(8,128)(2,1)S(1)}, bf16[4,256,128]{2,1,0:T(8,128)(2,1)S(1)}, f32[256,128]{1,0:T(8,128)S(1)}, bf16[128,256]{1,0:T(8,128)(2,1)S(1)}, bf16[4,128,1280]{2,1,0:T(8,128)(2,1)S(1)}) custom-call(s32[1]{0:T(128)} %bitcast.8.mine_ref, bf16[1536,64]{1,0:T(8,128)(2,1)S(1)} %get-tuple-element.48.rows_ref, ...), custom_call_target="tpu_custom_call" | custom-call | flops 939524096 | bytes 1000000 | tf_op jit(solution)/shard_map/mean_rows/pallas_call | solution.py:373
  47.1 0.5 collective-permute-start.8
  47.6 1.9 %collective-permute-start.7 = (bf16[64,768]{1,0:T(8,128)(2,1)S(1)}, bf16[64,768]{1,0:T(8,128)(2,1)S(1)}, u32[]{:S(2)}, u32[]{:S(2)}) collective-permute-start(bf16[64,768]{1,0:T(8,128)(2,1)S(1)} %get-tuple-element.59.refs_0_), channel_id=1, source_target_pairs={{0,2},{1,3},{2,0},{3,1},{4,6},{5,7},{6,4},{7,5},{8,10},{9,11},{10,... | collective-permute-start | bytes 294920 | tf_op jit(solution)/shard_map/ppermute | solution.py:656
  49.5 1.3 %collective-permute-done.5.refs_3_ = bf16[64,1280]{1,0:T(8,128)(2,1)S(1)} collective-permute-done((bf16[64,1280]{1,0:T(8,128)(2,1)S(1)}, bf16[64,1280]{1,0:T(8,128)(2,1)S(1)}, u32[]{:S(2)}, u32[]{:S(2)}) %collective-permute-start.5) | collective-permute-done | bytes 163872 | tf_op jit(solution)/shard_map/ppermute | solution.py:656
  50.8 0.6 collective-permute-start.6
  51.5 3.3 %dense.2 = (bf16[64,1280]{1,0:T(8,128)(2,1)S(1)}, bf16[64,1280]{1,0:T(8,128)(2,1)S(1)}, f32[64,1280]{1,0:T(8,128)S(1)}, f32[64,1536]{1,0:T(8,128)S(1)}, f32[64,2...) custom-call(bf16[64,1280]{1,0:T(8,128)(2,1)S(1)} %get-tuple-element.47.refs_0_, ...), custom_call_target="tpu_custom_call" | custom-call | flops 1073741824 | bytes 6000000 | tf_op jit(solution)/shard_map/dense/pallas_call | solution.py:536
  54.8 0.5 collective-permute-done.8.refs_3_
  55.3 0.0 collective-permute-done.7.refs_2_
  55.3 0.2 collective-permute-done.6.refs_1_
  55.5 4.5 %dense.3 = (bf16[64,768]{1,0:T(8,128)(2,1)S(1)}, bf16[64,768]{1,0:T(8,128)(2,1)S(1)}, f32[64,768]{1,0:T(8,128)S(1)}, bf16[1536,128]{1,0:T(8,128)(2,1)}) custom-call(s32[1]{0:T(128)} %bitcast.8.mine_ref, bf16[64,768]{1,0:T(8,128)(2,1)S(1)} %get-tuple-element.59.refs_0_, bf16[64,768]{1,0:T(8,128)(2,1)S(1)} %collective-permute-done.6.refs_1_, ...), custom_call_target="tpu_custom_call" | custom-call | flops 1073741824 | bytes 6000000 | tf_op jit(solution)/shard_map/dense/pallas_call | solution.py:551
  60.0 8.7 %all-to-all-start.1 = ((bf16[64,24,128]{2,1,0:T(8,128)(2,1)}), bf16[64,24,128]{2,1,0:T(8,128)(2,1)S(1)}, u32[]{:S(2)}, u32[]{:S(2)}) async-start(bf16[64,24,128]{2,1,0:T(8,128)(2,1)} %bitcast.10), calls=%async_computation.1 | async-start | bytes 786432 | tf_op jit(solution)/shard_map/all_to_all | solution.py:703
  68.7 5.1 %local_back.1 = (f32[64,2048]{1,0:T(8,128)S(1)}, bf16[64,2048]{1,0:T(8,128)(2,1)}) custom-call(f32[64,1280]{1,0:T(8,128)S(1)} %get-tuple-element.58.ginput0, f32[64,768]{1,0:T(8,128)S(1)} %get-tuple-element.64.ginput1, bf16[64,1280]{1,0:T(8,128)(2,1)S(1)} %get-tuple-element.65.gmean0, bf16[64,768]{1,0:T(8,128)(2,1)S(1)} %get-tuple-element.66.gmean1, ...), custom_call_target="tpu_custom_call" | custom-call | flops 2147483648 | bytes 10000000 | tf_op jit(solution)/shard_map/local_back/pallas_call | solution.py:584
  73.8 9.5 %all-to-all-done.1 = bf16[64,24,128]{2,1,0:T(8,128)(2,1)S(1)} async-done(((bf16[64,24,128]{2,1,0:T(8,128)(2,1)}), bf16[64,24,128]{2,1,0:T(8,128)(2,1)S(1)}, u32[]{:S(2)}, u32[]{:S(2)}) %all-to-all-start.1) | async-done | bytes 393248 | tf_op jit(solution)/shard_map/all_to_all | solution.py:703
  83.3 0.7 reduce_grads.1
  84.1 6.2 %all-to-all-start.2 = ((f32[64,4,128]{2,1,0:T(4,128)}), f32[64,4,128]{2,1,0:T(4,128)S(1)}, u32[]{:S(2)}, u32[]{:S(2)}) async-start(f32[64,4,128]{2,1,0:T(4,128)} %bitcast.13), calls=%async_computation.2 | async-start | bytes 262144 | tf_op jit(solution)/shard_map/all_to_all | solution.py:707
  90.3 3.4 %scatter_rows.1 = bf16[64,2048]{1,0:T(8,128)(2,1)} custom-call(bf16[1536,128]{1,0:T(8,128)(2,1)S(1)} %bitcast.24, f32[16,2048]{1,0:T(8,128)S(1)} %get-tuple-element.44.index_ref.refs_4_, f32[64,2048]{1,0:T(8,128)S(1)} %get-tuple-element.74.total_ref), custom_call_target="tpu_custom_call" | custom-call | flops 2147483648 | bytes 2000000 | tf_op jit(solution)/shard_map/scatter_rows/pallas_call | solution.py:643
  93.7 7.0 %all-to-all-done.2 = f32[64,4,128]{2,1,0:T(4,128)S(1)} async-done(((f32[64,4,128]{2,1,0:T(4,128)}), f32[64,4,128]{2,1,0:T(4,128)S(1)}, u32[]{:S(2)}, u32[]{:S(2)}) %all-to-all-start.2) | async-done | bytes 131104 | tf_op jit(solution)/shard_map/all_to_all | solution.py:707
  100.6 0.7 slice_bitcast_fusion
  (5 shorter events, 0.0 us)
Async XLA Ops:
  1.8 38.9 %collective-permute-start.2 = (bf16[144,2176]{1,0:T(8,128)(2,1)S(1)}, bf16[144,2176]{1,0:T(8,128)(2,1)S(1)}, u32[]{:S(2)}, u32[]{:S(2)}) collective-permute-start(bf16[144,2176]{1,0:T(8,128)(2,1)S(1)} %bundle.1.refs_2_.refs_9_), channel_id=1, source_target_pairs={{0,1},{1,2},{2,3},{3,0},{4,5},{5,6},{6,7},{7,4},{8,9},{9,10},{10,1... | collective-permute-start | bytes 1880072 | tf_op jit(solution)/shard_map/ppermute | solution.py:656
  3.9 36.8 %collective-permute-start.1 = (bf16[144,2176]{1,0:T(8,128)(2,1)S(1)}, bf16[144,2176]{1,0:T(8,128)(2,1)}, u32[]{:S(2)}, u32[]{:S(2)}) collective-permute-start(bf16[144,2176]{1,0:T(8,128)(2,1)S(1)} %bundle.1.refs_2_.refs_9_), channel_id=1, source_target_pairs={{0,2},{1,3},{2,0},{3,1},{4,6},{5,7},{6,4},{7,5},{8,10},{9,11},{10,... | collective-permute-start | bytes 1880072 | tf_op jit(solution)/shard_map/ppermute | solution.py:656
  6.3 34.3 %collective-permute-start = (bf16[144,2176]{1,0:T(8,128)(2,1)S(1)}, bf16[144,2176]{1,0:T(8,128)(2,1)}, u32[]{:S(2)}, u32[]{:S(2)}) collective-permute-start(bf16[144,2176]{1,0:T(8,128)(2,1)S(1)} %bundle.1.refs_2_.refs_9_), channel_id=1, source_target_pairs={{0,3},{1,0},{2,1},{3,2},{4,7},{5,4},{6,5},{7,6},{8,11},{9,8},{10,9... | collective-permute-start | bytes 1880072 | tf_op jit(solution)/shard_map/ppermute | solution.py:656
  10.9 25.2 %all-to-all-start = ((bf16[64,16,128]{2,1,0:T(8,128)(2,1)}), bf16[64,16,128]{2,1,0:T(8,128)(2,1)S(1)}, u32[]{:S(2)}, u32[]{:S(2)}) async-start(bf16[64,16,128]{2,1,0:T(8,128)(2,1)} %bitcast.6), calls=%async_computation | async-start | bytes 524288 | tf_op jit(solution)/shard_map/all_to_all | solution.py:688
  40.6 2.9 %copy-start = (bf16[144,2176]{1,0:T(8,128)(2,1)}, bf16[144,2176]{1,0:T(8,128)(2,1)S(1)}, u32[]{:S(2)}) copy-start(bf16[144,2176]{1,0:T(8,128)(2,1)S(1)} %collective-permute-done.2.refs_5_.refs_12_) | copy-start | bytes 1880068
  40.7 10.2 %collective-permute-start.5 = (bf16[64,1280]{1,0:T(8,128)(2,1)S(1)}, bf16[64,1280]{1,0:T(8,128)(2,1)S(1)}, u32[]{:S(2)}, u32[]{:S(2)}) collective-permute-start(bf16[64,1280]{1,0:T(8,128)(2,1)S(1)} %get-tuple-element.47.refs_0_), channel_id=1, source_target_pairs={{0,1},{1,2},{2,3},{3,0},{4,5},{5,6},{6,7},{7,4},{8,9},{9,10},{10,1... | collective-permute-start | bytes 491528 | tf_op jit(solution)/shard_map/ppermute | solution.py:656
  41.1 10.4 %collective-permute-start.4 = (bf16[64,1280]{1,0:T(8,128)(2,1)S(1)}, bf16[64,1280]{1,0:T(8,128)(2,1)S(1)}, u32[]{:S(2)}, u32[]{:S(2)}) collective-permute-start(bf16[64,1280]{1,0:T(8,128)(2,1)S(1)} %get-tuple-element.47.refs_0_), channel_id=1, source_target_pairs={{0,2},{1,3},{2,0},{3,1},{4,6},{5,7},{6,4},{7,5},{8,10},{9,11},{10,... | collective-permute-start | bytes 491528 | tf_op jit(solution)/shard_map/ppermute | solution.py:656
  41.6 9.8 %collective-permute-start.3 = (bf16[64,1280]{1,0:T(8,128)(2,1)S(1)}, bf16[64,1280]{1,0:T(8,128)(2,1)S(1)}, u32[]{:S(2)}, u32[]{:S(2)}) collective-permute-start(bf16[64,1280]{1,0:T(8,128)(2,1)S(1)} %get-tuple-element.47.refs_0_), channel_id=1, source_target_pairs={{0,3},{1,0},{2,1},{3,2},{4,7},{5,4},{6,5},{7,6},{8,11},{9,8},{10,9... | collective-permute-start | bytes 491528 | tf_op jit(solution)/shard_map/ppermute | solution.py:656
  47.1 8.3 %collective-permute-start.8 = (bf16[64,768]{1,0:T(8,128)(2,1)S(1)}, bf16[64,768]{1,0:T(8,128)(2,1)S(1)}, u32[]{:S(2)}, u32[]{:S(2)}) collective-permute-start(bf16[64,768]{1,0:T(8,128)(2,1)S(1)} %get-tuple-element.59.refs_0_), channel_id=1, source_target_pairs={{0,1},{1,2},{2,3},{3,0},{4,5},{5,6},{6,7},{7,4},{8,9},{9,10},{10,1... | collective-permute-start | bytes 294920 | tf_op jit(solution)/shard_map/ppermute | solution.py:656
  47.6 7.7 %collective-permute-start.7 = (bf16[64,768]{1,0:T(8,128)(2,1)S(1)}, bf16[64,768]{1,0:T(8,128)(2,1)S(1)}, u32[]{:S(2)}, u32[]{:S(2)}) collective-permute-start(bf16[64,768]{1,0:T(8,128)(2,1)S(1)} %get-tuple-element.59.refs_0_), channel_id=1, source_target_pairs={{0,2},{1,3},{2,0},{3,1},{4,6},{5,7},{6,4},{7,5},{8,10},{9,11},{10,... | collective-permute-start | bytes 294920 | tf_op jit(solution)/shard_map/ppermute | solution.py:656
  50.8 4.7 %collective-permute-start.6 = (bf16[64,768]{1,0:T(8,128)(2,1)S(1)}, bf16[64,768]{1,0:T(8,128)(2,1)S(1)}, u32[]{:S(2)}, u32[]{:S(2)}) collective-permute-start(bf16[64,768]{1,0:T(8,128)(2,1)S(1)} %get-tuple-element.59.refs_0_), channel_id=1, source_target_pairs={{0,3},{1,0},{2,1},{3,2},{4,7},{5,4},{6,5},{7,6},{8,11},{9,8},{10,9... | collective-permute-start | bytes 294920 | tf_op jit(solution)/shard_map/ppermute | solution.py:656
  60.0 23.3 %all-to-all-start.1 = ((bf16[64,24,128]{2,1,0:T(8,128)(2,1)}), bf16[64,24,128]{2,1,0:T(8,128)(2,1)S(1)}, u32[]{:S(2)}, u32[]{:S(2)}) async-start(bf16[64,24,128]{2,1,0:T(8,128)(2,1)} %bitcast.10), calls=%async_computation.1 | async-start | bytes 786432 | tf_op jit(solution)/shard_map/all_to_all | solution.py:703
  84.1 16.6 %all-to-all-start.2 = ((f32[64,4,128]{2,1,0:T(4,128)}), f32[64,4,128]{2,1,0:T(4,128)S(1)}, u32[]{:S(2)}, u32[]{:S(2)}) async-start(f32[64,4,128]{2,1,0:T(4,128)} %bitcast.13), calls=%async_computation.2 | async-start | bytes 262144 | tf_op jit(solution)/shard_map/all_to_all | solution.py:707
